TPU v7x, 32 devices: a whole 2x2x4 slice. The times are simulated.
32 devices in a mesh: expert: 16 (over z, y, core), dp: 2 (over x).
Axes of the slice: x: 2, y: 2, z: 4, core: 2. Of those that a mesh axis runs over, the one named last changes fastest.
Arguments:
- tokens: bfloat16 [4096, 2048], P(('expert', 'dp')), may hold values from -6 to 6
- d_output: bfloat16 [4096, 2048], P(('expert', 'dp')), may hold values from -6 to 6
- expert_ids: int32 [4096, 8], P(('expert', 'dp')), may hold values from 0 to 15, all different within a row; in each aligned block of 128 rows (0 to 127, 128 to 255, ...) at most 96 rows name the same one
- gate_weights: bfloat16 [4096, 8], P(('expert', 'dp')), may hold values from 0.019897461 to 0.29882812
- pre_acts: bfloat16 [2, 16, 1536, 768], P('dp', 'expert'), may hold values from -6 to 6
- w_gate_up: bfloat16 [16, 2048, 768], P('expert'), may hold values from -0.125 to 0.125
- w_down: bfloat16 [16, 384, 2048], P('expert'), may hold values from -0.3125 to 0.3125
Outputs:
- token_grads: bfloat16 [4096, 2048], P(('expert', 'dp'))
- gate_grads: bfloat16 [4096, 8], P(('expert', 'dp'))
- gate_up_grads: float32 [16, 2048, 768], P('expert', 'dp')
- down_grads: float32 [16, 384, 2048], P('expert', None, 'dp')
Inputs may be any that keep to these rules, and one draw needn't show every extreme that they name: `expert_ids`: each token names 8 different experts; among the 128 tokens of one device (aligned blocks) no expert is named by more than 96 tokens, a bound that some block reaches.
All inputs are finite; a program needn't handle non-finite values.
Results may differ from a plain program's by a relative error of at most 0.0057.
Values may be sent and summed in bfloat16 or wider, within the bound.
No kernel may reach another device: no remote copies, remote signals or barrier semaphores. Data moves between devices by JAX's collectives and lax.ppermute only.
A program may use at most 128 MiB of HBM per device.

v0:
```python
import jax
import jax.numpy as jnp
from jax import lax
from jax.sharding import PartitionSpec as P


def contract(left_side, right_side, left_dim, right_dim):
    return lax.dot_general(
        left_side,
        right_side,
        (((left_dim,), (right_dim,)), ((), ())),
        preferred_element_type=jnp.float32,
    )


def with_zero(values, picks):
    padding = jnp.zeros((1,) + values.shape[1:], values.dtype)
    return jnp.concatenate([values, padding], axis=0)[picks]


def expert_backward(grad_rows, gate_rows, saved_rows, gate_up_weight, down_weight):
    hidden = down_weight.shape[0]
    saved_vals = saved_rows.astype(jnp.float32)
    gate_input = saved_vals[:, :hidden]
    up_input = saved_vals[:, hidden:]
    logistic = jax.nn.sigmoid(gate_input)
    swish_val = gate_input * logistic
    activated = swish_val * up_input
    projected = contract(grad_rows, down_weight, 1, 1)
    gate_grad = jnp.sum(activated * projected, axis=1).astype(jnp.bfloat16)
    weights = gate_rows.astype(jnp.float32)[:, None]
    hidden_grad = weights * projected
    up_grad = hidden_grad * swish_val
    pre_grad = hidden_grad * up_input * logistic * (1.0 + gate_input * (1.0 - logistic))
    both_grad = jnp.concatenate([pre_grad, up_grad], axis=1).astype(jnp.bfloat16)
    scaled = (weights * activated).astype(jnp.bfloat16)
    down_grad = contract(scaled, grad_rows, 0, 0)
    route_grad = contract(both_grad, gate_up_weight, 1, 1).astype(jnp.bfloat16)
    return (gate_grad, both_grad, down_grad, route_grad)


def local_rows(received, local_index, sources, local_experts):
    shaped = received.reshape((sources, local_experts) + received.shape[1:])[:, local_index]
    return shaped.reshape((sources * received.shape[1],) + received.shape[2:])


def on_device(tokens, d_output, expert_ids, gate_weights, pre_acts, w_gate_up, w_down):
    sources = lax.axis_size("expert")
    tok_rows, model_width = tokens.shape
    top_count = expert_ids.shape[1]
    local_experts = w_down.shape[0]
    experts = local_experts * sources
    capacity = pre_acts.shape[2] // sources
    routes = tok_rows * top_count
    flat_ids = expert_ids.reshape(routes)
    onehot = (flat_ids[:, None] == jnp.arange(experts, dtype=jnp.int32)[None, :]).astype(jnp.int32)
    route_rank = jnp.sum((jnp.cumsum(onehot, axis=0) - onehot) * onehot, axis=1)
    position = flat_ids * capacity + route_rank
    slot_table = (
        jnp.full((experts * capacity,), routes, jnp.int32)
        .at[position]
        .set(jnp.arange(routes, dtype=jnp.int32))
    )
    token_pick = slot_table // top_count
    send_inputs = with_zero(tokens, token_pick).reshape(experts, capacity, model_width)
    send_grads = with_zero(d_output, token_pick).reshape(experts, capacity, model_width)
    send_gates = with_zero(gate_weights.reshape(routes), slot_table).reshape(experts, capacity)
    recv_inputs, recv_grads, recv_gates = (
        lax.all_to_all(send_inputs, "expert", split_axis=0, concat_axis=0, tiled=True),
        lax.all_to_all(send_grads, "expert", split_axis=0, concat_axis=0, tiled=True),
        lax.all_to_all(send_gates, "expert", split_axis=0, concat_axis=0, tiled=True),
    )
    local_index = 0
    grad_rows = local_rows(recv_grads, local_index, sources, local_experts)
    gate_rows = local_rows(recv_gates, local_index, sources, local_experts)
    saved_rows = pre_acts[0, local_index]
    gate_grad, both_grad, down_grad, route_grad = expert_backward(
        grad_rows, gate_rows, saved_rows, w_gate_up[local_index], w_down[local_index]
    )
    results = [(gate_grad, both_grad, down_grad, route_grad, None)]
    back_rows = jnp.stack(
        [record[3].reshape(sources, capacity, model_width) for record in results], axis=1
    ).reshape(experts, capacity, model_width)
    back_gates = jnp.stack(
        [record[0].reshape(sources, capacity) for record in results], axis=1
    ).reshape(experts, capacity)
    home_rows, home_gates = (
        lax.all_to_all(back_rows, "expert", split_axis=0, concat_axis=0, tiled=True),
        lax.all_to_all(back_gates, "expert", split_axis=0, concat_axis=0, tiled=True),
    )
    route_rows = home_rows.reshape(experts * capacity, model_width)[position].reshape(
        tok_rows, top_count, model_width
    )
    token_grads = jnp.sum(route_rows.astype(jnp.float32), axis=1).astype(jnp.bfloat16)
    gate_out = home_gates.reshape(experts * capacity)[position].reshape(tok_rows, top_count)
    local_index = 0
    input_rows = local_rows(recv_inputs, local_index, sources, local_experts)
    up_grads = [contract(input_rows, results[local_index][1], 0, 0)]
    gate_up_total = jnp.stack(up_grads, axis=0)
    down_total = jnp.stack([record[2] for record in results], axis=0)
    gate_up_share, down_share = (
        lax.psum_scatter(gate_up_total, "dp", scatter_dimension=1, tiled=True),
        lax.psum_scatter(down_total, "dp", scatter_dimension=2, tiled=True),
    )
    return (token_grads, gate_out, gate_up_share, down_share)


def solution(mesh):
    placed = (
        P(("expert", "dp"), None),
        P(("expert", "dp"), None),
        P(("expert", "dp"), None),
        P(("expert", "dp"), None),
        P("dp", "expert", None, None),
        P("expert", None, None),
        P("expert", None, None),
    )
    return jax.shard_map(
        on_device,
        mesh=mesh,
        in_specs=placed,
        out_specs=(
            P(("expert", "dp"), None),
            P(("expert", "dp"), None),
            P("expert", "dp", None),
            P("expert", None, "dp"),
        ),
        check_vma=False,
    )
```

profile of v0, /device:TPU:13, one launch (start us, length us, event | category | flops | bytes accessed | tf_op | source)
XLA Modules:
  0.0 529.7 jit_solution(7440218195838051375)
XLA Ops:
  10.2 4.5 reduce-window.6
  15.2 4.3 scatter_custom_fusion
  19.6 9.5 %gather_fusion = bf16[1536]{0:T(1024)(128)(2,1)S(1)} fusion(bf16[1025]{0:T(1024)(128)(2,1)S(1)} %pad_maximum_fusion.3, s32[2048]{0:T(1024)S(1)} %get-tuple-element.18), kind=kCustom, calls=%fused_computation | custom fusion | bytes 12288 | tf_op jit(solution)/shard_map/gather | solution.py:18
  29.7 6.6 %all-to-all-start = ((bf16[16,1,96]{2,1,0:T(2,128)(2,1)}), bf16[16,1,96]{2,1,0:T(2,128)(2,1)S(1)}, u32[]{:S(2)}, u32[]{:S(2)}) async-start(bf16[16,1,96]{2,1,0:T(2,128)(2,1)} %all_to_all.25), calls=%async_computation | async-start | bytes 16384 | tf_op jit(solution)/shard_map/all_to_all | solution.py:71
  36.3 1.9 concatenate.14
  38.2 13.8 %gather_fusion.1 = bf16[1536,2048]{1,0:T(8,128)(2,1)} fusion(bf16[129,2048]{1,0:T(8,128)(2,1)} %concatenate.14, s32[2048]{0:T(1024)S(1)} %get-tuple-element.17), kind=kCustom, calls=%fused_computation.1 | custom fusion | bytes 12589056 | tf_op jit(solution)/shard_map/gather | solution.py:18
  52.0 6.0 %all-to-all-start.1 = ((bf16[16,96,2048]{2,1,0:T(8,128)(2,1)}), bf16[16,96,2048]{2,1,0:T(8,128)(2,1)}, u32[]{:S(2)}, u32[]{:S(2)}) async-start(bf16[16,96,2048]{2,1,0:T(8,128)(2,1)} %bitcast.48), calls=%async_computation.1 | async-start | bytes 12582912 | tf_op jit(solution)/shard_map/all_to_all | solution.py:70
  58.0 1.9 concatenate.16
  59.9 13.9 %gather_fusion.4 = bf16[1536,2048]{1,0:T(8,128)(2,1)} fusion(bf16[129,2048]{1,0:T(8,128)(2,1)} %concatenate.16, s32[2048]{0:T(1024)S(1)} %get-tuple-element.17), kind=kCustom, calls=%fused_computation.4 | custom fusion | bytes 12589056 | tf_op jit(solution)/shard_map/gather | solution.py:18
  73.8 121.6 %all-to-all-done.1 = bf16[16,96,2048]{2,1,0:T(8,128)(2,1)} async-done(((bf16[16,96,2048]{2,1,0:T(8,128)(2,1)}), bf16[16,96,2048]{2,1,0:T(8,128)(2,1)}, u32[]{:S(2)}, u32[]{:S(2)}) %all-to-all-start.1) | async-done | bytes 6291488 | tf_op jit(solution)/shard_map/all_to_all | solution.py:70
  195.4 4.9 all-to-all-start.4
  200.6 4.3 copy.29
  204.8 4.5 bitcast_convert_fusion
  209.4 8.6 %convolution_bitcast_fusion.1 = f32[1,384,2048]{2,1,0:T(8,128)} fusion(bf16[1536,2048]{1,0:T(8,128)(2,1)} %bitcast.5, f32[1536]{0:T(1024)S(1)} %reshape.112, f32[1536,768]{0,1:T(8,128)} %bitcast_convert_fusion), kind=kOutput, calls=%fused_computation.10 | convolution fusion | flops 2420047872 | bytes 14161920 | tf_op jit(solution)/shard_map/dot_general | solution.py:8
  218.1 9.6 %multiply_convert_fusion.2 = (bf16[1536,384]{0,1:T(8,128)(2,1)}, bf16[1536,384]{0,1:T(8,128)(2,1)}, bf16[1536]{0:T(1024)(128)(2,1)S(1)}) fusion(f32[1536,768]{0,1:T(8,128)} %bitcast_convert_fusion, f32[1536]{0:T(1024)S(1)} %reshape.112, bf16[1536,2048]{1,0:T(8,128)(2,1)} %bitcast.5, bf16[1,384,2048]{2,1,0:T(8,128)(2,1)} %param.13), kind=kOutput, calls=%fused_computation.16 | convolution fusion | flops 2425944576 | bytes 14951424 | tf_op jit(solution)/shard_map/dot_general | solution.py:8
  228.3 109.4 %all-to-all-done.4 = bf16[16,96,2048]{2,1,0:T(8,128)(2,1)} async-done(((bf16[16,96,2048]{2,1,0:T(8,128)(2,1)}), bf16[16,96,2048]{2,1,0:T(8,128)(2,1)}, u32[]{:S(2)}, u32[]{:S(2)}) %all-to-all-start.4) | async-done | bytes 6291488 | tf_op jit(solution)/shard_map/all_to_all | solution.py:69
  337.8 4.9 all-to-all-start.3
  342.7 9.6 %convolution_bitcast_fusion = f32[1,2048,768]{2,1,0:T(8,128)} fusion(bf16[1536,2048]{1,0:T(8,128)(2,1)} %bitcast.14, bf16[1536,384]{0,1:T(8,128)(2,1)} %get-tuple-element.13, bf16[1536,384]{0,1:T(8,128)(2,1)} %get-tuple-element.12), kind=kOutput, calls=%fused_computation.8 | convolution fusion | flops 4836556800 | bytes 14942208 | tf_op jit(solution)/shard_map/dot_general | solution.py:8
  352.4 8.8 %convolution_convert_fusion = bf16[1536,2048]{1,0:T(8,128)(2,1)} fusion(bf16[1,2048,768]{2,1,0:T(8,128)(2,1)S(1)} %copy-done, bf16[1536,384]{0,1:T(8,128)(2,1)} %get-tuple-element.13, bf16[1536,384]{0,1:T(8,128)(2,1)} %get-tuple-element.12), kind=kOutput, calls=%fused_computation.6 | convolution fusion | flops 4839702528 | bytes 11796480 | tf_op jit(solution)/shard_map/dot_general | solution.py:8
  361.1 6.0 %all-to-all-start.2 = ((bf16[16,96,2048]{2,1,0:T(8,128)(2,1)}), bf16[16,96,2048]{2,1,0:T(8,128)(2,1)}, u32[]{:S(2)}, u32[]{:S(2)}) async-start(bf16[16,96,2048]{2,1,0:T(8,128)(2,1)} %bitcast.49), calls=%async_computation.2 | async-start | bytes 12582912 | tf_op jit(solution)/shard_map/all_to_all | solution.py:88
  367.3 6.8 %gather_fusion.3 = bf16[1024]{0:T(1024)(128)(2,1)S(1)} fusion(bf16[1536]{0:T(1024)(128)(2,1)S(1)} %reshape.109, s32[1024]{0:T(1024)S(1)} %broadcast_clamp_fusion), kind=kCustom, calls=%fused_computation.3 | custom fusion | bytes 8192 | tf_op jit(solution)/shard_map/gather | solution.py:95
  374.8 129.7 %all-to-all-done.2 = bf16[16,96,2048]{2,1,0:T(8,128)(2,1)} async-done(((bf16[16,96,2048]{2,1,0:T(8,128)(2,1)}), bf16[16,96,2048]{2,1,0:T(8,128)(2,1)}, u32[]{:S(2)}, u32[]{:S(2)}) %all-to-all-start.2) | async-done | bytes 6291488 | tf_op jit(solution)/shard_map/all_to_all | solution.py:88
  504.6 12.4 %gather_fusion.2 = bf16[1024,2048]{1,0:T(8,128)(2,1)} fusion(bf16[1536,2048]{1,0:T(8,128)(2,1)} %bitcast.11, s32[1024]{0:T(1024)S(1)} %broadcast_clamp_fusion), kind=kCustom, calls=%fused_computation.2 | custom fusion | bytes 8392704 | tf_op jit(solution)/shard_map/gather | solution.py:91
  517.0 5.9 %bitcast_reduce_fusion = bf16[128,2048]{1,0:T(8,128)(2,1)} fusion(bf16[1024,2048]{1,0:T(8,128)(2,1)} %gather_fusion.2), kind=kLoop, calls=%fused_computation.7 | loop fusion | flops 1835008 | bytes 4718592 | tf_op jit(solution)/shard_map/reduce_sum | solution.py:94
  (40 shorter events, 6.1 us)
Async XLA Ops:
  7.2 345.2 %copy-start = (bf16[1,2048,768]{2,1,0:T(8,128)(2,1)S(1)}, bf16[1,2048,768]{2,1,0:T(8,128)(2,1)}, u32[]{:S(2)}) copy-start(bf16[1,2048,768]{2,1,0:T(8,128)(2,1)} %param.12) | copy-start | bytes 9437188
  29.7 22.3 %all-to-all-start = ((bf16[16,1,96]{2,1,0:T(2,128)(2,1)}), bf16[16,1,96]{2,1,0:T(2,128)(2,1)S(1)}, u32[]{:S(2)}, u32[]{:S(2)}) async-start(bf16[16,1,96]{2,1,0:T(2,128)(2,1)} %all_to_all.25), calls=%async_computation | async-start | bytes 16384 | tf_op jit(solution)/shard_map/all_to_all | solution.py:71
  52.0 143.4 %all-to-all-start.1 = ((bf16[16,96,2048]{2,1,0:T(8,128)(2,1)}), bf16[16,96,2048]{2,1,0:T(8,128)(2,1)}, u32[]{:S(2)}, u32[]{:S(2)}) async-start(bf16[16,96,2048]{2,1,0:T(8,128)(2,1)} %bitcast.48), calls=%async_computation.1 | async-start | bytes 12582912 | tf_op jit(solution)/shard_map/all_to_all | solution.py:70
  195.4 142.3 %all-to-all-start.4 = ((bf16[16,96,2048]{2,1,0:T(8,128)(2,1)}), bf16[16,96,2048]{2,1,0:T(8,128)(2,1)}, u32[]{:S(2)}, u32[]{:S(2)}) async-start(bf16[16,96,2048]{2,1,0:T(8,128)(2,1)} %bitcast.47), calls=%async_computation.4 | async-start | bytes 12582912 | tf_op jit(solution)/shard_map/all_to_all | solution.py:69
  200.4 322.5 %reduce-scatter.5.cloned.1.call-start = ((), (), s32[]{:S(2)}) async-start(), calls=%async_computation.8 | async-start | bytes 4718592 | tf_op jit(solution)/shard_map/reduce_scatter | solution.py:103
  337.8 23.4 %all-to-all-start.3 = ((bf16[16,1,96]{2,1,0:T(2,128)(2,1)}), bf16[16,1,96]{2,1,0:T(2,128)(2,1)S(1)}, u32[]{:S(2)}, u32[]{:S(2)}) async-start(bf16[16,1,96]{2,1,0:T(2,128)(2,1)} %convert_element_type.58), calls=%async_computation.3 | async-start | bytes 16384 | tf_op jit(solution)/shard_map/all_to_all | solution.py:89
  342.7 180.2 %reduce-scatter.3.cloned.1.call-start = ((), (), s32[]{:S(2)}) async-start(), calls=%async_computation.7 | async-start | bytes 9437184 | tf_op jit(solution)/shard_map/reduce_scatter | solution.py:102
  361.1 143.4 %all-to-all-start.2 = ((bf16[16,96,2048]{2,1,0:T(8,128)(2,1)}), bf16[16,96,2048]{2,1,0:T(8,128)(2,1)}, u32[]{:S(2)}, u32[]{:S(2)}) async-start(bf16[16,96,2048]{2,1,0:T(8,128)(2,1)} %bitcast.49), calls=%async_computation.2 | async-start | bytes 12582912 | tf_op jit(solution)/shard_map/all_to_all | solution.py:88
Sparse Core Ops, SparseCore 0:
  218.2 43.8 reduce-scatter.4
  352.5 77.6 reduce-scatter.2
where the time goes:
time: 531 us; the launch traced here: 530 us
  waiting for transfers between devices  361 us (68%)
  local copies, waits for them, and re-layouts  73.5 us (14%)
  matrix products  36.6 us (7%)
  starting transfers between devices  28.7 us (5%)
  other arithmetic  16 us (3%)
  between operations  14.2 us (3%)
    all_to_all x1, waiting for transfers between devices, on_device(): lax.all_to_all(back_rows, 'expert', split_axis=0, concat_axis=0, tiled=True)  130 us
    all_to_all x1, waiting for transfers between devices, on_device(): lax.all_to_all(send_grads, 'expert', split_axis=0, concat_axis=0, tiled=T...  122 us
    all_to_all x1, waiting for transfers between devices, on_device(): lax.all_to_all(send_inputs, 'expert', split_axis=0, concat_axis=0, tiled=...  109 us
    gather x3, local copies, waits for them, and re-layouts, with_zero(): return jnp.concatenate([values, padding], axis=0)[picks]  37.1 us
    dot_general x4, matrix products, contract(): lax.dot_general(left_side, right_side, (((left_dim,), (right_dim,)), ((),...  36.6 us
    gather x1, local copies, waits for them, and re-layouts, on_device(): home_rows.reshape(experts * capacity, model_width)[position]  12.4 us
  transfers between devices with their start and end apart: 7, of which 3 were waited for; matrix products, arithmetic and copies ran while one was open for 20% of the time, Pallas kernels for 0%

commit v1 on v0

v1 whole, which is shorter than its diff:
```python
import functools

import jax
import jax.numpy as jnp
import numpy as np
from jax import lax
from jax.experimental import pallas as pl
from jax.experimental.pallas import tpu as pltpu
from jax.sharding import PartitionSpec as P

CORES = 2
VMEM = 56 * 1024 * 1024
DEPTH = 2048
ROOMY = 8 * 1024 * 1024


def ring_order(chips):
    return list(range(0, chips, 2)) + list(range(1, chips, 2))[::-1]


def ring_pairs(chips, step):
    order = ring_order(chips)
    return [
        (CORES * chip + core, CORES * order[(at + step) % chips] + core)
        for at, chip in enumerate(order)
        for core in range(CORES)
    ]


def core_pairs(devices):
    return [(i, i ^ 1) for i in range(devices)]


def source_table(devices):
    chips = devices // CORES
    order = ring_order(chips)
    place = {chip: at for at, chip in enumerate(order)}
    table = np.zeros((devices, devices), np.int32)
    for device in range(devices):
        at, core = place[device // CORES], device % CORES
        offsets = [0]
        for far in range(1, chips // 2):
            offsets += [-far, far]
        offsets.append(chips // 2)
        for j, offset in enumerate(offsets):
            chip = order[(at + offset) % chips]
            table[device, 2 * j] = CORES * chip + core
            table[device, 2 * j + 1] = CORES * chip + 1 - core
    return table


def gather_ring(block):
    devices = lax.axis_size("expert")
    chips = devices // CORES
    up, down, across = ring_pairs(chips, 1), ring_pairs(chips, -1), core_pairs(devices)
    half = block.shape[0] // 2
    pairs = [([block], [lax.ppermute(block, "expert", across)])]
    rising = falling = block
    for _ in range(1, chips // 2):
        rising = lax.ppermute(rising, "expert", up)
        falling = lax.ppermute(falling, "expert", down)
        pairs.append(([rising], [lax.ppermute(rising, "expert", across)]))
        pairs.append(([falling], [lax.ppermute(falling, "expert", across)]))
    top = lax.ppermute(rising[:half], "expert", up)
    bottom = lax.ppermute(falling[half:], "expert", down)
    pairs.append(
        ([top, bottom], [lax.ppermute(top, "expert", across), lax.ppermute(bottom, "expert", across)])
    )
    return pairs, rising


def dot(left, right, left_dim, right_dim):
    return lax.dot_general(
        left, right, (((left_dim,), (right_dim,)), ((), ())), preferred_element_type=jnp.float32
    )


def route_kernel(n_own, n_sib, sources, *refs):
    grads, refs = refs[: n_own + n_sib], refs[n_own + n_sib :]
    saved_refs, gate_refs, refs = refs[:2], refs[2:4], refs[4:]
    down_ref, up_ref, both_ref, scaled_ref, gate_grad_ref, own_ref, sib_ref = refs
    hidden = down_ref.shape[0]
    tokens = own_ref.shape[0]
    slots = saved_refs[0].shape[1]
    rows = jnp.concatenate([ref[...] for ref in grads], axis=0)
    projected = dot(rows, down_ref[...], 1, 1)
    line = lax.broadcasted_iota(jnp.int32, (tokens, tokens), 0)
    lane = lax.broadcasted_iota(jnp.int32, (tokens, tokens), 1)
    earlier = (line < lane).astype(jnp.bfloat16)
    diagonal = line == lane
    slot = lax.broadcasted_iota(jnp.int32, (slots, tokens), 0).astype(jnp.float32)
    saved, weights = [], []
    for saved_ref, gate_ref in zip(saved_refs, gate_refs):
        gates = gate_ref[0]
        named = gates > 0.0
        counted = jnp.broadcast_to(named.astype(jnp.bfloat16), (16, tokens))
        rank = dot(counted, earlier, 1, 0)[:1]
        rank = jnp.where(named, rank, -1.0)
        pick = (slot == rank).astype(jnp.bfloat16)
        saved.append(dot(pick, saved_ref[0], 0, 0))
        weights.append(jnp.sum(jnp.where(diagonal, gates, 0.0), axis=1, keepdims=True))
    saved = jnp.concatenate(saved, axis=0)
    weights = jnp.concatenate(weights, axis=0)
    gate_in, up_in = saved[:, :hidden], saved[:, hidden:]
    logistic = jax.nn.sigmoid(gate_in)
    swish = gate_in * logistic
    activated = swish * up_in
    gate_grad = jnp.sum(activated * projected, axis=1, keepdims=True)
    for i in range(2):
        column = gate_grad[i * tokens : (i + 1) * tokens]
        gate_grad_ref[i : i + 1] = jnp.sum(jnp.where(diagonal, column, 0.0), axis=0, keepdims=True)
    hidden_grad = weights * projected
    up_grad = hidden_grad * swish
    pre_grad = hidden_grad * up_in * logistic * (1.0 + gate_in * (1.0 - logistic))
    both = jnp.concatenate([pre_grad, up_grad], axis=1).astype(jnp.bfloat16)
    both_ref[...] = both
    scaled_ref[...] = (weights * activated).astype(jnp.bfloat16)
    route = dot(both, up_ref[...], 1, 1).astype(jnp.bfloat16)
    own_ref[...] = route[:tokens]
    sib_ref[...] = route[tokens:]


def route_pair(j, pair, sources, saved, gates, gate_up_weight, down_weight):
    own, sib = pair
    pieces = own + sib
    width = pieces[0].shape[1]
    tokens = sum(piece.shape[0] for piece in own)
    hidden = down_weight.shape[0]
    slots = saved.shape[1]

    def whole(shape):
        return pl.BlockSpec(shape, lambda i, source: (0,) * len(shape))

    def picked(shape, at):
        return pl.BlockSpec((1,) + shape, lambda i, source: (source[at], 0, 0))

    out_shape = [
        ((2 * tokens, 2 * hidden), jnp.bfloat16),
        ((2 * tokens, hidden), jnp.bfloat16),
        ((2, tokens), jnp.float32),
        ((tokens, width), jnp.bfloat16),
        ((tokens, width), jnp.bfloat16),
    ]
    flops = 2 * 2 * tokens * width * hidden * 3
    return pl.pallas_call(
        functools.partial(route_kernel, len(own), len(sib)),
        grid_spec=pltpu.PrefetchScalarGridSpec(
            num_scalar_prefetch=1,
            grid=(1,),
            in_specs=[whole(piece.shape) for piece in pieces]
            + [picked((slots, 2 * hidden), 0), picked((slots, 2 * hidden), 1)]
            + [picked((1, tokens), 0), picked((1, tokens), 1)]
            + [whole(down_weight.shape), whole(gate_up_weight.shape)],
            out_specs=[whole(shape) for shape, _ in out_shape],
        ),
        out_shape=[jax.ShapeDtypeStruct(*out) for out in out_shape],
        compiler_params=pltpu.CompilerParams(vmem_limit_bytes=VMEM),
        cost_estimate=pl.CostEstimate(flops=flops, bytes_accessed=12 << 20, transcendentals=0),
        name="route",
    )(sources[2 * j : 2 * j + 2], *pieces, saved, saved, gates, gates, down_weight, gate_up_weight)


def weight_kernel(n_wide, n_narrow, wide_first, share, *refs):
    wide, narrow, refs = refs[:n_wide], refs[n_wide : n_wide + n_narrow], refs[n_wide + n_narrow :]
    out_ref, left, right = refs
    at = 0
    for ref in wide:
        left[at : at + ref.shape[0]] = ref[...]
        at += ref.shape[0]

    @pl.when(pl.program_id(0) == 0)
    def _():
        at = 0
        for ref in narrow:
            right[at : at + ref.shape[0]] = ref[...]
            at += ref.shape[0]

    first, second = (left, right) if wide_first else (right, left)
    depth = left.shape[0]
    if depth <= DEPTH or depth % DEPTH:
        out_ref[...] = dot(first[...], second[...], 0, 0).astype(out_ref.dtype)
        return

    def step(k, total):
        part = pl.ds(pl.multiple_of(k * DEPTH, DEPTH), DEPTH)
        return total + dot(first[part], second[part], 0, 0)

    total = lax.fori_loop(0, depth // DEPTH, step, jnp.zeros(out_ref.shape, jnp.float32))
    out_ref[...] = total.astype(out_ref.dtype)


def weight_grad(wide, narrow, share, shares, wide_first, dtype):
    width = wide[0].shape[1]
    part = width // shares
    chunk = min(256, part)
    steps = part // chunk
    depth = sum(piece.shape[0] for piece in wide)
    thin = narrow[0].shape[1]
    if wide_first:
        shape, block, place = (part, thin), (chunk, thin), lambda i, share: (i, 0)
    else:
        shape, block, place = (thin, part), (thin, chunk), lambda i, share: (0, i)
    return pl.pallas_call(
        functools.partial(weight_kernel, len(wide), len(narrow), wide_first),
        grid_spec=pltpu.PrefetchScalarGridSpec(
            num_scalar_prefetch=1,
            grid=(steps,),
            in_specs=[
                pl.BlockSpec((piece.shape[0], chunk), lambda i, share: (0, share[0] * steps + i))
                for piece in wide
            ]
            + [pl.BlockSpec(piece.shape, lambda i, share: (0, 0)) for piece in narrow],
            out_specs=pl.BlockSpec(block, place),
            scratch_shapes=[
                pltpu.VMEM((depth, chunk), wide[0].dtype),
                pltpu.VMEM((depth, thin), narrow[0].dtype),
            ],
        ),
        out_shape=jax.ShapeDtypeStruct(shape, dtype),
        compiler_params=pltpu.CompilerParams(vmem_limit_bytes=VMEM),
        cost_estimate=pl.CostEstimate(
            flops=2 * depth * part * thin, bytes_accessed=depth * (part + thin) * 2, transcendentals=0
        ),
        name="weight_grad",
    )(share, *wide, *narrow)


def shared_weight_grad(wide, narrow, wide_first):
    shares, me = lax.axis_size("dp"), lax.axis_index("dp")
    arrived = []
    for far in range(1, shares):
        theirs = ((me + far) % shares).astype(jnp.int32).reshape(1)
        sent = weight_grad(wide, narrow, theirs, shares, wide_first, jnp.bfloat16)
        arrived.append(lax.ppermute(sent, "dp", [(i, (i + far) % shares) for i in range(shares)]))
    total = weight_grad(wide, narrow, me.astype(jnp.int32).reshape(1), shares, wide_first, jnp.float32)
    return total, arrived


def flat(pairs):
    return [piece for own, sib in pairs for piece in own + sib]


def on_device(tokens, d_output, expert_ids, gate_weights, pre_acts, w_gate_up, w_down):
    devices = lax.axis_size("expert")
    chips = devices // CORES
    up, down, across = ring_pairs(chips, 1), ring_pairs(chips, -1), core_pairs(devices)
    me = lax.axis_index("expert")
    rows = tokens.shape[0]
    half = rows // 2
    table = source_table(devices)
    sources = lax.dynamic_index_in_dim(jnp.asarray(table), me, 0, keepdims=False)
    numbered = lax.dynamic_index_in_dim(jnp.asarray(np.argsort(table, axis=1).astype(np.int32)), me, 0, keepdims=False)

    names = jnp.arange(devices, dtype=jnp.int32)[:, None, None] == expert_ids[None]
    send_gates = jnp.sum(jnp.where(names, gate_weights[None].astype(jnp.float32), 0.0), axis=2)
    gates = lax.all_to_all(
        send_gates.astype(jnp.bfloat16), "expert", split_axis=0, concat_axis=0, tiled=True
    )
    gates = gates.astype(jnp.float32).reshape(devices, 1, rows)
    saved = pre_acts[0, 0].reshape(devices, pre_acts.shape[2] // devices, pre_acts.shape[3])

    grad_pairs, last = gather_ring(d_output)

    roomy = devices * rows * tokens.shape[1] <= ROOMY
    records, shared = [], []
    for j, pair in enumerate(grad_pairs):
        if shared and not roomy:
            sources, _ = lax.optimization_barrier((sources, shared[-1]))
        records.append(route_pair(j, pair, sources, saved, gates, w_gate_up[0], w_down[0]))
        shared.append([records[-1][3], lax.ppermute(records[-1][4], "expert", across)])
        if not roomy:
            shared[-1] = [sum(part.astype(jnp.float32) for part in shared[-1]).astype(jnp.bfloat16)]
    both = [record[0] for record in records]
    scaled = [record[1] for record in records]

    gate_grads = jnp.concatenate([record[2] for record in records], axis=0).astype(jnp.bfloat16)
    home_gates = lax.all_to_all(gate_grads[numbered], "expert", split_axis=0, concat_axis=0, tiled=True)
    gate_out = jnp.sum(jnp.where(names, home_gates.astype(jnp.float32)[:, :, None], 0.0), axis=0)
    gate_out = gate_out.astype(jnp.bfloat16)

    down_total, down_arrived = shared_weight_grad(flat(grad_pairs), scaled, False)

    ahead = (last,) if roomy else (last, down_total, down_arrived)
    tokens = lax.optimization_barrier((tokens,) + ahead)[0]
    token_pairs, last = gather_ring(tokens)

    def added(j, arrived, cut=None):
        total = sum(part.astype(jnp.float32) for part in shared[j])
        if cut is not None:
            total = total[cut]
        for value in arrived:
            total = total + value.astype(jnp.float32)
        return total.astype(jnp.bfloat16)

    rising = added(len(shared) - 1, [], slice(0, half))
    falling = added(len(shared) - 1, [], slice(half, rows))
    rising, falling, _ = lax.optimization_barrier((rising, falling, last))
    rising = jnp.pad(lax.ppermute(rising, "expert", up), ((0, rows - half), (0, 0)))
    falling = jnp.pad(lax.ppermute(falling, "expert", down), ((half, 0), (0, 0)))
    for far in range(chips // 2 - 1, 0, -1):
        rising = lax.ppermute(added(2 * far, [rising]), "expert", up)
        falling = lax.ppermute(added(2 * far - 1, [falling]), "expert", down)
    token_grads = added(0, [rising, falling])

    up_total, up_arrived = shared_weight_grad(flat(token_pairs), both, True)
    for value in up_arrived:
        up_total = up_total + value.astype(jnp.float32)
    for value in down_arrived:
        down_total = down_total + value.astype(jnp.float32)
    return token_grads, gate_out, up_total[None], down_total[None]


def solution(mesh):
    placed = (
        P(("expert", "dp"), None),
        P(("expert", "dp"), None),
        P(("expert", "dp"), None),
        P(("expert", "dp"), None),
        P("dp", "expert", None, None),
        P("expert", None, None),
        P("expert", None, None),
    )
    return jax.shard_map(
        on_device,
        mesh=mesh,
        in_specs=placed,
        out_specs=(
            P(("expert", "dp"), None),
            P(("expert", "dp"), None),
            P("expert", "dp", None),
            P("expert", None, "dp"),
        ),
        check_vma=False,
    )
```

time: 531 us -> 251 us (0.47)
  the two profiles are of different devices: /device:TPU:13 before, /device:TPU:0 now
where the time goes in v1:
time: 251 us; the launch traced here: 250 us
  waiting for transfers between devices  89.6 us (36%)
  Pallas kernels  84.4 us (34%)
  starting transfers between devices  46.7 us (19%)
  other arithmetic  22.6 us (9%)
  local copies, waits for them, and re-layouts  5.25 us (2%)
    pallas_call x8, Pallas kernels, route_pair(): pl.pallas_call(functools.partial(route_kernel, len(own), len(sib)), grid_...  53.5 us
    ppermute x2, waiting for transfers between devices, shared_weight_grad(): lax.ppermute(sent, 'dp', [(i, (i + far) % shares) for i in range(shares)])  34.8 us
    ppermute x6, waiting for transfers between devices, gather_ring(): rising = lax.ppermute(rising, 'expert', up)  34.2 us
    pallas_call x4, Pallas kernels, weight_grad(): pl.pallas_call(functools.partial(weight_kernel, len(wide), len(narrow), w...  30.9 us
    ppermute x6, starting transfers between devices, gather_ring(): rising = lax.ppermute(rising, 'expert', up)  10.9 us
    convert_element_type x7, other arithmetic, added(): return total.astype(jnp.bfloat16)  8.83 us
    ppermute x3, waiting for transfers between devices, on_device(): rising = lax.ppermute(added(2 * far, [rising]), 'expert', up)  8.73 us
    all_to_all x1, starting transfers between devices, on_device(): lax.all_to_all(send_gates.astype(jnp.bfloat16), 'expert', split_axis=0, c...  5.95 us
  transfers between devices with their start and end apart: 54, of which 11 were waited for; matrix products, arithmetic and copies ran while one was open for 9% of the time, Pallas kernels for 34%

profile of v1, /device:TPU:0, one launch (start us, length us, event | category | flops | bytes accessed | tf_op | source)
XLA Modules:
  0.0 249.8 jit_solution(8592102818427751477)
XLA Ops:
  0.6 3.1 %collective-permute-start.11 = (bf16[128,2048]{1,0:T(8,128)(2,1)}, bf16[128,2048]{1,0:T(8,128)(2,1)S(1)}, u32[]{:S(2)}, u32[]{:S(2)}) collective-permute-start(bf16[128,2048]{1,0:T(8,128)(2,1)} %refs_0_.7), channel_id=1, source_target_pairs={{0,8},{2,10},{8,16},{10,18},{16,24},{18,26},{24,28},{26,30},{28,20... | collective-permute-start | bytes 1572872 | tf_op jit(solution)/shard_map/ppermute | solution.py:60
  3.7 12.1 %collective-permute-done.11.refs_0_.refs_2_ = bf16[128,2048]{1,0:T(8,128)(2,1)S(1)} collective-permute-done((bf16[128,2048]{1,0:T(8,128)(2,1)}, bf16[128,2048]{1,0:T(8,128)(2,1)S(1)}, u32[]{:S(2)}, u32[]{:S(2)}) %collective-permute-start.11) | collective-permute-done | bytes 524320 | tf_op jit(solution)/shard_map/ppermute | solution.py:60
  17.8 11.1 %collective-permute-done.12.refs_0_.refs_6_ = bf16[128,2048]{1,0:T(8,128)(2,1)S(1)} collective-permute-done((bf16[128,2048]{1,0:T(8,128)(2,1)S(1)}, bf16[128,2048]{1,0:T(8,128)(2,1)S(1)}, u32[]{:S(2)}, u32[]{:S(2)}) %collective-permute-start.12) | collective-permute-done | bytes 524320 | tf_op jit(solution)/shard_map/ppermute | solution.py:60
  33.5 6.0 %all-to-all-start = ((bf16[16,1,128]{2,1,0:T(2,128)(2,1)}), bf16[16,1,128]{2,1,0:T(2,128)(2,1)S(1)}, u32[]{:S(2)}, u32[]{:S(2)}) async-start(bf16[16,1,128]{2,1,0:T(2,128)(2,1)} %copy.22), calls=%async_computation | async-start | bytes 16384 | tf_op jit(solution)/shard_map/all_to_all | solution.py:256
  47.2 4.0 %collective-permute-done.14.refs_0_.refs_14_ = bf16[64,2048]{1,0:T(8,128)(2,1)S(1)} collective-permute-done((bf16[64,2048]{1,0:T(8,128)(2,1)S(1)}, bf16[64,2048]{1,0:T(8,128)(2,1)S(1)}, u32[]{:S(2)}, u32[]{:S(2)}) %collective-permute-start.14) | collective-permute-done | bytes 262176 | tf_op jit(solution)/shard_map/ppermute | solution.py:64
  52.3 6.6 %route.8 = (bf16[256,768]{1,0:T(8,128)(2,1)}, bf16[256,384]{1,0:T(8,128)(2,1)}, f32[2,128]{1,0:T(2,128)}, bf16[128,2048]{1,0:T(8,128)(2,1)}, bf16[128,2048]{1,0:T(8,128)(2,1)}) custom-call(s32[2]{0:T(128)} %get-tuple-element.92.sources, bf16[128,2048]{1,0:T(8,128)(2,1)} %refs_0_.7, bf16[128,2048]{1,0:T(8,128)(2,1)} %collective-permute-done.refs_1_, ...), custom_call_target="tpu_custom_call" | custom-call | flops 1207959552 | bytes 12582912 | tf_op jit(solution)/shard_map/route/pallas_call | solution.py:145
  59.8 6.8 %route.9 = (bf16[256,768]{1,0:T(8,128)(2,1)}, bf16[256,384]{1,0:T(8,128)(2,1)}, f32[2,128]{1,0:T(2,128)}, bf16[128,2048]{1,0:T(8,128)(2,1)}, bf16[128,2048]{1,0:T(8,128)(2,1)}) custom-call(s32[2]{0:T(128)} %get-tuple-element.99.sources, bf16[128,2048]{1,0:T(8,128)(2,1)} %copy-done.4, bf16[128,2048]{1,0:T(8,128)(2,1)} %collective-permute-done.3.refs_1_.refs_5_, ...), custom_call_target="tpu_custom_call" | custom-call | flops 1207959552 | bytes 12582912 | tf_op jit(solution)/shard_map/route/pallas_call | solution.py:145
  68.3 6.6 %route.12 = (bf16[256,768]{1,0:T(8,128)(2,1)}, bf16[256,384]{1,0:T(8,128)(2,1)}, f32[2,128]{1,0:T(2,128)}, bf16[128,2048]{1,0:T(8,128)(2,1)}, bf16[128,2048]{1,0:T(8,128)(2,1)}) custom-call(s32[2]{0:T(128)} %get-tuple-element.96.sources, bf16[64,2048]{1,0:T(8,128)(2,1)} %copy-done.11, bf16[64,2048]{1,0:T(8,128)(2,1)} %collective-permute-done.15.refs_1_.refs_15_, ...), custom_call_target="tpu_custom_call" | custom-call | flops 1207959552 | bytes 12582912 | tf_op jit(solution)/shard_map/route/pallas_call | solution.py:145
  76.5 6.7 %route.13 = (bf16[256,768]{1,0:T(8,128)(2,1)}, bf16[256,384]{1,0:T(8,128)(2,1)}, f32[2,128]{1,0:T(2,128)}, bf16[128,2048]{1,0:T(8,128)(2,1)}, bf16[128,2048]{1,0:T(8,128)(2,1)}) custom-call(s32[2]{0:T(128)} %get-tuple-element.95.sources, bf16[128,2048]{1,0:T(8,128)(2,1)} %copy-done.3, bf16[128,2048]{1,0:T(8,128)(2,1)} %collective-permute-done.26.refs_1_.refs_3_, ...), custom_call_target="tpu_custom_call" | custom-call | flops 1207959552 | bytes 12582912 | tf_op jit(solution)/shard_map/route/pallas_call | solution.py:145
  83.8 6.6 %route.10 = (bf16[256,768]{1,0:T(8,128)(2,1)}, bf16[256,384]{1,0:T(8,128)(2,1)}, f32[2,128]{1,0:T(2,128)}, bf16[128,2048]{1,0:T(8,128)(2,1)}, bf16[128,2048]{1,0:T(8,128)(2,1)}) custom-call(s32[2]{0:T(128)} %get-tuple-element.98.sources, bf16[128,2048]{1,0:T(8,128)(2,1)} %copy-done.6, bf16[128,2048]{1,0:T(8,128)(2,1)} %collective-permute-done.6.refs_1_.refs_9_, ...), custom_call_target="tpu_custom_call" | custom-call | flops 1207959552 | bytes 12582912 | tf_op jit(solution)/shard_map/route/pallas_call | solution.py:145
  91.1 6.8 %route.14 = (bf16[256,768]{1,0:T(8,128)(2,1)}, bf16[256,384]{1,0:T(8,128)(2,1)}, f32[2,128]{1,0:T(2,128)}, bf16[128,2048]{1,0:T(8,128)(2,1)}, bf16[128,2048]{1,0:T(8,128)(2,1)}) custom-call(s32[2]{0:T(128)} %get-tuple-element.94.sources, bf16[128,2048]{1,0:T(8,128)(2,1)} %copy-done.5, bf16[128,2048]{1,0:T(8,128)(2,1)} %collective-permute-done.28.refs_1_.refs_7_, ...), custom_call_target="tpu_custom_call" | custom-call | flops 1207959552 | bytes 12582912 | tf_op jit(solution)/shard_map/route/pallas_call | solution.py:145
  99.3 6.6 %route.11 = (bf16[256,768]{1,0:T(8,128)(2,1)}, bf16[256,384]{1,0:T(8,128)(2,1)}, f32[2,128]{1,0:T(2,128)}, bf16[128,2048]{1,0:T(8,128)(2,1)}, bf16[128,2048]{1,0:T(8,128)(2,1)}) custom-call(s32[2]{0:T(128)} %get-tuple-element.97.sources, bf16[128,2048]{1,0:T(8,128)(2,1)} %copy-done.1, bf16[128,2048]{1,0:T(8,128)(2,1)} %copy-done.7, ...), custom_call_target="tpu_custom_call" | custom-call | flops 1207959552 | bytes 12582912 | tf_op jit(solution)/shard_map/route/pallas_call | solution.py:145
  107.0 6.8 %route.15 = (bf16[256,768]{1,0:T(8,128)(2,1)}, bf16[256,384]{1,0:T(8,128)(2,1)}, f32[2,128]{1,0:T(2,128)}, bf16[128,2048]{1,0:T(8,128)(2,1)}, bf16[128,2048]{1,0:T(8,128)(2,1)}) custom-call(s32[2]{0:T(128)} %get-tuple-element.93.sources, bf16[128,2048]{1,0:T(8,128)(2,1)} %copy-done, bf16[128,2048]{1,0:T(8,128)(2,1)} %copy-done.8, ...), custom_call_target="tpu_custom_call" | custom-call | flops 1207959552 | bytes 12582912 | tf_op jit(solution)/shard_map/route/pallas_call | solution.py:145
  115.6 5.3 %all-to-all-start.1 = ((bf16[16,1,128]{2,1,0:T(2,128)(2,1)}), bf16[16,1,128]{2,1,0:T(2,128)(2,1)S(1)}, u32[]{:S(2)}, u32[]{:S(2)}) async-start(bf16[16,1,128]{2,1,0:T(2,128)(2,1)} %copy.23), calls=%async_computation.1 | async-start | bytes 16384 | tf_op jit(solution)/shard_map/all_to_all | solution.py:277
  125.5 10.1 %collective-permute-done.21.refs_10_ = bf16[128,2048]{1,0:T(8,128)(2,1)S(1)} collective-permute-done((bf16[128,2048]{1,0:T(8,128)(2,1)S(1)}, bf16[128,2048]{1,0:T(8,128)(2,1)S(1)}, u32[]{:S(2)}, u32[]{:S(2)}) %collective-permute-start.21) | collective-permute-done | bytes 524320 | tf_op jit(solution)/shard_map/ppermute | solution.py:60
  137.3 6.5 %weight_grad.7 = bf16[384,1024]{1,0:T(8,128)(2,1)} custom-call(s32[1]{0:T(128)} %bitcast.17.share, bf16[128,2048]{1,0:T(8,128)(2,1)} %refs_0_.7, bf16[128,2048]{1,0:T(8,128)(2,1)} %collective-permute-done.refs_1_, bf16[128,2048]{1,0:T(8,128)(2,1)} %copy-done.3, bf16[128,2048]{1,0:T(8,128)(2,1)} %collective-permute-done.26.refs_1_.refs_3_, ...), custom_call_target="tpu_custom_call" | custom-call | flops 1610612736 | bytes 5767168 | tf_op jit(solution)/shard_map/weight_grad/pallas_call | solution.py:203
  144.5 6.6 %weight_grad.6 = f32[384,1024]{1,0:T(8,128)} custom-call(s32[1]{0:T(128)} %bitcast.16.share, bf16[128,2048]{1,0:T(8,128)(2,1)} %refs_0_.7, bf16[128,2048]{1,0:T(8,128)(2,1)} %collective-permute-done.refs_1_, bf16[128,2048]{1,0:T(8,128)(2,1)} %copy-done.3, bf16[128,2048]{1,0:T(8,128)(2,1)} %collective-permute-done.26.refs_1_.refs_3_, ...), custom_call_target="tpu_custom_call" | custom-call | flops 1610612736 | bytes 5767168 | tf_op jit(solution)/shard_map/weight_grad/pallas_call | solution.py:203
  155.9 5.2 %collective-permute-done.32 = bf16[64,2048]{1,0:T(8,128)(2,1)S(1)} collective-permute-done((bf16[64,2048]{1,0:T(8,128)(2,1)}, bf16[64,2048]{1,0:T(8,128)(2,1)S(1)}, u32[]{:S(2)}, u32[]{:S(2)}) %collective-permute-start.32) | collective-permute-done | bytes 262176 | tf_op jit(solution)/shard_map/ppermute | solution.py:299
  167.2 8.7 %collective-permute-done.23 = bf16[128,2048]{1,0:T(8,128)(2,1)S(1)} collective-permute-done((bf16[128,2048]{1,0:T(8,128)(2,1)S(1)}, bf16[128,2048]{1,0:T(8,128)(2,1)S(1)}, u32[]{:S(2)}, u32[]{:S(2)}) %collective-permute-start.23) | collective-permute-done | bytes 524320 | tf_op jit(solution)/shard_map/ppermute | solution.py:301
  183.7 8.9 %weight_grad.5 = bf16[1024,768]{1,0:T(8,128)(2,1)} custom-call(s32[1]{0:T(128)} %bitcast.17.share, bf16[128,2048]{1,0:T(8,128)(2,1)} %refs_0_.5, bf16[128,2048]{1,0:T(8,128)(2,1)} %collective-permute-done.36.refs_1_, bf16[128,2048]{1,0:T(8,128)(2,1)} %collective-permute-done.19.refs_2_, bf16[128,2048]{1,0:T(8,128)(2,1)} %copy-done.17, ...), custom_call_target="tpu_custom_call" | custom-call | flops 3221225472 | bytes 7340032 | tf_op jit(solution)/shard_map/weight_grad/pallas_call | solution.py:203
  199.7 13.4 %collective-permute-done.51 = bf16[384,1024]{1,0:T(8,128)(2,1)S(1)} collective-permute-done((bf16[384,1024]{1,0:T(8,128)(2,1)S(1)}, bf16[384,1024]{1,0:T(8,128)(2,1)S(1)}, u32[]{:S(2)}, u32[]{:S(2)}) %collective-permute-start.51) | collective-permute-done | bytes 786464 | tf_op jit(solution)/shard_map/ppermute | solution.py:234
  214.5 8.8 %weight_grad.4 = f32[1024,768]{1,0:T(8,128)} custom-call(s32[1]{0:T(128)} %bitcast.16.share, bf16[128,2048]{1,0:T(8,128)(2,1)} %refs_0_.5, bf16[128,2048]{1,0:T(8,128)(2,1)} %collective-permute-done.36.refs_1_, bf16[128,2048]{1,0:T(8,128)(2,1)} %collective-permute-done.19.refs_2_, bf16[128,2048]{1,0:T(8,128)(2,1)} %copy-done.17, ...), custom_call_target="tpu_custom_call" | custom-call | flops 3221225472 | bytes 7340032 | tf_op jit(solution)/shard_map/weight_grad/pallas_call | solution.py:203
  224.5 21.4 %collective-permute-done.50 = bf16[1024,768]{1,0:T(8,128)(2,1)S(1)} collective-permute-done((bf16[1024,768]{1,0:T(8,128)(2,1)}, bf16[1024,768]{1,0:T(8,128)(2,1)S(1)}, u32[]{:S(2)}, u32[]{:S(2)}) %collective-permute-start.50) | collective-permute-done | bytes 1572896 | tf_op jit(solution)/shard_map/ppermute | solution.py:234
  246.0 3.9 %add_bitcast_fusion = f32[1,1024,768]{2,1,0:T(8,128)} fusion(f32[1024,768]{1,0:T(8,128)} %weight_grad.4, bf16[1024,768]{1,0:T(8,128)(2,1)S(1)} %collective-permute-done.50), kind=kLoop, calls=%fused_computation.1 | loop fusion | flops 1572864 | bytes 7864320 | tf_op jit(solution)/shard_map/broadcast_in_dim | solution.py:310
  (206 shorter events, 60.0 us)
Async XLA Ops:
  33.5 18.3 %all-to-all-start = ((bf16[16,1,128]{2,1,0:T(2,128)(2,1)}), bf16[16,1,128]{2,1,0:T(2,128)(2,1)S(1)}, u32[]{:S(2)}, u32[]{:S(2)}) async-start(bf16[16,1,128]{2,1,0:T(2,128)(2,1)} %copy.22), calls=%async_computation | async-start | bytes 16384 | tf_op jit(solution)/shard_map/all_to_all | solution.py:256
  41.1 18.6 %collective-permute-start.28 = (bf16[128,2048]{1,0:T(8,128)(2,1)S(1)}, bf16[128,2048]{1,0:T(8,128)(2,1)}, u32[]{:S(2)}, u32[]{:S(2)}) collective-permute-start(bf16[128,2048]{1,0:T(8,128)(2,1)S(1)} %collective-permute-done.12.refs_0_.refs_6_), channel_id=1, source_target_pairs={{0,2},{2,0},{4,6},{6,4},{8,10},{10,8},{12,14},{14,12},{16,18},{18,... | collective-permute-start | bytes 1572872 | tf_op jit(solution)/shard_map/ppermute | solution.py:62
  44.8 30.1 %collective-permute-start.6 = (bf16[128,2048]{1,0:T(8,128)(2,1)S(1)}, bf16[128,2048]{1,0:T(8,128)(2,1)}, u32[]{:S(2)}, u32[]{:S(2)}) collective-permute-start(bf16[128,2048]{1,0:T(8,128)(2,1)S(1)} %collective-permute-done.5.refs_0_.refs_8_), channel_id=1, source_target_pairs={{0,2},{2,0},{4,6},{6,4},{8,10},{10,8},{12,14},{14,12},{16,18},{18,... | collective-permute-start | bytes 1572872 | tf_op jit(solution)/shard_map/ppermute | solution.py:63
  44.8 30.4 %collective-permute-start.19 = (bf16[128,2048]{1,0:T(8,128)(2,1)}, bf16[128,2048]{1,0:T(8,128)(2,1)}, u32[]{:S(2)}, u32[]{:S(2)}) collective-permute-start(bf16[128,2048]{1,0:T(8,128)(2,1)} %refs_0_.5), channel_id=1, source_target_pairs={{0,8},{2,10},{8,16},{10,18},{16,24},{18,26},{24,28},{26,30},{28,20... | collective-permute-start | bytes 1572872 | tf_op jit(solution)/shard_map/ppermute | solution.py:60
  51.2 16.1 %collective-permute-start.16 = (bf16[64,2048]{1,0:T(8,128)(2,1)S(1)}, bf16[64,2048]{1,0:T(8,128)(2,1)}, u32[]{:S(2)}, u32[]{:S(2)}) collective-permute-start(bf16[64,2048]{1,0:T(8,128)(2,1)S(1)} %collective-permute-done.14.refs_0_.refs_14_), channel_id=1, source_target_pairs={{0,2},{2,0},{4,6},{6,4},{8,10},{10,8},{12,14},{14,12},{16,18},{18,... | collective-permute-start | bytes 786440 | tf_op jit(solution)/shard_map/ppermute | solution.py:67
  51.2 16.9 %collective-permute-start.17 = (bf16[64,2048]{1,0:T(8,128)(2,1)}, bf16[64,2048]{1,0:T(8,128)(2,1)}, u32[]{:S(2)}, u32[]{:S(2)}) collective-permute-start(bf16[64,2048]{1,0:T(8,128)(2,1)} %collective-permute-done.15.refs_1_.refs_15_), channel_id=1, source_target_pairs={{0,2},{2,0},{4,6},{6,4},{8,10},{10,8},{12,14},{14,12},{16,18},{18,... | collective-permute-start | bytes 786440 | tf_op jit(solution)/shard_map/ppermute | solution.py:67
  59.7 38.8 %collective-permute-start.9 = (bf16[128,2048]{1,0:T(8,128)(2,1)S(1)}, bf16[128,2048]{1,0:T(8,128)(2,1)S(1)}, u32[]{:S(2)}, u32[]{:S(2)}) collective-permute-start(bf16[128,2048]{1,0:T(8,128)(2,1)S(1)} %collective-permute-done.8.refs_0_.refs_12_), channel_id=1, source_target_pairs={{0,2},{2,0},{4,6},{6,4},{8,10},{10,8},{12,14},{14,12},{16,18},{18,... | collective-permute-start | bytes 1572872 | tf_op jit(solution)/shard_map/ppermute | solution.py:63
  67.3 38.7 %collective-permute-start.38 = (bf16[128,2048]{1,0:T(8,128)(2,1)S(1)}, bf16[128,2048]{1,0:T(8,128)(2,1)S(1)}, u32[]{:S(2)}, u32[]{:S(2)}) collective-permute-start(bf16[128,2048]{1,0:T(8,128)(2,1)S(1)} %copy-done.12), channel_id=1, source_target_pairs={{0,4},{2,6},{8,0},{10,2},{16,8},{18,10},{24,16},{26,18},{28,24},{3... | collective-permute-start | bytes 1572872 | tf_op jit(solution)/shard_map/ppermute | solution.py:61
  68.1 37.9 %collective-permute-start.30 = (bf16[128,2048]{1,0:T(8,128)(2,1)S(1)}, bf16[128,2048]{1,0:T(8,128)(2,1)S(1)}, u32[]{:S(2)}, u32[]{:S(2)}) collective-permute-start(bf16[128,2048]{1,0:T(8,128)(2,1)S(1)} %collective-permute-done.13.refs_0_.refs_10_), channel_id=1, source_target_pairs={{0,2},{2,0},{4,6},{6,4},{8,10},{10,8},{12,14},{14,12},{16,18},{18,... | collective-permute-start | bytes 1572872 | tf_op jit(solution)/shard_map/ppermute | solution.py:62
  74.9 46.0 %collective-permute-start.18 = (bf16[128,2048]{1,0:T(8,128)(2,1)}, bf16[128,2048]{1,0:T(8,128)(2,1)}, u32[]{:S(2)}, u32[]{:S(2)}) collective-permute-start(bf16[128,2048]{1,0:T(8,128)(2,1)} %get-tuple-element.56), channel_id=1, source_target_pairs={{0,2},{2,0},{4,6},{6,4},{8,10},{10,8},{12,14},{14,12},{16,18},{18,... | collective-permute-start | bytes 1572872 | tf_op jit(solution)/shard_map/ppermute | solution.py:270
  75.3 46.1 %collective-permute-start.20 = (bf16[128,2048]{1,0:T(8,128)(2,1)}, bf16[128,2048]{1,0:T(8,128)(2,1)S(1)}, u32[]{:S(2)}, u32[]{:S(2)}) collective-permute-start(bf16[128,2048]{1,0:T(8,128)(2,1)} %collective-permute-done.19.refs_2_), channel_id=1, source_target_pairs={{0,8},{2,10},{8,16},{10,18},{16,24},{18,26},{24,28},{26,30},{28,20... | collective-permute-start | bytes 1572872 | tf_op jit(solution)/shard_map/ppermute | solution.py:60
  98.5 45.3 %collective-permute-start.36 = (bf16[128,2048]{1,0:T(8,128)(2,1)S(1)}, bf16[128,2048]{1,0:T(8,128)(2,1)}, u32[]{:S(2)}, u32[]{:S(2)}) collective-permute-start(bf16[128,2048]{1,0:T(8,128)(2,1)S(1)} %copy-done.12), channel_id=1, source_target_pairs={{0,2},{2,0},{4,6},{6,4},{8,10},{10,8},{12,14},{14,12},{16,18},{18,... | collective-permute-start | bytes 1572872 | tf_op jit(solution)/shard_map/ppermute | solution.py:57
  106.0 37.9 %collective-permute-start.7 = (bf16[128,2048]{1,0:T(8,128)(2,1)}, bf16[128,2048]{1,0:T(8,128)(2,1)}, u32[]{:S(2)}, u32[]{:S(2)}) collective-permute-start(bf16[128,2048]{1,0:T(8,128)(2,1)} %get-tuple-element.52), channel_id=1, source_target_pairs={{0,2},{2,0},{4,6},{6,4},{8,10},{10,8},{12,14},{14,12},{16,18},{18,... | collective-permute-start | bytes 1572872 | tf_op jit(solution)/shard_map/ppermute | solution.py:270
  106.1 18.2 %collective-permute-start.41 = (bf16[128,2048]{1,0:T(8,128)(2,1)S(1)}, bf16[128,2048]{1,0:T(8,128)(2,1)S(1)}, u32[]{:S(2)}, u32[]{:S(2)}) collective-permute-start(bf16[128,2048]{1,0:T(8,128)(2,1)S(1)} %collective-permute-done.38.refs_4_), channel_id=1, source_target_pairs={{0,4},{2,6},{8,0},{10,2},{16,8},{18,10},{24,16},{26,18},{28,24},{3... | collective-permute-start | bytes 1572872 | tf_op jit(solution)/shard_map/ppermute | solution.py:61
  115.6 35.5 %all-to-all-start.1 = ((bf16[16,1,128]{2,1,0:T(2,128)(2,1)}), bf16[16,1,128]{2,1,0:T(2,128)(2,1)S(1)}, u32[]{:S(2)}, u32[]{:S(2)}) async-start(bf16[16,1,128]{2,1,0:T(2,128)(2,1)} %copy.23), calls=%async_computation.1 | async-start | bytes 16384 | tf_op jit(solution)/shard_map/all_to_all | solution.py:277
  120.9 30.3 %collective-permute-start.10 = (bf16[128,2048]{1,0:T(8,128)(2,1)}, bf16[128,2048]{1,0:T(8,128)(2,1)}, u32[]{:S(2)}, u32[]{:S(2)}) collective-permute-start(bf16[128,2048]{1,0:T(8,128)(2,1)} %get-tuple-element.54), channel_id=1, source_target_pairs={{0,2},{2,0},{4,6},{6,4},{8,10},{10,8},{12,14},{14,12},{16,18},{18,... | collective-permute-start | bytes 1572872 | tf_op jit(solution)/shard_map/ppermute | solution.py:270
  124.3 20.1 %collective-permute-start.44 = (bf16[128,2048]{1,0:T(8,128)(2,1)S(1)}, bf16[128,2048]{1,0:T(8,128)(2,1)S(1)}, u32[]{:S(2)}, u32[]{:S(2)}) collective-permute-start(bf16[128,2048]{1,0:T(8,128)(2,1)S(1)} %collective-permute-done.41.refs_8_), channel_id=1, source_target_pairs={{0,4},{2,6},{8,0},{10,2},{16,8},{18,10},{24,16},{26,18},{28,24},{3... | collective-permute-start | bytes 1572872 | tf_op jit(solution)/shard_map/ppermute | solution.py:61
  135.6 16.1 %collective-permute-start.22 = (bf16[64,2048]{1,0:T(8,128)(2,1)}, bf16[64,2048]{1,0:T(8,128)(2,1)S(1)}, u32[]{:S(2)}, u32[]{:S(2)}) collective-permute-start(bf16[64,2048]{1,0:T(8,128)(2,1)} %get-tuple-element.58), channel_id=1, source_target_pairs={{0,8},{2,10},{8,16},{10,18},{16,24},{18,26},{24,28},{26,30},{28,20... | collective-permute-start | bytes 786440 | tf_op jit(solution)/shard_map/ppermute | solution.py:298
  166.7 16.1 %collective-permute-start.43 = (bf16[128,2048]{1,0:T(8,128)(2,1)S(1)}, bf16[128,2048]{1,0:T(8,128)(2,1)S(1)}, u32[]{:S(2)}, u32[]{:S(2)}) collective-permute-start(bf16[128,2048]{1,0:T(8,128)(2,1)S(1)} %collective-permute-done.21.refs_10_), channel_id=1, source_target_pairs={{0,2},{2,0},{4,6},{6,4},{8,10},{10,8},{12,14},{14,12},{16,18},{18,... | collective-permute-start | bytes 1572872 | tf_op jit(solution)/shard_map/ppermute | solution.py:62
  182.3 41.1 %collective-permute-start.1 = (bf16[128,2048]{1,0:T(8,128)(2,1)}, bf16[128,2048]{1,0:T(8,128)(2,1)S(1)}, u32[]{:S(2)}, u32[]{:S(2)}) collective-permute-start(bf16[128,2048]{1,0:T(8,128)(2,1)} %get-tuple-element.48), channel_id=1, source_target_pairs={{0,2},{2,0},{4,6},{6,4},{8,10},{10,8},{12,14},{14,12},{16,18},{18,... | collective-permute-start | bytes 1572872 | tf_op jit(solution)/shard_map/ppermute | solution.py:270
  192.6 20.5 %collective-permute-start.51 = (bf16[384,1024]{1,0:T(8,128)(2,1)S(1)}, bf16[384,1024]{1,0:T(8,128)(2,1)S(1)}, u32[]{:S(2)}, u32[]{:S(2)}) collective-permute-start(bf16[384,1024]{1,0:T(8,128)(2,1)S(1)} %copy-done.26), channel_id=1, source_target_pairs={{0,1},{1,0},{2,3},{3,2},{4,5},{5,4},{6,7},{7,6},{8,9},{9,8},{10,11... | collective-permute-start | bytes 2359304 | tf_op jit(solution)/shard_map/ppermute | solution.py:234
  194.2 51.7 %collective-permute-start.50 = (bf16[1024,768]{1,0:T(8,128)(2,1)}, bf16[1024,768]{1,0:T(8,128)(2,1)S(1)}, u32[]{:S(2)}, u32[]{:S(2)}) collective-permute-start(bf16[1024,768]{1,0:T(8,128)(2,1)} %weight_grad.5), channel_id=1, source_target_pairs={{0,1},{1,0},{2,3},{3,2},{4,5},{5,4},{6,7},{7,6},{8,9},{9,8},{10,11... | collective-permute-start | bytes 4718600 | tf_op jit(solution)/shard_map/ppermute | solution.py:234
  196.3 27.1 %collective-permute-start.25 = (bf16[128,2048]{1,0:T(8,128)(2,1)S(1)}, bf16[128,2048]{1,0:T(8,128)(2,1)S(1)}, u32[]{:S(2)}, u32[]{:S(2)}) collective-permute-start(bf16[128,2048]{1,0:T(8,128)(2,1)S(1)} %add_convert_fusion.4), channel_id=1, source_target_pairs={{0,8},{2,10},{8,16},{10,18},{16,24},{18,26},{24,28},{26,30},{28,20... | collective-permute-start | bytes 1572872 | tf_op jit(solution)/shard_map/ppermute | solution.py:301
  199.1 24.3 %collective-permute-start.35 = (bf16[128,2048]{1,0:T(8,128)(2,1)S(1)}, bf16[128,2048]{1,0:T(8,128)(2,1)S(1)}, u32[]{:S(2)}, u32[]{:S(2)}) collective-permute-start(bf16[128,2048]{1,0:T(8,128)(2,1)S(1)} %add_convert_fusion.1), channel_id=1, source_target_pairs={{0,4},{2,6},{8,0},{10,2},{16,8},{18,10},{24,16},{26,18},{28,24},{3... | collective-permute-start | bytes 1572872 | tf_op jit(solution)/shard_map/ppermute | solution.py:302
  (67 other events, 966.9 us)

commit v2 on v1

v2 whole, which is shorter than its diff:
```python
import functools

import jax
import jax.numpy as jnp
import numpy as np
from jax import lax
from jax.experimental import pallas as pl
from jax.experimental.pallas import tpu as pltpu
from jax.sharding import PartitionSpec as P

CORES = 2
VMEM = 24 * 1024 * 1024
DEPTH = 2048
ROUTE_CHUNKS = 4
ROOMY = 8 * 1024 * 1024


def ring_order(chips):
    return list(range(0, chips, 2)) + list(range(1, chips, 2))[::-1]


def ring_pairs(chips, step):
    order = ring_order(chips)
    return [
        (CORES * chip + core, CORES * order[(at + step) % chips] + core)
        for at, chip in enumerate(order)
        for core in range(CORES)
    ]


def core_pairs(devices):
    return [(i, i ^ 1) for i in range(devices)]


def source_table(devices):
    chips = devices // CORES
    order = ring_order(chips)
    place = {chip: at for at, chip in enumerate(order)}
    table = np.zeros((devices, devices), np.int32)
    for device in range(devices):
        at, core = place[device // CORES], device % CORES
        offsets = [0]
        for far in range(1, chips // 2):
            offsets += [-far, far]
        offsets.append(chips // 2)
        for j, offset in enumerate(offsets):
            chip = order[(at + offset) % chips]
            table[device, 2 * j] = CORES * chip + core
            table[device, 2 * j + 1] = CORES * chip + 1 - core
    return table


def dot(left, right, left_dim, right_dim):
    return lax.dot_general(
        left, right, (((left_dim,), (right_dim,)), ((), ())), preferred_element_type=jnp.float32
    )


def route_kernel(counts, sources, *refs):
    blocks = len(counts)
    grads, refs = refs[: sum(counts)], refs[sum(counts) :]
    saved_ref, gate_ref, down_ref, up_ref, both_out, scaled_out, gate_out, refs = *refs[:7], refs[7:]
    outs, (both_ref, scaled_ref, gate_grad_ref, route_ref, sems) = refs[:blocks], refs[blocks:]
    hidden = down_ref.shape[0]
    tokens, width = outs[0].shape
    slots = saved_ref.shape[1]
    rows = jnp.concatenate([ref[...] for ref in grads], axis=0)
    projected = dot(rows, down_ref[...], 1, 1)
    line = lax.broadcasted_iota(jnp.int32, (tokens, tokens), 0)
    lane = lax.broadcasted_iota(jnp.int32, (tokens, tokens), 1)
    earlier = (line < lane).astype(jnp.bfloat16)
    diagonal = line == lane
    slot = lax.broadcasted_iota(jnp.int32, (slots, tokens), 0).astype(jnp.float32)
    saved, weights = [], []
    for i in range(blocks):
        gates = gate_ref[sources[i]]
        named = gates > 0.0
        counted = jnp.broadcast_to(named.astype(jnp.bfloat16), (16, tokens))
        rank = dot(counted, earlier, 1, 0)[:1]
        rank = jnp.where(named, rank, -1.0)
        pick = (slot == rank).astype(jnp.bfloat16)
        saved.append(dot(pick, saved_ref[sources[i]], 0, 0))
        weights.append(jnp.sum(jnp.where(diagonal, gates, 0.0), axis=1, keepdims=True))
    saved = jnp.concatenate(saved, axis=0)
    weights = jnp.concatenate(weights, axis=0)
    gate_in, up_in = saved[:, :hidden], saved[:, hidden:]
    logistic = jax.nn.sigmoid(gate_in)
    swish = gate_in * logistic
    activated = swish * up_in
    gate_grad = jnp.sum(activated * projected, axis=1, keepdims=True)
    for i in range(blocks):
        column = gate_grad[i * tokens : (i + 1) * tokens]
        gate_grad_ref[i : i + 1] = jnp.sum(jnp.where(diagonal, column, 0.0), axis=0, keepdims=True)
    hidden_grad = weights * projected
    up_grad = hidden_grad * swish
    pre_grad = hidden_grad * up_in * logistic * (1.0 + gate_in * (1.0 - logistic))
    both = jnp.concatenate([pre_grad, up_grad], axis=1).astype(jnp.bfloat16)
    both_ref[...] = both
    scaled_ref[...] = (weights * activated).astype(jnp.bfloat16)
    copies = [
        pltpu.make_async_copy(both_ref, both_out, sems.at[0]),
        pltpu.make_async_copy(scaled_ref, scaled_out, sems.at[1]),
        pltpu.make_async_copy(gate_grad_ref, gate_out, sems.at[2]),
    ]
    for copy in copies:
        copy.start()
    chunk = width // ROUTE_CHUNKS
    for part in range(ROUTE_CHUNKS):
        columns = slice(part * chunk, (part + 1) * chunk)
        route_ref[:, columns] = dot(both, up_ref[columns], 1, 1).astype(jnp.bfloat16)
        for i, out in enumerate(outs):
            copies.append(
                pltpu.make_async_copy(
                    route_ref.at[i * tokens : (i + 1) * tokens, columns],
                    out.at[:, columns],
                    sems.at[3 + part * blocks + i],
                )
            )
            copies[-1].start()
    for copy in copies:
        copy.wait()


def in_vmem(count):
    return [pl.BlockSpec(memory_space=pltpu.VMEM)] * count


def in_hbm(count):
    return [pl.BlockSpec(memory_space=pltpu.HBM)] * count


def route_blocks(blocks, sources, saved, gates, gate_up_weight, down_weight):
    pieces = [piece for block in blocks for piece in block]
    width = pieces[0].shape[1]
    tokens = sum(piece.shape[0] for piece in blocks[0])
    hidden = down_weight.shape[0]
    count = len(blocks)
    shapes = [
        ((count * tokens, 2 * hidden), jnp.bfloat16),
        ((count * tokens, hidden), jnp.bfloat16),
        ((count, tokens), jnp.float32),
    ]
    outs = shapes + [((tokens, width), jnp.bfloat16)] * count
    scratch = shapes + [((count * tokens, width), jnp.bfloat16)]
    return pl.pallas_call(
        functools.partial(route_kernel, [len(block) for block in blocks]),
        in_specs=[pl.BlockSpec(memory_space=pltpu.SMEM)] + in_vmem(len(pieces) + 4),
        out_specs=in_hbm(len(outs)),
        out_shape=[pltpu.HBM(*out) for out in outs],
        scratch_shapes=[pltpu.VMEM(*shape) for shape in scratch]
        + [pltpu.SemaphoreType.DMA((3 + ROUTE_CHUNKS * count,))],
        compiler_params=pltpu.CompilerParams(vmem_limit_bytes=VMEM),
        cost_estimate=pl.CostEstimate(
            flops=6 * count * tokens * width * hidden, bytes_accessed=16 << 20, transcendentals=0
        ),
        name="route",
    )(sources, *pieces, saved, gates, down_weight, gate_up_weight)


def weight_kernel(n_wide, n_narrow, wide_first, share, *refs):
    wide, narrow, refs = refs[:n_wide], refs[n_wide : n_wide + n_narrow], refs[n_wide + n_narrow :]
    out_ref, left, right = refs
    at = 0
    for ref in wide:
        left[at : at + ref.shape[0]] = ref[...]
        at += ref.shape[0]

    @pl.when(pl.program_id(0) == 0)
    def _():
        at = 0
        for ref in narrow:
            right[at : at + ref.shape[0]] = ref[...]
            at += ref.shape[0]

    first, second = (left, right) if wide_first else (right, left)
    depth = left.shape[0]
    if depth <= DEPTH or depth % DEPTH:
        out_ref[...] = dot(first[...], second[...], 0, 0).astype(out_ref.dtype)
        return

    def step(k, total):
        part = pl.ds(pl.multiple_of(k * DEPTH, DEPTH), DEPTH)
        return total + dot(first[part], second[part], 0, 0)

    total = lax.fori_loop(0, depth // DEPTH, step, jnp.zeros(out_ref.shape, jnp.float32))
    out_ref[...] = total.astype(out_ref.dtype)


def weight_grad(wide, narrow, share, shares, wide_first, dtype):
    wide, narrow = [[pltpu.with_memory_space_constraint(x, pltpu.HBM) for x in group] for group in (wide, narrow)]
    width = wide[0].shape[1]
    part = width // shares
    chunk = min(512, part)
    steps = part // chunk
    depth = sum(piece.shape[0] for piece in wide)
    thin = narrow[0].shape[1]
    if wide_first:
        shape, block, place = (part, thin), (chunk, thin), lambda i, share: (i, 0)
    else:
        shape, block, place = (thin, part), (thin, chunk), lambda i, share: (0, i)
    return pl.pallas_call(
        functools.partial(weight_kernel, len(wide), len(narrow), wide_first),
        grid_spec=pltpu.PrefetchScalarGridSpec(
            num_scalar_prefetch=1,
            grid=(steps,),
            in_specs=[
                pl.BlockSpec((piece.shape[0], chunk), lambda i, share: (0, share[0] * steps + i))
                for piece in wide
            ]
            + [pl.BlockSpec(piece.shape, lambda i, share: (0, 0)) for piece in narrow],
            out_specs=pl.BlockSpec(block, place),
            scratch_shapes=[
                pltpu.VMEM((depth, chunk), wide[0].dtype),
                pltpu.VMEM((depth, thin), narrow[0].dtype),
            ],
        ),
        out_shape=pltpu.HBM(shape, dtype),
        compiler_params=pltpu.CompilerParams(vmem_limit_bytes=2 * VMEM),
        cost_estimate=pl.CostEstimate(
            flops=2 * depth * part * thin, bytes_accessed=4 * depth * (part + thin) * 2, transcendentals=0
        ),
        name="weight_grad",
    )(share, *wide, *narrow)


def thirds(part):
    units = part // 128
    sizes = [128 * (units // 3 + (i < units % 3)) for i in range(3)]
    return [size for size in sizes if size]


class Ring:
    def __init__(self, block, devices):
        chips = devices // CORES
        self.far = chips // 2
        self.paths = ring_pairs(chips, 1), ring_pairs(chips, -1)
        self.across = core_pairs(devices)
        self.heads = block, block
        self.fresh = [[block]]
        self.own, self.sib = [], []
        self.sent = 0

    def send(self):
        self.sent += 1
        rising, falling = self.heads
        half = rising.shape[0] // 2
        if self.sent == self.far:
            rising, falling = rising[:half], falling[half:]
        rising = lax.ppermute(rising, "expert", self.paths[0])
        falling = lax.ppermute(falling, "expert", self.paths[1])
        self.heads = rising, falling
        return [[rising, falling]] if self.sent == self.far else [[rising], [falling]]

    def share(self):
        for pieces in self.fresh:
            self.own.append(pieces)
            self.sib.append([lax.ppermute(piece, "expert", self.across) for piece in pieces])
        self.fresh = []

    def state(self):
        return self.heads, self.fresh, self.own, self.sib

    def restore(self, state):
        self.heads, self.fresh, self.own, self.sib = state

    def pieces(self):
        return [piece for own, sib in zip(self.own, self.sib) for piece in own + sib]


class Sum:
    def __init__(self, devices, rows):
        chips = devices // CORES
        self.far = chips // 2
        self.paths = ring_pairs(chips, 1), ring_pairs(chips, -1)
        self.half = rows // 2
        self.parts = {}
        self.heads = None
        self.sent = 0

    def total(self, j, arrived=(), cut=slice(None)):
        total = sum(part[cut].astype(jnp.float32) for part in self.parts[j])
        for value in arrived:
            total = total + value.astype(jnp.float32)
        return total.astype(jnp.bfloat16)

    def send(self):
        self.sent += 1
        if self.sent == 1:
            rising = self.total(2 * self.far - 1, (), slice(0, self.half))
            falling = self.total(2 * self.far - 1, (), slice(self.half, None))
        else:
            rising, falling = self.heads
            if self.sent == 2:
                rising = jnp.pad(rising, ((0, self.half), (0, 0)))
                falling = jnp.pad(falling, ((self.half, 0), (0, 0)))
            left = self.far + 1 - self.sent
            rising = self.total(2 * left, [rising])
            falling = self.total(2 * left - 1, [falling])
        rising, falling = fence(rising, falling)
        rising = lax.ppermute(rising, "expert", self.paths[0])
        falling = lax.ppermute(falling, "expert", self.paths[1])
        self.heads = rising, falling


class Swap:
    def __init__(self, values):
        self.shares = len(values) + 1
        self.sizes = thirds(values[0].shape[0])
        self.starts = [sum(self.sizes[:i]) for i in range(len(self.sizes))]
        self.parts = [[value[at : at + size] for value in values] for at, size in zip(self.starts, self.sizes)]
        self.come = []

    def send(self):
        if len(self.come) < len(self.parts):
            parts = self.parts[len(self.come)]
            if self.come:
                parts = fence(parts, self.come[-1])[0]
            self.come.append(
                [
                    lax.ppermute(part, "dp", [(i, (i + k) % self.shares) for i in range(self.shares)])
                    for k, part in enumerate(parts, 1)
                ]
            )

    def add_to(self, total):
        while len(self.come) < len(self.parts):
            self.send()
        for k in range(self.shares - 1):
            arrived = jnp.concatenate([parts[k] for parts in self.come], axis=0)
            total = total + arrived.astype(jnp.float32)
        return total


def fence(*values):
    return lax.optimization_barrier(values)


def on_device(tokens, d_output, expert_ids, gate_weights, pre_acts, w_gate_up, w_down):
    devices = lax.axis_size("expert")
    chips = devices // CORES
    far = chips // 2
    across = core_pairs(devices)
    me = lax.axis_index("expert")
    rows = tokens.shape[0]
    roomy = devices * rows * tokens.shape[1] <= ROOMY
    table = source_table(devices)
    sources = lax.dynamic_index_in_dim(jnp.asarray(table), me, 0, keepdims=False)
    numbered = lax.dynamic_index_in_dim(jnp.asarray(np.argsort(table, axis=1).astype(np.int32)), me, 0, keepdims=False)
    names = jnp.arange(devices, dtype=jnp.int32)[:, None, None] == expert_ids[None]
    saved = pre_acts[0, 0].reshape(devices, pre_acts.shape[2] // devices, pre_acts.shape[3])

    grads, inputs, home = Ring(d_output, devices), Ring(tokens, devices), Sum(devices, rows)
    waiting = {}

    def trade():
        for j in list(waiting):
            own, sib = waiting.pop(j)
            home.parts[j] = [own, lax.ppermute(sib, "expert", across)]
            if not roomy:
                home.parts[j] = [home.total(j)]

    def by(ring, *values):
        ring.heads = fence(ring.heads, values)[0]

    send_gates = jnp.sum(jnp.where(names, gate_weights[None].astype(jnp.float32), 0.0), axis=2)
    gates = lax.all_to_all(send_gates.astype(jnp.bfloat16), "expert", split_axis=0, concat_axis=0, tiled=True)
    gates = gates.astype(jnp.float32).reshape(devices, 1, rows)
    shares, share = lax.axis_size("dp"), lax.axis_index("dp")

    def weight_part(ring, kind, far_share, dtype):
        whose = ((share + far_share) % shares).astype(jnp.int32).reshape(1)
        return weight_grad(ring.pieces(), [record[kind] for record in records], whose, shares, kind == 0, dtype)

    def partners(ring, kind):
        return [weight_part(ring, kind, k, jnp.bfloat16) for k in range(1, shares)]

    records = []

    def work(job):
        if not job:
            return
        blocks = [block for j in job for block in (grads.own[j], grads.sib[j])]
        first = 2 * job[0]
        record = route_blocks(blocks, sources[first : first + len(blocks)], saved, gates, w_gate_up[0], w_down[0])
        records.append(record[:3])
        for i, j in enumerate(job):
            waiting[j] = record[3 + 2 * i : 5 + 2 * i]

    pairs = list(range(chips))
    if roomy and far > 3:
        jobs = [pairs[:1]] + [pairs[2 * k - 1 : 2 * k + 1] for k in range(1, far - 2)]
        jobs += [pairs[2 * far - 5 : 2 * far - 4], pairs[2 * far - 4 : -1], pairs[-1:]]
    else:
        jobs = [pairs[:1]] + [pairs[2 * k - 1 : 2 * k + 1] for k in range(1, far)] + [pairs[-1:]]
    done = 0

    for step in range(1, far + 1):
        if step == 2:
            by(grads, gates)
        if step > 2:
            by(grads, records, home.parts if step == far else ())
        grads.share()
        grads.fresh = grads.send()
        if step > 1:
            if step < far - 1:
                trade()
            work(jobs[done])
            if step == far - 1:
                trade()
            done += 1
    down_swap = None
    if not roomy:
        while done < len(jobs):
            grads.share()
            trade()
            work(jobs[done])
            done += 1
        trade()
        down_swap = Swap(partners(grads, 1))
        down = weight_part(grads, 1, 0, jnp.float32)
        by(inputs, down, down_swap.parts)
        inputs.fresh = [[inputs.heads[0]]]
    for step in range(1, far + 1):
        if roomy:
            by(inputs, grads.heads, records)
        if step == far:
            by(inputs, down_swap.come)
        inputs.share()
        if roomy:
            grads.share()
        inputs.fresh = inputs.send()
        trade()
        if done < len(jobs):
            work(jobs[done])
            done += 1
        elif down_swap is None:
            down_swap = Swap(partners(grads, 1))
            down_swap.send()
    down_swap.send()
    inputs.share()
    gate_grads = jnp.concatenate([record[2] for record in records], axis=0).astype(jnp.bfloat16)
    home_gates = lax.all_to_all(gate_grads[numbered], "expert", split_axis=0, concat_axis=0, tiled=True)
    home.parts = fence(home.parts, inputs.heads, inputs.sib[-1], down_swap.come)[0]
    up_swap = None
    for step in range(1, far + 1):
        if step == 2:
            by(home, up_swap.parts, down_swap.come)
        if step > 2:
            by(home, up_swap.come[: step - 2])
        home.send()
        if step == 1:
            down_swap.send()
            up_swap = Swap(partners(inputs, 0))
        up_swap.send()
    if roomy:
        down = weight_part(grads, 1, 0, jnp.float32)
    down = down_swap.add_to(down)
    up = up_swap.add_to(weight_part(inputs, 0, 0, jnp.float32))
    gate_out = jnp.sum(jnp.where(names, home_gates.astype(jnp.float32)[:, :, None], 0.0), axis=0)
    gate_out = gate_out.astype(jnp.bfloat16)
    token_grads = home.total(0, home.heads)
    return token_grads, gate_out, up[None], down[None]


def solution(mesh):
    placed = (
        P(("expert", "dp"), None),
        P(("expert", "dp"), None),
        P(("expert", "dp"), None),
        P(("expert", "dp"), None),
        P("dp", "expert", None, None),
        P("expert", None, None),
        P("expert", None, None),
    )
    return jax.shard_map(
        on_device,
        mesh=mesh,
        in_specs=placed,
        out_specs=(
            P(("expert", "dp"), None),
            P(("expert", "dp"), None),
            P("expert", "dp", None),
            P("expert", None, "dp"),
        ),
        check_vma=False,
    )
```

time: 251 us -> 191 us (0.76)
  waiting for transfers between devices: 89.6 us -> 54.3 us
  Pallas kernels: 84.4 us -> 52.7 us
  local copies, waits for them, and re-layouts: 5.25 us -> 15.7 us
  other arithmetic: 22.6 us -> 17.1 us
    ppermute x52 -> x56, waiting for transfers between devices: 89.6 us -> 47.9 us  [the longest x12 19.5 us: send(): rising = lax.ppermute(rising, 'expert', self.paths[0])]
    pallas_call x8 -> x5, Pallas kernels: 53.5 us -> 24.7 us  [route_blocks(): pl.pallas_call(functools.partial(route_kernel, [len(block) for block in b...]
    unnamed x74 -> x128, local copies, waits for them, and re-layouts: 1.1 us -> 9.77 us
    all_to_all x1, waiting for transfers between devices: 0.01 us -> 6.44 us  [on_device(): lax.all_to_all(send_gates.astype(jnp.bfloat16), 'expert', split_axis=0, c...]
    another operation x9 -> x5, other arithmetic: 5.21 us -> 0.02 us
    ppermute x52 -> x56, starting transfers between devices: 35.4 us -> 38.6 us  [the longest x12 14 us: send(): rising = lax.ppermute(rising, 'expert', self.paths[0])]
    pallas_call x4, Pallas kernels: 30.9 us -> 28 us  [weight_grad(): pl.pallas_call(functools.partial(weight_kernel, len(wide), len(narrow), w...]
  transfers between devices with their start and end apart: 54 -> 58, of which waited for: 11 -> 25; matrix products, arithmetic and copies ran while one was open for 9% -> 11% of each run, Pallas kernels for 34% -> 28%
where the time goes in v2:
time: 191 us; the launch traced here: 190 us
  waiting for transfers between devices  54.3 us (28%)
  Pallas kernels  52.7 us (28%)
  starting transfers between devices  48.8 us (26%)
  other arithmetic  17.1 us (9%)
  local copies, waits for them, and re-layouts  15.7 us (8%)
    pallas_call x4, Pallas kernels, weight_grad(): pl.pallas_call(functools.partial(weight_kernel, len(wide), len(narrow), w...  28 us
    pallas_call x5, Pallas kernels, route_blocks(): pl.pallas_call(functools.partial(route_kernel, [len(block) for block in b...  24.7 us
    ppermute x12, waiting for transfers between devices, send(): rising = lax.ppermute(rising, 'expert', self.paths[0])  19.5 us
    ppermute x6, waiting for transfers between devices, send(): lax.ppermute(part, 'dp', [(i, (i + k) % self.shares) for i in range(self....  16.5 us
    ppermute x12, starting transfers between devices, send(): rising = lax.ppermute(rising, 'expert', self.paths[0])  14 us
    ppermute x12, starting transfers between devices, send(): falling = lax.ppermute(falling, 'expert', self.paths[1])  12 us
    ppermute x12, waiting for transfers between devices, send(): falling = lax.ppermute(falling, 'expert', self.paths[1])  9.85 us
    unnamed x128, local copies, waits for them, and re-layouts  9.77 us
  transfers between devices with their start and end apart: 58, of which 25 were waited for; matrix products, arithmetic and copies ran while one was open for 11% of the time, Pallas kernels for 28%

profile of v2, /device:TPU:0, one launch (start us, length us, event | category | flops | bytes accessed | tf_op | source)
XLA Modules:
  0.0 190.1 jit_solution(9789505339763743268)
XLA Ops:
  0.6 3.1 %collective-permute-start.2 = (bf16[128,2048]{1,0:T(8,128)(2,1)}, bf16[128,2048]{1,0:T(8,128)(2,1)S(1)}, u32[]{:S(2)}, u32[]{:S(2)}) collective-permute-start(bf16[128,2048]{1,0:T(8,128)(2,1)} %refs_0_.9), channel_id=1, source_target_pairs={{0,8},{2,10},{8,16},{10,18},{16,24},{18,26},{24,28},{26,30},{28,20... | collective-permute-start | bytes 1572872 | tf_op jit(solution)/shard_map/ppermute | solution.py:249
  5.7 6.5 %all-to-all-start = ((bf16[16,1,128]{2,1,0:T(2,128)(2,1)}), bf16[16,1,128]{2,1,0:T(2,128)(2,1)S(1)}, u32[]{:S(2)}, u32[]{:S(2)}) async-start(bf16[16,1,128]{2,1,0:T(2,128)(2,1)} %copy.22), calls=%async_computation | async-start | bytes 16384 | tf_op jit(solution)/shard_map/all_to_all | solution.py:366
  12.9 6.4 %all-to-all-done = bf16[16,1,128]{2,1,0:T(2,128)(2,1)S(1)} async-done(((bf16[16,1,128]{2,1,0:T(2,128)(2,1)}), bf16[16,1,128]{2,1,0:T(2,128)(2,1)S(1)}, u32[]{:S(2)}, u32[]{:S(2)}) %all-to-all-start) | async-done | bytes 4128 | tf_op jit(solution)/shard_map/all_to_all | solution.py:366
  28.3 3.6 %route.5 = (bf16[256,768]{1,0:T(8,128)(2,1)}, bf16[256,384]{1,0:T(8,128)(2,1)}, f32[2,128]{1,0:T(2,128)}, bf16[128,2048]{1,0:T(8,128)(2,1)}, bf16[128,2048]{1,0:T(8,128)(2,1)}) custom-call(s32[2]{0:T(128)S(1)} %get-tuple-element.175.sources, bf16[128,2048]{1,0:T(8,128)(2,1)S(1)} %copy-done.8, bf16[128,2048]{1,0:T(8,128)(2,1)S(1)} %collective-permute-done.refs_1_, ...), custom_call_target="tpu_custom_call" | custom-call | flops 1207959552 | bytes 16777216 | tf_op jit(solution)/shard_map/route/pallas_call | solution.py:145
  36.4 5.6 %route.6 = (bf16[512,768]{1,0:T(8,128)(2,1)}, bf16[512,384]{1,0:T(8,128)(2,1)}, f32[4,128]{1,0:T(4,128)}, bf16[128,2048]{1,0:T(8,128)(2,1)}, bf16[128,2048]{1,0:...) custom-call(s32[4]{0:T(128)S(1)} %slice_bitcast_fusion.3.sources, ...), custom_call_target="tpu_custom_call" | custom-call | flops 2415919104 | bytes 16777216 | tf_op jit(solution)/shard_map/route/pallas_call | solution.py:145
  42.7 4.1 %collective-permute-done.13.refs_2_.refs_10_ = bf16[128,2048]{1,0:T(8,128)(2,1)S(1)} collective-permute-done((bf16[128,2048]{1,0:T(8,128)(2,1)S(1)}, bf16[128,2048]{1,0:T(8,128)(2,1)S(1)}, u32[]{:S(2)}, u32[]{:S(2)}) %collective-permute-start.13) | collective-permute-done | bytes 524320 | tf_op jit(solution)/shard_map/ppermute | solution.py:249
  49.9 3.6 %route.7 = (bf16[256,768]{1,0:T(8,128)(2,1)}, bf16[256,384]{1,0:T(8,128)(2,1)}, f32[2,128]{1,0:T(2,128)}, bf16[128,2048]{1,0:T(8,128)(2,1)}, bf16[128,2048]{1,0:T(8,128)(2,1)}) custom-call(s32[2]{0:T(128)S(1)} %get-tuple-element.174.sources, bf16[128,2048]{1,0:T(8,128)(2,1)S(1)} %collective-permute-done.8.refs_0_.refs_6_, ...), custom_call_target="tpu_custom_call" | custom-call | flops 1207959552 | bytes 16777216 | tf_op jit(solution)/shard_map/route/pallas_call | solution.py:145
  53.5 2.7 %collective-permute-done.20.refs_0_.refs_14_ = bf16[64,2048]{1,0:T(8,128)(2,1)S(1)} collective-permute-done((bf16[64,2048]{1,0:T(8,128)(2,1)S(1)}, bf16[64,2048]{1,0:T(8,128)(2,1)S(1)}, u32[]{:S(2)}, u32[]{:S(2)}) %collective-permute-start.20) | collective-permute-done | bytes 262176 | tf_op jit(solution)/shard_map/ppermute | solution.py:249
  58.8 7.7 %route.8 = (bf16[768,768]{1,0:T(8,128)(2,1)}, bf16[768,384]{1,0:T(8,128)(2,1)}, f32[6,128]{1,0:T(8,128)}, bf16[128,2048]{1,0:T(8,128)(2,1)}, bf16[128,2048]{1,0:...) custom-call(s32[6]{0:T(128)S(1)} %slice_bitcast_fusion.1.sources, ...), custom_call_target="tpu_custom_call" | custom-call | flops 3623878656 | bytes 16777216 | tf_op jit(solution)/shard_map/route/pallas_call | solution.py:145
  66.5 3.1 %collective-permute-done.25.refs_2_ = bf16[128,2048]{1,0:T(8,128)(2,1)} collective-permute-done((bf16[128,2048]{1,0:T(8,128)(2,1)S(1)}, bf16[128,2048]{1,0:T(8,128)(2,1)}, u32[]{:S(2)}, u32[]{:S(2)}) %collective-permute-start.25) | collective-permute-done | bytes 524320 | tf_op jit(solution)/shard_map/ppermute | solution.py:249
  77.6 4.2 %route.9 = (bf16[256,768]{1,0:T(8,128)(2,1)}, bf16[256,384]{1,0:T(8,128)(2,1)}, f32[2,128]{1,0:T(2,128)}, bf16[128,2048]{1,0:T(8,128)(2,1)}, bf16[128,2048]{1,0:T(8,128)(2,1)}) custom-call(s32[2]{0:T(128)S(1)} %get-tuple-element.173.sources, bf16[64,2048]{1,0:T(8,128)(2,1)S(1)} %collective-permute-done.20.refs_0_.refs_14_, ...), custom_call_target="tpu_custom_call" | custom-call | flops 1207959552 | bytes 16777216 | tf_op jit(solution)/shard_map/route/pallas_call | solution.py:145
  84.3 5.7 %weight_grad.4 = bf16[384,1024]{1,0:T(8,128)(2,1)} custom-call(s32[1]{0:T(128)} %bitcast.9.share, bf16[128,2048]{1,0:T(8,128)(2,1)} %refs_0_.9, bf16[128,2048]{1,0:T(8,128)(2,1)} %copy-done.9, bf16[128,2048]{1,0:T(8,128)(2,1)} %copy-done.12, bf16[128,2048]{1,0:T(8,128)(2,1)} %copy-done.14, bf16[128,2048]{1,0:T(8,128)(2,1)} %copy-done.13, ...), custom_call_target="tpu_custom_call" | custom-call | flops 1610612736 | bytes 23068672 | tf_op jit(solution)/shard_map/weight_grad/pallas_call | solution.py:201
  94.3 4.8 %collective-permute-done.31 = bf16[128,1024]{1,0:T(8,128)(2,1)} collective-permute-done((bf16[128,1024]{1,0:T(8,128)(2,1)S(1)}, bf16[128,1024]{1,0:T(8,128)(2,1)}, u32[]{:S(2)}, u32[]{:S(2)}) %collective-permute-start.31) | collective-permute-done | bytes 262176 | tf_op jit(solution)/shard_map/ppermute | solution.py:320
  99.6 3.4 %collective-permute-done.30.refs_12_ = bf16[128,2048]{1,0:T(8,128)(2,1)S(1)} collective-permute-done((bf16[128,2048]{1,0:T(8,128)(2,1)}, bf16[128,2048]{1,0:T(8,128)(2,1)S(1)}, u32[]{:S(2)}, u32[]{:S(2)}) %collective-permute-start.30) | collective-permute-done | bytes 524320 | tf_op jit(solution)/shard_map/ppermute | solution.py:250
  104.5 4.8 %collective-permute-done.36 = bf16[128,1024]{1,0:T(8,128)(2,1)S(1)} collective-permute-done((bf16[128,1024]{1,0:T(8,128)(2,1)S(1)}, bf16[128,1024]{1,0:T(8,128)(2,1)S(1)}, u32[]{:S(2)}, u32[]{:S(2)}) %collective-permute-start.36) | collective-permute-done | bytes 262176 | tf_op jit(solution)/shard_map/ppermute | solution.py:320
  112.2 5.9 %collective-permute-done.32.refs_14_ = bf16[64,2048]{1,0:T(8,128)(2,1)S(1)} collective-permute-done((bf16[64,2048]{1,0:T(8,128)(2,1)S(1)}, bf16[64,2048]{1,0:T(8,128)(2,1)S(1)}, u32[]{:S(2)}, u32[]{:S(2)}) %collective-permute-start.32) | collective-permute-done | bytes 262176 | tf_op jit(solution)/shard_map/ppermute | solution.py:249
  121.4 8.1 %weight_grad.5 = bf16[1024,768]{1,0:T(8,128)(2,1)} custom-call(s32[1]{0:T(128)} %bitcast.9.share, bf16[128,2048]{1,0:T(8,128)(2,1)} %refs_0_.8, bf16[128,2048]{1,0:T(8,128)(2,1)} %copy-done.28, bf16[128,2048]{1,0:T(8,128)(2,1)} %collective-permute-done.25.refs_2_, bf16[128,2048]{1,0:T(8,128)(2,1)} %copy-done.29, ...), custom_call_target="tpu_custom_call" | custom-call | flops 3221225472 | bytes 29360128 | tf_op jit(solution)/shard_map/weight_grad/pallas_call | solution.py:201
  135.9 4.7 %collective-permute-done.46 = bf16[128,1024]{1,0:T(8,128)(2,1)S(1)} collective-permute-done((bf16[128,1024]{1,0:T(8,128)(2,1)S(1)}, bf16[128,1024]{1,0:T(8,128)(2,1)S(1)}, u32[]{:S(2)}, u32[]{:S(2)}) %collective-permute-start.46) | collective-permute-done | bytes 262176 | tf_op jit(solution)/shard_map/ppermute | solution.py:320
  146.7 3.7 %all-to-all-start.1 = ((bf16[16,1,128]{2,1,0:T(2,128)(2,1)}), bf16[16,1,128]{2,1,0:T(2,128)(2,1)S(1)}, u32[]{:S(2)}, u32[]{:S(2)}) async-start(bf16[16,1,128]{2,1,0:T(2,128)(2,1)} %copy.23), calls=%async_computation.1 | async-start | bytes 16384 | tf_op jit(solution)/shard_map/all_to_all | solution.py:442
  161.4 5.8 %weight_grad.7 = f32[384,1024]{1,0:T(8,128)} custom-call(s32[1]{0:T(128)} %bitcast.14.share, bf16[128,2048]{1,0:T(8,128)(2,1)} %refs_0_.9, bf16[128,2048]{1,0:T(8,128)(2,1)} %copy-done.9, bf16[128,2048]{1,0:T(8,128)(2,1)} %copy-done.12, bf16[128,2048]{1,0:T(8,128)(2,1)} %copy-done.14, bf16[128,2048]{1,0:T(8,128)(2,1)} %copy-done.13, ...), custom_call_target="tpu_custom_call" | custom-call | flops 1610612736 | bytes 23068672 | tf_op jit(solution)/shard_map/weight_grad/pallas_call | solution.py:201
  167.9 3.1 %add_bitcast_fusion.1 = f32[1,384,1024]{2,1,0:T(8,128)} fusion(f32[384,1024]{1,0:T(8,128)} %weight_grad.7, bf16[128,1024]{1,0:T(8,128)(2,1)} %copy-done.52, bf16[128,1024]{1,0:T(8,128)(2,1)} %copy-done.51, bf16[128,1024]{1,0:T(8,128)(2,1)} %collective-permute-done.31), kind=kLoop, calls=%fused_computation.2 | loop fusion | flops 2752512 | bytes 3932160 | tf_op jit(solution)/shard_map/broadcast_in_dim | solution.py:462
  175.7 8.3 %weight_grad.6 = f32[1024,768]{1,0:T(8,128)} custom-call(s32[1]{0:T(128)} %bitcast.14.share, bf16[128,2048]{1,0:T(8,128)(2,1)} %refs_0_.8, bf16[128,2048]{1,0:T(8,128)(2,1)} %copy-done.28, bf16[128,2048]{1,0:T(8,128)(2,1)} %collective-permute-done.25.refs_2_, bf16[128,2048]{1,0:T(8,128)(2,1)} %copy-done.29, ...), custom_call_target="tpu_custom_call" | custom-call | flops 3221225472 | bytes 29360128 | tf_op jit(solution)/shard_map/weight_grad/pallas_call | solution.py:201
  184.0 3.9 %add_bitcast_fusion = f32[1,1024,768]{2,1,0:T(8,128)} fusion(f32[1024,768]{1,0:T(8,128)} %weight_grad.6, bf16[256,768]{1,0:T(8,128)(2,1)S(1)} %collective-permute-done.55, bf16[384,768]{1,0:T(8,128)(2,1)S(1)} %collective-permute-done.52, bf16[384,768]{1,0:T(8,128)(2,1)S(1)} %collective-permute-done.49), kind=kLoop, calls=%fused_computation.1 | loop fusion | flops 5505024 | bytes 7864320 | tf_op jit(solution)/shard_map/broadcast_in_dim | solution.py:462
  187.9 2.2 %add_convert_fusion = bf16[128,2048]{1,0:T(8,128)(2,1)} fusion(bf16[128,2048]{1,0:T(8,128)(2,1)S(1)} %collective-permute-done.54, bf16[128,2048]{1,0:T(8,128)(2,1)S(1)} %collective-permute-done.53, bf16[128,2048]{1,0:T(8,128)(2,1)} %collective-permute-done.1, bf16[128,2048]{1,0:T(8,128)(2,1)S(1)} %copy-done.39), kind=kLoop, calls=%fused_computation.3 | loop fusion | flops 2097152 | bytes 2621440 | tf_op jit(solution)/shard_map/convert_element_type | solution.py:284
  (265 shorter events, 73.4 us)
Async XLA Ops:
  0.6 18.8 %collective-permute-start.2 = (bf16[128,2048]{1,0:T(8,128)(2,1)}, bf16[128,2048]{1,0:T(8,128)(2,1)S(1)}, u32[]{:S(2)}, u32[]{:S(2)}) collective-permute-start(bf16[128,2048]{1,0:T(8,128)(2,1)} %refs_0_.9), channel_id=1, source_target_pairs={{0,8},{2,10},{8,16},{10,18},{16,24},{18,26},{24,28},{26,30},{28,20... | collective-permute-start | bytes 1572872 | tf_op jit(solution)/shard_map/ppermute | solution.py:249
  3.7 15.7 %collective-permute-start.4 = (bf16[128,2048]{1,0:T(8,128)(2,1)}, bf16[128,2048]{1,0:T(8,128)(2,1)S(1)}, u32[]{:S(2)}, u32[]{:S(2)}) collective-permute-start(bf16[128,2048]{1,0:T(8,128)(2,1)} %refs_0_.9), channel_id=1, source_target_pairs={{0,4},{2,6},{8,0},{10,2},{16,8},{18,10},{24,16},{26,18},{28,24},{3... | collective-permute-start | bytes 1572872 | tf_op jit(solution)/shard_map/ppermute | solution.py:250
  3.7 18.4 %collective-permute-start = (bf16[128,2048]{1,0:T(8,128)(2,1)}, bf16[128,2048]{1,0:T(8,128)(2,1)S(1)}, u32[]{:S(2)}, u32[]{:S(2)}) collective-permute-start(bf16[128,2048]{1,0:T(8,128)(2,1)} %refs_0_.9), channel_id=1, source_target_pairs={{0,2},{2,0},{4,6},{6,4},{8,10},{10,8},{12,14},{14,12},{16,18},{18,... | collective-permute-start | bytes 1572872 | tf_op jit(solution)/shard_map/ppermute | solution.py:257
  5.7 13.6 %all-to-all-start = ((bf16[16,1,128]{2,1,0:T(2,128)(2,1)}), bf16[16,1,128]{2,1,0:T(2,128)(2,1)S(1)}, u32[]{:S(2)}, u32[]{:S(2)}) async-start(bf16[16,1,128]{2,1,0:T(2,128)(2,1)} %copy.22), calls=%async_computation | async-start | bytes 16384 | tf_op jit(solution)/shard_map/all_to_all | solution.py:366
  19.4 13.7 %collective-permute-start.11 = (bf16[128,2048]{1,0:T(8,128)(2,1)S(1)}, bf16[128,2048]{1,0:T(8,128)(2,1)S(1)}, u32[]{:S(2)}, u32[]{:S(2)}) collective-permute-start(bf16[128,2048]{1,0:T(8,128)(2,1)S(1)} %collective-permute-done.4.refs_2_.refs_4_), channel_id=1, source_target_pairs={{0,4},{2,6},{8,0},{10,2},{16,8},{18,10},{24,16},{26,18},{28,24},{3... | collective-permute-start | bytes 1572872 | tf_op jit(solution)/shard_map/ppermute | solution.py:250
  20.9 13.4 %collective-permute-start.8 = (bf16[128,2048]{1,0:T(8,128)(2,1)S(1)}, bf16[128,2048]{1,0:T(8,128)(2,1)S(1)}, u32[]{:S(2)}, u32[]{:S(2)}) collective-permute-start(bf16[128,2048]{1,0:T(8,128)(2,1)S(1)} %collective-permute-done.2.refs_0_.refs_2_), channel_id=1, source_target_pairs={{0,8},{2,10},{8,16},{10,18},{16,24},{18,26},{24,28},{26,30},{28,20... | collective-permute-start | bytes 1572872 | tf_op jit(solution)/shard_map/ppermute | solution.py:249
  21.5 14.9 %collective-permute-start.3 = (bf16[128,2048]{1,0:T(8,128)(2,1)S(1)}, bf16[128,2048]{1,0:T(8,128)(2,1)S(1)}, u32[]{:S(2)}, u32[]{:S(2)}) collective-permute-start(bf16[128,2048]{1,0:T(8,128)(2,1)S(1)} %collective-permute-done.2.refs_0_.refs_2_), channel_id=1, source_target_pairs={{0,2},{2,0},{4,6},{6,4},{8,10},{10,8},{12,14},{14,12},{16,18},{18,... | collective-permute-start | bytes 1572872 | tf_op jit(solution)/shard_map/ppermute | solution.py:257
  21.5 14.9 %collective-permute-start.5 = (bf16[128,2048]{1,0:T(8,128)(2,1)S(1)}, bf16[128,2048]{1,0:T(8,128)(2,1)S(1)}, u32[]{:S(2)}, u32[]{:S(2)}) collective-permute-start(bf16[128,2048]{1,0:T(8,128)(2,1)S(1)} %collective-permute-done.4.refs_2_.refs_4_), channel_id=1, source_target_pairs={{0,2},{2,0},{4,6},{6,4},{8,10},{10,8},{12,14},{14,12},{16,18},{18,... | collective-permute-start | bytes 1572872 | tf_op jit(solution)/shard_map/ppermute | solution.py:257
  56.6 13.0 %collective-permute-start.25 = (bf16[128,2048]{1,0:T(8,128)(2,1)S(1)}, bf16[128,2048]{1,0:T(8,128)(2,1)}, u32[]{:S(2)}, u32[]{:S(2)}) collective-permute-start(bf16[128,2048]{1,0:T(8,128)(2,1)S(1)} %copy-done.26), channel_id=1, source_target_pairs={{0,8},{2,10},{8,16},{10,18},{16,24},{18,26},{24,28},{26,30},{28,20... | collective-permute-start | bytes 1572872 | tf_op jit(solution)/shard_map/ppermute | solution.py:249
  57.7 12.6 %collective-permute-start.26 = (bf16[128,2048]{1,0:T(8,128)(2,1)S(1)}, bf16[128,2048]{1,0:T(8,128)(2,1)}, u32[]{:S(2)}, u32[]{:S(2)}) collective-permute-start(bf16[128,2048]{1,0:T(8,128)(2,1)S(1)} %copy-done.26), channel_id=1, source_target_pairs={{0,4},{2,6},{8,0},{10,2},{16,8},{18,10},{24,16},{26,18},{28,24},{3... | collective-permute-start | bytes 1572872 | tf_op jit(solution)/shard_map/ppermute | solution.py:250
  83.2 15.9 %collective-permute-start.29 = (bf16[128,2048]{1,0:T(8,128)(2,1)}, bf16[128,2048]{1,0:T(8,128)(2,1)S(1)}, u32[]{:S(2)}, u32[]{:S(2)}) collective-permute-start(bf16[128,2048]{1,0:T(8,128)(2,1)} %collective-permute-done.27.refs_6_), channel_id=1, source_target_pairs={{0,8},{2,10},{8,16},{10,18},{16,24},{18,26},{24,28},{26,30},{28,20... | collective-permute-start | bytes 1572872 | tf_op jit(solution)/shard_map/ppermute | solution.py:249
  90.1 12.9 %collective-permute-start.30 = (bf16[128,2048]{1,0:T(8,128)(2,1)}, bf16[128,2048]{1,0:T(8,128)(2,1)S(1)}, u32[]{:S(2)}, u32[]{:S(2)}) collective-permute-start(bf16[128,2048]{1,0:T(8,128)(2,1)} %collective-permute-done.28.refs_8_), channel_id=1, source_target_pairs={{0,4},{2,6},{8,0},{10,2},{16,8},{18,10},{24,16},{26,18},{28,24},{3... | collective-permute-start | bytes 1572872 | tf_op jit(solution)/shard_map/ppermute | solution.py:250
  93.8 15.6 %collective-permute-start.40 = (bf16[128,2048]{1,0:T(8,128)(2,1)}, bf16[128,2048]{1,0:T(8,128)(2,1)S(1)}, u32[]{:S(2)}, u32[]{:S(2)}) collective-permute-start(bf16[128,2048]{1,0:T(8,128)(2,1)} %collective-permute-done.25.refs_2_), channel_id=1, source_target_pairs={{0,2},{2,0},{4,6},{6,4},{8,10},{10,8},{12,14},{14,12},{16,18},{18,... | collective-permute-start | bytes 1572872 | tf_op jit(solution)/shard_map/ppermute | solution.py:257
  104.5 14.7 %collective-permute-start.43 = (bf16[128,2048]{1,0:T(8,128)(2,1)}, bf16[128,2048]{1,0:T(8,128)(2,1)S(1)}, u32[]{:S(2)}, u32[]{:S(2)}) collective-permute-start(bf16[128,2048]{1,0:T(8,128)(2,1)} %collective-permute-done.28.refs_8_), channel_id=1, source_target_pairs={{0,2},{2,0},{4,6},{6,4},{8,10},{10,8},{12,14},{14,12},{16,18},{18,... | collective-permute-start | bytes 1572872 | tf_op jit(solution)/shard_map/ppermute | solution.py:257
  119.7 13.2 %collective-permute-start.24 = (bf16[128,2048]{1,0:T(8,128)(2,1)S(1)}, bf16[128,2048]{1,0:T(8,128)(2,1)S(1)}, u32[]{:S(2)}, u32[]{:S(2)}) collective-permute-start(bf16[128,2048]{1,0:T(8,128)(2,1)S(1)} %copy-done.60), channel_id=1, source_target_pairs={{0,2},{2,0},{4,6},{6,4},{8,10},{10,8},{12,14},{14,12},{16,18},{18,... | collective-permute-start | bytes 1572872 | tf_op jit(solution)/shard_map/ppermute | solution.py:358
  119.8 13.0 %collective-permute-start.17 = (bf16[128,2048]{1,0:T(8,128)(2,1)S(1)}, bf16[128,2048]{1,0:T(8,128)(2,1)S(1)}, u32[]{:S(2)}, u32[]{:S(2)}) collective-permute-start(bf16[128,2048]{1,0:T(8,128)(2,1)S(1)} %copy-done.59), channel_id=1, source_target_pairs={{0,2},{2,0},{4,6},{6,4},{8,10},{10,8},{12,14},{14,12},{16,18},{18,... | collective-permute-start | bytes 1572872 | tf_op jit(solution)/shard_map/ppermute | solution.py:358
  135.3 17.3 %collective-permute-start.49 = (bf16[384,768]{1,0:T(8,128)(2,1)S(1)}, bf16[384,768]{1,0:T(8,128)(2,1)S(1)}, u32[]{:S(2)}, u32[]{:S(2)}) collective-permute-start(bf16[384,768]{1,0:T(8,128)(2,1)S(1)} %get-tuple-element.167), channel_id=1, source_target_pairs={{0,1},{1,0},{2,3},{3,2},{4,5},{5,4},{6,7},{7,6},{8,9},{9,8},{10,11... | collective-permute-start | bytes 1769480 | tf_op jit(solution)/shard_map/ppermute | solution.py:320
  142.5 12.8 %collective-permute-start.47 = (bf16[128,2048]{1,0:T(8,128)(2,1)S(1)}, bf16[128,2048]{1,0:T(8,128)(2,1)}, u32[]{:S(2)}, u32[]{:S(2)}) collective-permute-start(bf16[128,2048]{1,0:T(8,128)(2,1)S(1)} %add_convert_fusion.6), channel_id=1, source_target_pairs={{0,8},{2,10},{8,16},{10,18},{16,24},{18,26},{24,28},{26,30},{28,20... | collective-permute-start | bytes 1572872 | tf_op jit(solution)/shard_map/ppermute | solution.py:300
  144.1 12.5 %collective-permute-start.48 = (bf16[128,2048]{1,0:T(8,128)(2,1)S(1)}, bf16[128,2048]{1,0:T(8,128)(2,1)}, u32[]{:S(2)}, u32[]{:S(2)}) collective-permute-start(bf16[128,2048]{1,0:T(8,128)(2,1)S(1)} %add_convert_fusion.5), channel_id=1, source_target_pairs={{0,4},{2,6},{8,0},{10,2},{16,8},{18,10},{24,16},{26,18},{28,24},{3... | collective-permute-start | bytes 1572872 | tf_op jit(solution)/shard_map/ppermute | solution.py:301
  146.7 20.6 %all-to-all-start.1 = ((bf16[16,1,128]{2,1,0:T(2,128)(2,1)}), bf16[16,1,128]{2,1,0:T(2,128)(2,1)S(1)}, u32[]{:S(2)}, u32[]{:S(2)}) async-start(bf16[16,1,128]{2,1,0:T(2,128)(2,1)} %copy.23), calls=%async_computation.1 | async-start | bytes 16384 | tf_op jit(solution)/shard_map/all_to_all | solution.py:442
  152.5 18.5 %collective-permute-start.52 = (bf16[384,768]{1,0:T(8,128)(2,1)S(1)}, bf16[384,768]{1,0:T(8,128)(2,1)S(1)}, u32[]{:S(2)}, u32[]{:S(2)}) collective-permute-start(bf16[384,768]{1,0:T(8,128)(2,1)S(1)} %get-tuple-element.158), channel_id=1, source_target_pairs={{0,1},{1,0},{2,3},{3,2},{4,5},{5,4},{6,7},{7,6},{8,9},{9,8},{10,11... | collective-permute-start | bytes 1769480 | tf_op jit(solution)/shard_map/ppermute | solution.py:320
  171.1 12.9 %collective-permute-start.55 = (bf16[256,768]{1,0:T(8,128)(2,1)S(1)}, bf16[256,768]{1,0:T(8,128)(2,1)S(1)}, u32[]{:S(2)}, u32[]{:S(2)}) collective-permute-start(bf16[256,768]{1,0:T(8,128)(2,1)S(1)} %copy-done.50), channel_id=1, source_target_pairs={{0,1},{1,0},{2,3},{3,2},{4,5},{5,4},{6,7},{7,6},{8,9},{9,8},{10,11... | collective-permute-start | bytes 1179656 | tf_op jit(solution)/shard_map/ppermute | solution.py:320
  173.6 14.3 %collective-permute-start.53 = (bf16[128,2048]{1,0:T(8,128)(2,1)S(1)}, bf16[128,2048]{1,0:T(8,128)(2,1)S(1)}, u32[]{:S(2)}, u32[]{:S(2)}) collective-permute-start(bf16[128,2048]{1,0:T(8,128)(2,1)S(1)} %get-tuple-element.163), channel_id=1, source_target_pairs={{0,8},{2,10},{8,16},{10,18},{16,24},{18,26},{24,28},{26,30},{28,20... | collective-permute-start | bytes 1572872 | tf_op jit(solution)/shard_map/ppermute | solution.py:300
  174.6 13.3 %collective-permute-start.54 = (bf16[128,2048]{1,0:T(8,128)(2,1)S(1)}, bf16[128,2048]{1,0:T(8,128)(2,1)S(1)}, u32[]{:S(2)}, u32[]{:S(2)}) collective-permute-start(bf16[128,2048]{1,0:T(8,128)(2,1)S(1)} %get-tuple-element.164), channel_id=1, source_target_pairs={{0,4},{2,6},{8,0},{10,2},{16,8},{18,10},{24,16},{26,18},{28,24},{3... | collective-permute-start | bytes 1572872 | tf_op jit(solution)/shard_map/ppermute | solution.py:301
  (98 other events, 895.3 us)

commit v3 on v2

--- a/solution.py
+++ b/solution.py
@@ -10,8 +10,9 @@
 
 CORES = 2
 VMEM = 24 * 1024 * 1024
-DEPTH = 2048
+DEPTH = 512
 ROUTE_CHUNKS = 4
+LANES = 128
 ROOMY = 8 * 1024 * 1024
 
 
@@ -59,10 +60,11 @@
 def route_kernel(counts, sources, *refs):
     blocks = len(counts)
     grads, refs = refs[: sum(counts)], refs[sum(counts) :]
-    saved_ref, gate_ref, down_ref, up_ref, both_out, scaled_out, gate_out, refs = *refs[:7], refs[7:]
-    outs, (both_ref, scaled_ref, gate_grad_ref, route_ref, sems) = refs[:blocks], refs[blocks:]
+    saved_ref, gate_ref, down_ref, up_ref, both_out, scaled_out, refs = *refs[:6], refs[6:]
+    outs, (both_ref, scaled_ref, route_ref, sems) = refs[:blocks], refs[blocks:]
     hidden = down_ref.shape[0]
-    tokens, width = outs[0].shape
+    tokens = outs[0].shape[0]
+    width = up_ref.shape[0]
     slots = saved_ref.shape[1]
     rows = jnp.concatenate([ref[...] for ref in grads], axis=0)
     projected = dot(rows, down_ref[...], 1, 1)
@@ -88,9 +90,9 @@
     swish = gate_in * logistic
     activated = swish * up_in
     gate_grad = jnp.sum(activated * projected, axis=1, keepdims=True)
-    for i in range(blocks):
-        column = gate_grad[i * tokens : (i + 1) * tokens]
-        gate_grad_ref[i : i + 1] = jnp.sum(jnp.where(diagonal, column, 0.0), axis=0, keepdims=True)
+    extra = route_ref.shape[1] - width
+    at_expert = lax.broadcasted_iota(jnp.int32, (blocks * tokens, extra), 1) == sources[blocks]
+    route_ref[:, width:] = jnp.where(at_expert, gate_grad, 0.0).astype(jnp.bfloat16)
     hidden_grad = weights * projected
     up_grad = hidden_grad * swish
     pre_grad = hidden_grad * up_in * logistic * (1.0 + gate_in * (1.0 - logistic))
@@ -100,7 +102,6 @@
     copies = [
         pltpu.make_async_copy(both_ref, both_out, sems.at[0]),
         pltpu.make_async_copy(scaled_ref, scaled_out, sems.at[1]),
-        pltpu.make_async_copy(gate_grad_ref, gate_out, sems.at[2]),
     ]
     for copy in copies:
         copy.start()
@@ -108,12 +109,14 @@
     for part in range(ROUTE_CHUNKS):
         columns = slice(part * chunk, (part + 1) * chunk)
         route_ref[:, columns] = dot(both, up_ref[columns], 1, 1).astype(jnp.bfloat16)
+        if part == ROUTE_CHUNKS - 1:
+            columns = slice(part * chunk, width + extra)
         for i, out in enumerate(outs):
             copies.append(
                 pltpu.make_async_copy(
                     route_ref.at[i * tokens : (i + 1) * tokens, columns],
                     out.at[:, columns],
-                    sems.at[3 + part * blocks + i],
+                    sems.at[2 + part * blocks + i],
                 )
             )
             copies[-1].start()
@@ -138,17 +141,17 @@
     shapes = [
         ((count * tokens, 2 * hidden), jnp.bfloat16),
         ((count * tokens, hidden), jnp.bfloat16),
-        ((count, tokens), jnp.float32),
     ]
-    outs = shapes + [((tokens, width), jnp.bfloat16)] * count
-    scratch = shapes + [((count * tokens, width), jnp.bfloat16)]
+    wider = width + LANES * pl.cdiv(saved.shape[0], LANES)
+    outs = shapes + [((tokens, wider), jnp.bfloat16)] * count
+    scratch = shapes + [((count * tokens, wider), jnp.bfloat16)]
     return pl.pallas_call(
         functools.partial(route_kernel, [len(block) for block in blocks]),
         in_specs=[pl.BlockSpec(memory_space=pltpu.SMEM)] + in_vmem(len(pieces) + 4),
         out_specs=in_hbm(len(outs)),
         out_shape=[pltpu.HBM(*out) for out in outs],
         scratch_shapes=[pltpu.VMEM(*shape) for shape in scratch]
-        + [pltpu.SemaphoreType.DMA((3 + ROUTE_CHUNKS * count,))],
+        + [pltpu.SemaphoreType.DMA((2 + ROUTE_CHUNKS * count,))],
         compiler_params=pltpu.CompilerParams(vmem_limit_bytes=VMEM),
         cost_estimate=pl.CostEstimate(
             flops=6 * count * tokens * width * hidden, bytes_accessed=16 << 20, transcendentals=0
@@ -157,76 +160,78 @@
     )(sources, *pieces, saved, gates, down_weight, gate_up_weight)
 
 
+def thirds(part):
+    units = part // 128
+    sizes = [128 * (units // 3 + (i < units % 3)) for i in range(3)]
+    return [size for size in sizes if size]
+
+
+def first_rows(part):
+    return [32, part - 32]
+
+
 def weight_kernel(n_wide, n_narrow, wide_first, share, *refs):
     wide, narrow, refs = refs[:n_wide], refs[n_wide : n_wide + n_narrow], refs[n_wide + n_narrow :]
-    out_ref, left, right = refs
-    at = 0
-    for ref in wide:
-        left[at : at + ref.shape[0]] = ref[...]
-        at += ref.shape[0]
-
-    @pl.when(pl.program_id(0) == 0)
-    def _():
+    outs, (left, right, total, stage, sems) = refs[:-5], refs[-5:]
+    depth, part = left.shape
+    columns = pl.ds(pl.multiple_of(share[0] * part, 128), part)
+    copies = []
+    for sources, target, cut in ((wide, left, columns), (narrow, right, slice(None))):
         at = 0
-        for ref in narrow:
-            right[at : at + ref.shape[0]] = ref[...]
+        for ref in sources:
+            rows = slice(at, at + ref.shape[0])
+            copies.append((at, pltpu.make_async_copy(ref.at[:, cut], target.at[rows], sems.at[len(copies)])))
             at += ref.shape[0]
-
+    copies.sort(key=lambda entry: entry[0])
+    for _, copy in copies:
+        copy.start()
     first, second = (left, right) if wide_first else (right, left)
-    depth = left.shape[0]
-    if depth <= DEPTH or depth % DEPTH:
-        out_ref[...] = dot(first[...], second[...], 0, 0).astype(out_ref.dtype)
-        return
-
-    def step(k, total):
-        part = pl.ds(pl.multiple_of(k * DEPTH, DEPTH), DEPTH)
-        return total + dot(first[part], second[part], 0, 0)
-
-    total = lax.fori_loop(0, depth // DEPTH, step, jnp.zeros(out_ref.shape, jnp.float32))
-    out_ref[...] = total.astype(out_ref.dtype)
-
-
-def weight_grad(wide, narrow, share, shares, wide_first, dtype):
+    sent = []
+    for at in range(0, depth, DEPTH):
+        end = min(at + DEPTH, depth)
+        while copies and copies[0][0] < end:
+            copies.pop(0)[1].wait()
+        if end < depth:
+            product = dot(first[at:end], second[at:end], 0, 0)
+            total[...] = product if at == 0 else total[...] + product
+            continue
+        start = 0
+        for out in outs:
+            rows = slice(start, start + out.shape[0])
+            product = dot(first[at:end, rows], second[at:end], 0, 0)
+            stage[rows] = (product if at == 0 else total[rows] + product).astype(stage.dtype)
+            sent.append(pltpu.make_async_copy(stage.at[rows], out, sems.at[n_wide + n_narrow + len(sent)]))
+            sent[-1].start()
+            start += out.shape[0]
+    for copy in sent:
+        copy.wait()
+
+
+def weight_grad(wide, narrow, share, shares, wide_first, dtype, cuts):
     wide, narrow = [[pltpu.with_memory_space_constraint(x, pltpu.HBM) for x in group] for group in (wide, narrow)]
-    width = wide[0].shape[1]
-    part = width // shares
-    chunk = min(512, part)
-    steps = part // chunk
+    part = wide[0].shape[1] // shares
     depth = sum(piece.shape[0] for piece in wide)
     thin = narrow[0].shape[1]
-    if wide_first:
-        shape, block, place = (part, thin), (chunk, thin), lambda i, share: (i, 0)
-    else:
-        shape, block, place = (thin, part), (thin, chunk), lambda i, share: (0, i)
+    shape = (part, thin) if wide_first else (thin, part)
+    sizes = cuts(shape[0]) if cuts else shape[:1]
     return pl.pallas_call(
         functools.partial(weight_kernel, len(wide), len(narrow), wide_first),
-        grid_spec=pltpu.PrefetchScalarGridSpec(
-            num_scalar_prefetch=1,
-            grid=(steps,),
-            in_specs=[
-                pl.BlockSpec((piece.shape[0], chunk), lambda i, share: (0, share[0] * steps + i))
-                for piece in wide
-            ]
-            + [pl.BlockSpec(piece.shape, lambda i, share: (0, 0)) for piece in narrow],
-            out_specs=pl.BlockSpec(block, place),
-            scratch_shapes=[
-                pltpu.VMEM((depth, chunk), wide[0].dtype),
-                pltpu.VMEM((depth, thin), narrow[0].dtype),
-            ],
-        ),
-        out_shape=pltpu.HBM(shape, dtype),
+        in_specs=[pl.BlockSpec(memory_space=pltpu.SMEM)] + in_hbm(len(wide) + len(narrow)),
+        out_specs=in_hbm(len(sizes)),
+        out_shape=[pltpu.HBM((size, shape[1]), dtype) for size in sizes],
+        scratch_shapes=[
+            pltpu.VMEM((depth, part), wide[0].dtype),
+            pltpu.VMEM((depth, thin), narrow[0].dtype),
+            pltpu.VMEM(shape, jnp.float32),
+            pltpu.VMEM(shape, dtype),
+            pltpu.SemaphoreType.DMA((len(wide) + len(narrow) + len(sizes),)),
+        ],
         compiler_params=pltpu.CompilerParams(vmem_limit_bytes=2 * VMEM),
         cost_estimate=pl.CostEstimate(
             flops=2 * depth * part * thin, bytes_accessed=4 * depth * (part + thin) * 2, transcendentals=0
         ),
         name="weight_grad",
     )(share, *wide, *narrow)
-
-
-def thirds(part):
-    units = part // 128
-    sizes = [128 * (units // 3 + (i < units % 3)) for i in range(3)]
-    return [size for size in sizes if size]
 
 
 class Ring:
@@ -240,14 +245,19 @@
         self.own, self.sib = [], []
         self.sent = 0
 
-    def send(self):
+    def send(self, home=None):
         self.sent += 1
         rising, falling = self.heads
         half = rising.shape[0] // 2
         if self.sent == self.far:
             rising, falling = rising[:half], falling[half:]
+        if home is not None:
+            sums = home.sums()
+            rising, falling = [jnp.concatenate(both, axis=1) for both in ((rising, sums[0]), (falling, sums[1]))]
         rising = lax.ppermute(rising, "expert", self.paths[0])
         falling = lax.ppermute(falling, "expert", self.paths[1])
+        if home is not None:
+            home.heads = rising, falling
         self.heads = rising, falling
         return [[rising, falling]] if self.sent == self.far else [[rising], [falling]]
 
@@ -283,7 +293,7 @@
             total = total + value.astype(jnp.float32)
         return total.astype(jnp.bfloat16)
 
-    def send(self):
+    def sums(self):
         self.sent += 1
         if self.sent == 1:
             rising = self.total(2 * self.far - 1, (), slice(0, self.half))
@@ -291,12 +301,16 @@
         else:
             rising, falling = self.heads
             if self.sent == 2:
+                rising, falling = [head[:, head.shape[1] - self.parts[0][0].shape[1] :] for head in (rising, falling)]
                 rising = jnp.pad(rising, ((0, self.half), (0, 0)))
                 falling = jnp.pad(falling, ((self.half, 0), (0, 0)))
             left = self.far + 1 - self.sent
             rising = self.total(2 * left, [rising])
             falling = self.total(2 * left - 1, [falling])
-        rising, falling = fence(rising, falling)
+        return fence(rising, falling)
+
+    def send(self):
+        rising, falling = self.sums()
         rising = lax.ppermute(rising, "expert", self.paths[0])
         falling = lax.ppermute(falling, "expert", self.paths[1])
         self.heads = rising, falling
@@ -305,9 +319,7 @@
 class Swap:
     def __init__(self, values):
         self.shares = len(values) + 1
-        self.sizes = thirds(values[0].shape[0])
-        self.starts = [sum(self.sizes[:i]) for i in range(len(self.sizes))]
-        self.parts = [[value[at : at + size] for value in values] for at, size in zip(self.starts, self.sizes)]
+        self.parts = list(zip(*values))
         self.come = []
 
     def send(self):
@@ -345,7 +357,6 @@
     roomy = devices * rows * tokens.shape[1] <= ROOMY
     table = source_table(devices)
     sources = lax.dynamic_index_in_dim(jnp.asarray(table), me, 0, keepdims=False)
-    numbered = lax.dynamic_index_in_dim(jnp.asarray(np.argsort(table, axis=1).astype(np.int32)), me, 0, keepdims=False)
     names = jnp.arange(devices, dtype=jnp.int32)[:, None, None] == expert_ids[None]
     saved = pre_acts[0, 0].reshape(devices, pre_acts.shape[2] // devices, pre_acts.shape[3])
 
@@ -367,12 +378,22 @@
     gates = gates.astype(jnp.float32).reshape(devices, 1, rows)
     shares, share = lax.axis_size("dp"), lax.axis_index("dp")
 
-    def weight_part(ring, kind, far_share, dtype):
+    def weight_part(ring, kind, far_share=0):
         whose = ((share + far_share) % shares).astype(jnp.int32).reshape(1)
-        return weight_grad(ring.pieces(), [record[kind] for record in records], whose, shares, kind == 0, dtype)
+        own = far_share == 0
+        parts = weight_grad(
+            ring.pieces(),
+            [record[kind] for record in records],
+            whose,
+            shares,
+            kind == 0,
+            jnp.float32 if own else jnp.bfloat16,
+            None if own else (thirds if kind == 0 else first_rows),
+        )
+        return parts[0] if own else parts
 
     def partners(ring, kind):
-        return [weight_part(ring, kind, k, jnp.bfloat16) for k in range(1, shares)]
+        return Swap([weight_part(ring, kind, k) for k in range(1, shares)])
 
     records = []
 
@@ -381,10 +402,10 @@
             return
         blocks = [block for j in job for block in (grads.own[j], grads.sib[j])]
         first = 2 * job[0]
-        record = route_blocks(blocks, sources[first : first + len(blocks)], saved, gates, w_gate_up[0], w_down[0])
-        records.append(record[:3])
+        record = route_blocks(blocks, jnp.append(sources[first : first + len(blocks)], me.astype(jnp.int32)), saved, gates, w_gate_up[0], w_down[0])
+        records.append(record[:2])
         for i, j in enumerate(job):
-            waiting[j] = record[3 + 2 * i : 5 + 2 * i]
+            waiting[j] = record[2 + 2 * i : 4 + 2 * i]
 
     pairs = list(range(chips))
     if roomy and far > 3:
@@ -398,17 +419,14 @@
         if step == 2:
             by(grads, gates)
         if step > 2:
-            by(grads, records, home.parts if step == far else ())
+            by(grads, records[: step - 2])
         grads.share()
         grads.fresh = grads.send()
         if step > 1:
-            if step < far - 1:
-                trade()
+            trade()
             work(jobs[done])
-            if step == far - 1:
-                trade()
             done += 1
-    down_swap = None
+    down_swap = down = None
     if not roomy:
         while done < len(jobs):
             grads.share()
@@ -416,49 +434,52 @@
             work(jobs[done])
             done += 1
         trade()
-        down_swap = Swap(partners(grads, 1))
-        down = weight_part(grads, 1, 0, jnp.float32)
-        by(inputs, down, down_swap.parts)
+        down_swap = partners(grads, 1)
+        down = weight_part(grads, 1)
+        inputs.heads, down, down_swap.parts = fence(inputs.heads, down, down_swap.parts)
         inputs.fresh = [[inputs.heads[0]]]
     for step in range(1, far + 1):
         if roomy:
             by(inputs, grads.heads, records)
         if step == far:
-            by(inputs, down_swap.come)
+            inputs.heads, home.parts = fence(inputs.heads, home.parts)
         inputs.share()
         if roomy:
             grads.share()
-        inputs.fresh = inputs.send()
+        inputs.fresh = inputs.send(home if step == far else None)
         trade()
-        if done < len(jobs):
+        if step == far:
+            down_swap.send()
+            if roomy:
+                down = weight_part(grads, 1)
+        elif done < len(jobs):
             work(jobs[done])
             done += 1
         elif down_swap is None:
-            down_swap = Swap(partners(grads, 1))
+            down_swap = partners(grads, 1)
             down_swap.send()
-    down_swap.send()
     inputs.share()
-    gate_grads = jnp.concatenate([record[2] for record in records], axis=0).astype(jnp.bfloat16)
-    home_gates = lax.all_to_all(gate_grads[numbered], "expert", split_axis=0, concat_axis=0, tiled=True)
-    home.parts = fence(home.parts, inputs.heads, inputs.sib[-1], down_swap.come)[0]
     up_swap = None
-    for step in range(1, far + 1):
+    for step in range(2, far + 1):
         if step == 2:
-            by(home, up_swap.parts, down_swap.come)
-        if step > 2:
-            by(home, up_swap.come[: step - 2])
+            by(home, inputs.heads, down_swap.come, down)
+        elif step == 3:
+            by(home, up_swap.parts)
+        elif step == 4:
+            by(home, up_swap.come[:1], up)
         home.send()
-        if step == 1:
+        if step == 2:
             down_swap.send()
-            up_swap = Swap(partners(inputs, 0))
+            up_swap = partners(inputs, 0)
         up_swap.send()
-    if roomy:
-        down = weight_part(grads, 1, 0, jnp.float32)
+        if step == min(3, far):
+            up = weight_part(inputs, 0)
     down = down_swap.add_to(down)
-    up = up_swap.add_to(weight_part(inputs, 0, 0, jnp.float32))
-    gate_out = jnp.sum(jnp.where(names, home_gates.astype(jnp.float32)[:, :, None], 0.0), axis=0)
+    up = up_swap.add_to(up)
+    total = home.total(0, home.heads)
+    token_grads, gate_grads = total[:, : tokens.shape[1]], total[:, tokens.shape[1] :][:, :devices]
+    gate_out = jnp.sum(jnp.where(names, gate_grads.astype(jnp.float32).T[:, :, None], 0.0), axis=0)
     gate_out = gate_out.astype(jnp.bfloat16)
-    token_grads = home.total(0, home.heads)
     return token_grads, gate_out, up[None], down[None]
 
 

time: 191 us -> 175 us (0.916)
  starting transfers between devices: 48.8 us -> 43 us
  other arithmetic: 17.1 us -> 13.2 us
  local copies, waits for them, and re-layouts: 15.7 us -> 12.5 us
  waiting for transfers between devices: 54.3 us -> 52.3 us
    convert_element_type x7, other arithmetic: 7.27 us -> 2.78 us  [total(): return total.astype(jnp.bfloat16)]
    all_to_all x1 -> x0, starting transfers between devices: 3.67 us -> none  [on_device(): lax.all_to_all(gate_grads[numbered], 'expert', split_axis=0, concat_axis=...]
    ppermute x12 -> x11, waiting for transfers between devices: 9.85 us -> 6.74 us  [send(): falling = lax.ppermute(falling, 'expert', self.paths[1])]
    slice x3, local copies, waits for them, and re-layouts: 3.14 us -> 0.89 us  [the longest x1 0.85 us: on_device(): total[:, :tokens.shape[1]]]
    concatenate x0 -> x7, other arithmetic: none -> 2.09 us  [the longest x2 1.71 us: send(): jnp.concatenate(both, axis=1)]
    ppermute x12 -> x11, waiting for transfers between devices: 19.5 us -> 17.5 us  [send(): rising = lax.ppermute(rising, 'expert', self.paths[0])]
    ppermute x12 -> x11, starting transfers between devices: 12 us -> 10.5 us  [send(): falling = lax.ppermute(falling, 'expert', self.paths[1])]
    ppermute x12 -> x11, starting transfers between devices: 14 us -> 13.1 us  [send(): rising = lax.ppermute(rising, 'expert', self.paths[0])]
  transfers between devices with their start and end apart: 58 -> 54, of which waited for: 25 -> 28; matrix products, arithmetic and copies ran while one was open for 11% -> 8% of each run, Pallas kernels for 28% -> 30%
where the time goes in v3:
time: 175 us; the launch traced here: 174 us
  waiting for transfers between devices  52.3 us (30%)
  Pallas kernels  51.8 us (30%)
  starting transfers between devices  43 us (25%)
  other arithmetic  13.2 us (8%)
  local copies, waits for them, and re-layouts  12.5 us (7%)
    pallas_call x4, Pallas kernels, weight_grad(): pl.pallas_call(functools.partial(weight_kernel, len(wide), len(narrow), w...  27.2 us
    pallas_call x5, Pallas kernels, route_blocks(): pl.pallas_call(functools.partial(route_kernel, [len(block) for block in b...  24.5 us
    ppermute x11, waiting for transfers between devices, send(): rising = lax.ppermute(rising, 'expert', self.paths[0])  17.5 us
    ppermute x5, waiting for transfers between devices, send(): lax.ppermute(part, 'dp', [(i, (i + k) % self.shares) for i in range(self....  17.2 us
    ppermute x11, starting transfers between devices, send(): rising = lax.ppermute(rising, 'expert', self.paths[0])  13.1 us
    ppermute x11, starting transfers between devices, send(): falling = lax.ppermute(falling, 'expert', self.paths[1])  10.5 us
    unnamed x152, local copies, waits for them, and re-layouts  9.14 us
    ppermute x5, starting transfers between devices, send(): lax.ppermute(part, 'dp', [(i, (i + k) % self.shares) for i in range(self....  7.71 us
  transfers between devices with their start and end apart: 54, of which 28 were waited for; matrix products, arithmetic and copies ran while one was open for 8% of the time, Pallas kernels for 30%

profile of v3, /device:TPU:0, one launch (start us, length us, event | category | flops | bytes accessed | tf_op | source)
XLA Modules:
  0.0 174.3 jit_solution(4588300890532083301)
XLA Ops:
  0.6 3.1 %collective-permute-start = (bf16[128,2048]{1,0:T(8,128)(2,1)}, bf16[128,2048]{1,0:T(8,128)(2,1)S(1)}, u32[]{:S(2)}, u32[]{:S(2)}) collective-permute-start(bf16[128,2048]{1,0:T(8,128)(2,1)} %refs_0_.7), channel_id=1, source_target_pairs={{0,8},{2,10},{8,16},{10,18},{16,24},{18,26},{24,28},{26,30},{28,20... | collective-permute-start | bytes 1572872 | tf_op jit(solution)/shard_map/ppermute | solution.py:257
  5.7 6.5 %all-to-all-start = ((bf16[16,1,128]{2,1,0:T(2,128)(2,1)}), bf16[16,1,128]{2,1,0:T(2,128)(2,1)S(1)}, u32[]{:S(2)}, u32[]{:S(2)}) async-start(bf16[16,1,128]{2,1,0:T(2,128)(2,1)} %copy.19), calls=%async_computation | async-start | bytes 16384 | tf_op jit(solution)/shard_map/all_to_all | solution.py:377
  12.2 7.1 %all-to-all-done = bf16[16,1,128]{2,1,0:T(2,128)(2,1)S(1)} async-done(((bf16[16,1,128]{2,1,0:T(2,128)(2,1)}), bf16[16,1,128]{2,1,0:T(2,128)(2,1)S(1)}, u32[]{:S(2)}, u32[]{:S(2)}) %all-to-all-start) | async-done | bytes 4128 | tf_op jit(solution)/shard_map/all_to_all | solution.py:377
  22.9 2.1 %copy-done = bf16[1,2048,768]{2,1,0:T(8,128)(2,1)S(1)} copy-done((bf16[1,2048,768]{2,1,0:T(8,128)(2,1)S(1)}, bf16[1,2048,768]{2,1,0:T(8,128)(2,1)}, u32[]{:S(2)}) %copy-start) | copy-done | bytes 3145752
  29.1 3.7 %route.5 = (bf16[256,768]{1,0:T(8,128)(2,1)}, bf16[256,384]{1,0:T(8,128)(2,1)}, bf16[128,2176]{1,0:T(8,128)(2,1)}, bf16[128,2176]{1,0:T(8,128)(2,1)}) custom-call(s32[3]{0:T(128)S(1)} %pad_add_fusion.sources, bf16[128,2048]{1,0:T(8,128)(2,1)S(1)} %copy-done.6, bf16[128,2048]{1,0:T(8,128)(2,1)S(1)} %collective-permute-done.4.refs_1_, ...), custom_call_target="tpu_custom_call" | custom-call | flops 1207959552 | bytes 16777216 | tf_op jit(solution)/shard_map/route/pallas_call | solution.py:148
  35.7 5.8 %route.6 = (bf16[512,768]{1,0:T(8,128)(2,1)}, bf16[512,384]{1,0:T(8,128)(2,1)}, bf16[128,2176]{1,0:T(8,128)(2,1)}, bf16[128,2176]{1,0:T(8,128)(2,1)}, bf16[128,2...) custom-call(s32[5]{0:T(128)S(1)} %pad_add_fusion.1.sources, bf16[128,2048]{1,0:T(8,128)(2,1)S(1)} %collective-permute-done.refs_0_.refs_2_, ...), custom_call_target="tpu_custom_call" | custom-call | flops 2415919104 | bytes 16777216 | tf_op jit(solution)/shard_map/route/pallas_call | solution.py:148
  41.5 5.3 %collective-permute-done.5.refs_2_.refs_10_ = bf16[128,2048]{1,0:T(8,128)(2,1)S(1)} collective-permute-done((bf16[128,2048]{1,0:T(8,128)(2,1)S(1)}, bf16[128,2048]{1,0:T(8,128)(2,1)S(1)}, u32[]{:S(2)}, u32[]{:S(2)}) %collective-permute-start.5) | collective-permute-done | bytes 524320 | tf_op jit(solution)/shard_map/ppermute | solution.py:257
  49.9 3.7 %route.7 = (bf16[256,768]{1,0:T(8,128)(2,1)}, bf16[256,384]{1,0:T(8,128)(2,1)}, bf16[128,2176]{1,0:T(8,128)(2,1)}, bf16[128,2176]{1,0:T(8,128)(2,1)}) custom-call(s32[3]{0:T(128)S(1)} %pad_add_fusion.2.sources, bf16[128,2048]{1,0:T(8,128)(2,1)S(1)} %collective-permute-done.2.refs_0_.refs_6_, bf16[128,2048]{1,0:T(8,128)(2,1)S(1)} %collective-permute-done.11.refs_1_.refs_7_, ...), custom_call_target="tpu_custom_call" | custom-call | flops 1207959552 | bytes 16777216 | tf_op jit(solution)/shard_map/route/pallas_call | solution.py:148
  57.0 7.8 %route.8 = (bf16[768,768]{1,0:T(8,128)(2,1)}, bf16[768,384]{1,0:T(8,128)(2,1)}, bf16[128,2176]{1,0:T(8,128)(2,1)}, bf16[128,2176]{1,0:T(8,128)(2,1)}, bf16[128,2...) custom-call(s32[7]{0:T(128)S(1)} %pad_add_fusion.3.sources, ...), custom_call_target="tpu_custom_call" | custom-call | flops 3623878656 | bytes 16777216 | tf_op jit(solution)/shard_map/route/pallas_call | solution.py:148
  64.8 3.1 %collective-permute-done.12.refs_2_ = bf16[128,2048]{1,0:T(8,128)(2,1)S(1)} collective-permute-done((bf16[128,2048]{1,0:T(8,128)(2,1)S(1)}, bf16[128,2048]{1,0:T(8,128)(2,1)S(1)}, u32[]{:S(2)}, u32[]{:S(2)}) %collective-permute-start.12) | collective-permute-done | bytes 524320 | tf_op jit(solution)/shard_map/ppermute | solution.py:257
  73.0 3.7 %route.9 = (bf16[256,768]{1,0:T(8,128)(2,1)}, bf16[256,384]{1,0:T(8,128)(2,1)}, bf16[128,2176]{1,0:T(8,128)(2,1)}, bf16[128,2176]{1,0:T(8,128)(2,1)}) custom-call(s32[3]{0:T(128)S(1)} %pad_add_fusion.4.sources, bf16[64,2048]{1,0:T(8,128)(2,1)S(1)} %collective-permute-done.9.refs_0_.refs_14_, bf16[64,2048]{1,0:T(8,128)(2,1)S(1)} %collective-permute-done.10.refs_1_.refs_15_, ...), custom_call_target="tpu_custom_call" | custom-call | flops 1207959552 | bytes 16777216 | tf_op jit(solution)/shard_map/route/pallas_call | solution.py:148
  76.7 4.4 %collective-permute-done.17.refs_6_ = bf16[128,2048]{1,0:T(8,128)(2,1)S(1)} collective-permute-done((bf16[128,2048]{1,0:T(8,128)(2,1)S(1)}, bf16[128,2048]{1,0:T(8,128)(2,1)S(1)}, u32[]{:S(2)}, u32[]{:S(2)}) %collective-permute-start.17) | collective-permute-done | bytes 524320 | tf_op jit(solution)/shard_map/ppermute | solution.py:257
  84.3 4.9 %weight_grad.4 = (bf16[32,1024]{1,0:T(8,128)(2,1)}, bf16[352,1024]{1,0:T(8,128)(2,1)}) custom-call(s32[1]{0:T(128)} %bitcast.10.share, bf16[128,2048]{1,0:T(8,128)(2,1)} %refs_0_.7, bf16[128,2048]{1,0:T(8,128)(2,1)} %copy-done.7, bf16[128,2048]{1,0:T(8,128)(2,1)} %copy-done.10, bf16[128,2048]{1,0:T(8,128)(2,1)} %copy-done.12, bf16[128,2048]{1,0:T(8,128)(2,1)} %copy-done.11, ...), custom_call_target="tpu_custom_call" | custom-call | flops 1610612736 | bytes 23068672 | tf_op jit(solution)/shard_map/weight_grad/pallas_call | solution.py:217
  91.5 2.3 %collective-permute-done.33 = bf16[32,1024]{1,0:T(8,128)(2,1)S(1)} collective-permute-done((bf16[32,1024]{1,0:T(8,128)(2,1)}, bf16[32,1024]{1,0:T(8,128)(2,1)S(1)}, u32[]{:S(2)}, u32[]{:S(2)}) %collective-permute-start.33) | collective-permute-done | bytes 65568 | tf_op jit(solution)/shard_map/ppermute | solution.py:332
  102.2 5.0 %weight_grad.5 = f32[384,1024]{1,0:T(8,128)} custom-call(s32[1]{0:T(128)} %bitcast.11.share, bf16[128,2048]{1,0:T(8,128)(2,1)} %refs_0_.7, bf16[128,2048]{1,0:T(8,128)(2,1)} %copy-done.7, bf16[128,2048]{1,0:T(8,128)(2,1)} %copy-done.10, bf16[128,2048]{1,0:T(8,128)(2,1)} %copy-done.12, bf16[128,2048]{1,0:T(8,128)(2,1)} %copy-done.11, ...), custom_call_target="tpu_custom_call" | custom-call | flops 1610612736 | bytes 23068672 | tf_op jit(solution)/shard_map/weight_grad/pallas_call | solution.py:217
  107.7 5.6 %collective-permute-done.34 = bf16[352,1024]{1,0:T(8,128)(2,1)} collective-permute-done((bf16[352,1024]{1,0:T(8,128)(2,1)}, bf16[352,1024]{1,0:T(8,128)(2,1)}, u32[]{:S(2)}, u32[]{:S(2)}) %collective-permute-start.34) | collective-permute-done | bytes 720928 | tf_op jit(solution)/shard_map/ppermute | solution.py:332
  120.9 8.3 %weight_grad.6 = (bf16[384,768]{1,0:T(8,128)(2,1)}, bf16[384,768]{1,0:T(8,128)(2,1)}, bf16[256,768]{1,0:T(8,128)(2,1)}) custom-call(s32[1]{0:T(128)} %bitcast.10.share, bf16[128,2048]{1,0:T(8,128)(2,1)} %refs_0_.9, bf16[128,2048]{1,0:T(8,128)(2,1)} %collective-permute-done.37.refs_1_, bf16[128,2048]{1,0:T(8,128)(2,1)} %copy-done.34, ...), custom_call_target="tpu_custom_call" | custom-call | flops 3221225472 | bytes 29360128 | tf_op jit(solution)/shard_map/weight_grad/pallas_call | solution.py:217
  133.8 1.7 collective-permute-start.46
  135.9 9.1 %weight_grad.7 = f32[1024,768]{1,0:T(8,128)} custom-call(s32[1]{0:T(128)} %bitcast.11.share, bf16[128,2048]{1,0:T(8,128)(2,1)} %refs_0_.9, bf16[128,2048]{1,0:T(8,128)(2,1)} %collective-permute-done.37.refs_1_, bf16[128,2048]{1,0:T(8,128)(2,1)} %copy-done.34, bf16[128,2048]{1,0:T(8,128)(2,1)} %copy-done.41, bf16[128,2048]{1,0:T(8,128)(2,1)} %copy-done.36, ...), custom_call_target="tpu_custom_call" | custom-call | flops 3221225472 | bytes 29360128 | tf_op jit(solution)/shard_map/weight_grad/pallas_call | solution.py:217
  145.0 2.7 %collective-permute-done.46 = bf16[128,2176]{1,0:T(8,128)(2,1)S(1)} collective-permute-done((bf16[128,2176]{1,0:T(8,128)(2,1)S(1)}, bf16[128,2176]{1,0:T(8,128)(2,1)S(1)}, u32[]{:S(2)}, u32[]{:S(2)}) %collective-permute-start.46) | collective-permute-done | bytes 557088 | tf_op jit(solution)/shard_map/ppermute | solution.py:314
  153.2 2.5 %add_bitcast_fusion.1 = f32[1,384,1024]{2,1,0:T(8,128)} fusion(f32[384,1024]{1,0:T(8,128)S(1)} %copy-done.25, bf16[352,1024]{1,0:T(8,128)(2,1)} %collective-permute-done.34, bf16[32,1024]{1,0:T(8,128)(2,1)S(1)} %collective-permute-done.33), kind=kLoop, calls=%fused_computation.1 | loop fusion | flops 1966080 | bytes 3932160 | tf_op jit(solution)/shard_map/broadcast_in_dim | solution.py:483
  155.7 6.9 %collective-permute-done.51 = bf16[384,768]{1,0:T(8,128)(2,1)S(1)} collective-permute-done((bf16[384,768]{1,0:T(8,128)(2,1)S(1)}, bf16[384,768]{1,0:T(8,128)(2,1)S(1)}, u32[]{:S(2)}, u32[]{:S(2)}) %collective-permute-start.51) | collective-permute-done | bytes 589856 | tf_op jit(solution)/shard_map/ppermute | solution.py:332
  168.6 2.4 %collective-permute-done.52 = bf16[256,768]{1,0:T(8,128)(2,1)S(1)} collective-permute-done((bf16[256,768]{1,0:T(8,128)(2,1)}, bf16[256,768]{1,0:T(8,128)(2,1)S(1)}, u32[]{:S(2)}, u32[]{:S(2)}) %collective-permute-start.52) | collective-permute-done | bytes 393248 | tf_op jit(solution)/shard_map/ppermute | solution.py:332
  171.0 3.2 %add_bitcast_fusion = f32[1,1024,768]{2,1,0:T(8,128)} fusion(f32[1024,768]{1,0:T(8,128)S(1)} %copy-done.24, bf16[256,768]{1,0:T(8,128)(2,1)S(1)} %collective-permute-done.52, bf16[384,768]{1,0:T(8,128)(2,1)} %copy-done.48, bf16[384,768]{1,0:T(8,128)(2,1)} %copy-done.47), kind=kLoop, calls=%fused_computation | loop fusion | flops 5505024 | bytes 7864320 | tf_op jit(solution)/shard_map/broadcast_in_dim | solution.py:483
  (279 shorter events, 62.0 us)
Async XLA Ops:
  0.6 18.8 %collective-permute-start = (bf16[128,2048]{1,0:T(8,128)(2,1)}, bf16[128,2048]{1,0:T(8,128)(2,1)S(1)}, u32[]{:S(2)}, u32[]{:S(2)}) collective-permute-start(bf16[128,2048]{1,0:T(8,128)(2,1)} %refs_0_.7), channel_id=1, source_target_pairs={{0,8},{2,10},{8,16},{10,18},{16,24},{18,26},{24,28},{26,30},{28,20... | collective-permute-start | bytes 1572872 | tf_op jit(solution)/shard_map/ppermute | solution.py:257
  3.7 15.7 %collective-permute-start.1 = (bf16[128,2048]{1,0:T(8,128)(2,1)}, bf16[128,2048]{1,0:T(8,128)(2,1)S(1)}, u32[]{:S(2)}, u32[]{:S(2)}) collective-permute-start(bf16[128,2048]{1,0:T(8,128)(2,1)} %refs_0_.7), channel_id=1, source_target_pairs={{0,4},{2,6},{8,0},{10,2},{16,8},{18,10},{24,16},{26,18},{28,24},{3... | collective-permute-start | bytes 1572872 | tf_op jit(solution)/shard_map/ppermute | solution.py:258
  3.7 19.1 %collective-permute-start.4 = (bf16[128,2048]{1,0:T(8,128)(2,1)}, bf16[128,2048]{1,0:T(8,128)(2,1)S(1)}, u32[]{:S(2)}, u32[]{:S(2)}) collective-permute-start(bf16[128,2048]{1,0:T(8,128)(2,1)} %refs_0_.7), channel_id=1, source_target_pairs={{0,2},{2,0},{4,6},{6,4},{8,10},{10,8},{12,14},{14,12},{16,18},{18,... | collective-permute-start | bytes 1572872 | tf_op jit(solution)/shard_map/ppermute | solution.py:267
  5.7 13.6 %all-to-all-start = ((bf16[16,1,128]{2,1,0:T(2,128)(2,1)}), bf16[16,1,128]{2,1,0:T(2,128)(2,1)S(1)}, u32[]{:S(2)}, u32[]{:S(2)}) async-start(bf16[16,1,128]{2,1,0:T(2,128)(2,1)} %copy.19), calls=%async_computation | async-start | bytes 16384 | tf_op jit(solution)/shard_map/all_to_all | solution.py:377
  19.4 13.7 %collective-permute-start.2 = (bf16[128,2048]{1,0:T(8,128)(2,1)S(1)}, bf16[128,2048]{1,0:T(8,128)(2,1)S(1)}, u32[]{:S(2)}, u32[]{:S(2)}) collective-permute-start(bf16[128,2048]{1,0:T(8,128)(2,1)S(1)} %collective-permute-done.refs_0_.refs_2_), channel_id=1, source_target_pairs={{0,8},{2,10},{8,16},{10,18},{16,24},{18,26},{24,28},{26,30},{28,20... | collective-permute-start | bytes 1572872 | tf_op jit(solution)/shard_map/ppermute | solution.py:257
  20.1 13.4 %collective-permute-start.3 = (bf16[128,2048]{1,0:T(8,128)(2,1)S(1)}, bf16[128,2048]{1,0:T(8,128)(2,1)S(1)}, u32[]{:S(2)}, u32[]{:S(2)}) collective-permute-start(bf16[128,2048]{1,0:T(8,128)(2,1)S(1)} %collective-permute-done.1.refs_2_.refs_4_), channel_id=1, source_target_pairs={{0,4},{2,6},{8,0},{10,2},{16,8},{18,10},{24,16},{26,18},{28,24},{3... | collective-permute-start | bytes 1572872 | tf_op jit(solution)/shard_map/ppermute | solution.py:258
  22.3 13.4 %collective-permute-start.7 = (bf16[128,2048]{1,0:T(8,128)(2,1)S(1)}, bf16[128,2048]{1,0:T(8,128)(2,1)S(1)}, u32[]{:S(2)}, u32[]{:S(2)}) collective-permute-start(bf16[128,2048]{1,0:T(8,128)(2,1)S(1)} %collective-permute-done.refs_0_.refs_2_), channel_id=1, source_target_pairs={{0,2},{2,0},{4,6},{6,4},{8,10},{10,8},{12,14},{14,12},{16,18},{18,... | collective-permute-start | bytes 1572872 | tf_op jit(solution)/shard_map/ppermute | solution.py:267
  22.3 13.4 %collective-permute-start.8 = (bf16[128,2048]{1,0:T(8,128)(2,1)S(1)}, bf16[128,2048]{1,0:T(8,128)(2,1)S(1)}, u32[]{:S(2)}, u32[]{:S(2)}) collective-permute-start(bf16[128,2048]{1,0:T(8,128)(2,1)S(1)} %collective-permute-done.1.refs_2_.refs_4_), channel_id=1, source_target_pairs={{0,2},{2,0},{4,6},{6,4},{8,10},{10,8},{12,14},{14,12},{16,18},{18,... | collective-permute-start | bytes 1572872 | tf_op jit(solution)/shard_map/ppermute | solution.py:267
  33.5 13.3 %collective-permute-start.5 = (bf16[128,2048]{1,0:T(8,128)(2,1)S(1)}, bf16[128,2048]{1,0:T(8,128)(2,1)S(1)}, u32[]{:S(2)}, u32[]{:S(2)}) collective-permute-start(bf16[128,2048]{1,0:T(8,128)(2,1)S(1)} %collective-permute-done.2.refs_0_.refs_6_), channel_id=1, source_target_pairs={{0,8},{2,10},{8,16},{10,18},{16,24},{18,26},{24,28},{26,30},{28,20... | collective-permute-start | bytes 1572872 | tf_op jit(solution)/shard_map/ppermute | solution.py:257
  35.5 14.2 %collective-permute-start.11 = (bf16[128,2048]{1,0:T(8,128)(2,1)S(1)}, bf16[128,2048]{1,0:T(8,128)(2,1)S(1)}, u32[]{:S(2)}, u32[]{:S(2)}) collective-permute-start(bf16[128,2048]{1,0:T(8,128)(2,1)S(1)} %collective-permute-done.2.refs_0_.refs_6_), channel_id=1, source_target_pairs={{0,2},{2,0},{4,6},{6,4},{8,10},{10,8},{12,14},{14,12},{16,18},{18,... | collective-permute-start | bytes 1572872 | tf_op jit(solution)/shard_map/ppermute | solution.py:267
  54.8 13.2 %collective-permute-start.12 = (bf16[128,2048]{1,0:T(8,128)(2,1)S(1)}, bf16[128,2048]{1,0:T(8,128)(2,1)S(1)}, u32[]{:S(2)}, u32[]{:S(2)}) collective-permute-start(bf16[128,2048]{1,0:T(8,128)(2,1)S(1)} %copy-done.32), channel_id=1, source_target_pairs={{0,8},{2,10},{8,16},{10,18},{16,24},{18,26},{24,28},{26,30},{28,20... | collective-permute-start | bytes 1572872 | tf_op jit(solution)/shard_map/ppermute | solution.py:257
  71.5 17.8 %collective-permute-start.23 = (bf16[128,2176]{1,0:T(8,128)(2,1)}, bf16[128,2176]{1,0:T(8,128)(2,1)}, u32[]{:S(2)}, u32[]{:S(2)}) collective-permute-start(bf16[128,2176]{1,0:T(8,128)(2,1)} %get-tuple-element.109), channel_id=1, source_target_pairs={{0,2},{2,0},{4,6},{6,4},{8,10},{10,8},{12,14},{14,12},{16,18},{18,... | collective-permute-start | bytes 1671176 | tf_op jit(solution)/shard_map/ppermute | solution.py:369
  72.4 18.4 %collective-permute-start.24 = (bf16[128,2176]{1,0:T(8,128)(2,1)}, bf16[128,2176]{1,0:T(8,128)(2,1)S(1)}, u32[]{:S(2)}, u32[]{:S(2)}) collective-permute-start(bf16[128,2176]{1,0:T(8,128)(2,1)} %get-tuple-element.111), channel_id=1, source_target_pairs={{0,2},{2,0},{4,6},{6,4},{8,10},{10,8},{12,14},{14,12},{16,18},{18,... | collective-permute-start | bytes 1671176 | tf_op jit(solution)/shard_map/ppermute | solution.py:369
  72.8 18.1 %collective-permute-start.25 = (bf16[128,2176]{1,0:T(8,128)(2,1)}, bf16[128,2176]{1,0:T(8,128)(2,1)S(1)}, u32[]{:S(2)}, u32[]{:S(2)}) collective-permute-start(bf16[128,2176]{1,0:T(8,128)(2,1)} %get-tuple-element.113), channel_id=1, source_target_pairs={{0,2},{2,0},{4,6},{6,4},{8,10},{10,8},{12,14},{14,12},{16,18},{18,... | collective-permute-start | bytes 1671176 | tf_op jit(solution)/shard_map/ppermute | solution.py:369
  94.5 18.8 %collective-permute-start.34 = (bf16[352,1024]{1,0:T(8,128)(2,1)}, bf16[352,1024]{1,0:T(8,128)(2,1)}, u32[]{:S(2)}, u32[]{:S(2)}) collective-permute-start(bf16[352,1024]{1,0:T(8,128)(2,1)} %get-tuple-element.140), channel_id=1, source_target_pairs={{0,1},{1,0},{2,3},{3,2},{4,5},{5,4},{6,7},{7,6},{8,9},{9,8},{10,11... | collective-permute-start | bytes 2162696 | tf_op jit(solution)/shard_map/ppermute | solution.py:332
  99.2 14.5 %collective-permute-start.31 = (bf16[64,4224]{1,0:T(8,128)(2,1)}, bf16[64,4224]{1,0:T(8,128)(2,1)S(1)}, u32[]{:S(2)}, u32[]{:S(2)}) collective-permute-start(bf16[64,4224]{1,0:T(8,128)(2,1)} %pad_maximum_fusion), channel_id=1, source_target_pairs={{0,8},{2,10},{8,16},{10,18},{16,24},{18,26},{24,28},{26,30},{28,20... | collective-permute-start | bytes 1622024 | tf_op jit(solution)/shard_map/ppermute | solution.py:257
  100.8 14.2 %collective-permute-start.32 = (bf16[64,4224]{1,0:T(8,128)(2,1)}, bf16[64,4224]{1,0:T(8,128)(2,1)S(1)}, u32[]{:S(2)}, u32[]{:S(2)}) collective-permute-start(bf16[64,4224]{1,0:T(8,128)(2,1)} %pad_maximum_fusion.1), channel_id=1, source_target_pairs={{0,4},{2,6},{8,0},{10,2},{16,8},{18,10},{24,16},{26,18},{28,24},{3... | collective-permute-start | bytes 1622024 | tf_op jit(solution)/shard_map/ppermute | solution.py:258
  102.1 13.2 %collective-permute-start.37 = (bf16[128,2048]{1,0:T(8,128)(2,1)S(1)}, bf16[128,2048]{1,0:T(8,128)(2,1)}, u32[]{:S(2)}, u32[]{:S(2)}) collective-permute-start(bf16[128,2048]{1,0:T(8,128)(2,1)S(1)} %copy-done.33), channel_id=1, source_target_pairs={{0,2},{2,0},{4,6},{6,4},{8,10},{10,8},{12,14},{14,12},{16,18},{18,... | collective-permute-start | bytes 1572872 | tf_op jit(solution)/shard_map/ppermute | solution.py:267
  116.9 15.0 %collective-permute-start.35 = (bf16[128,2176]{1,0:T(8,128)(2,1)S(1)}, bf16[128,2176]{1,0:T(8,128)(2,1)S(1)}, u32[]{:S(2)}, u32[]{:S(2)}) collective-permute-start(bf16[128,2176]{1,0:T(8,128)(2,1)S(1)} %add_convert_fusion.6), channel_id=1, source_target_pairs={{0,8},{2,10},{8,16},{10,18},{16,24},{18,26},{24,28},{26,30},{28,20... | collective-permute-start | bytes 1671176 | tf_op jit(solution)/shard_map/ppermute | solution.py:314
  117.7 14.7 %collective-permute-start.36 = (bf16[128,2176]{1,0:T(8,128)(2,1)S(1)}, bf16[128,2176]{1,0:T(8,128)(2,1)S(1)}, u32[]{:S(2)}, u32[]{:S(2)}) collective-permute-start(bf16[128,2176]{1,0:T(8,128)(2,1)S(1)} %add_convert_fusion.5), channel_id=1, source_target_pairs={{0,4},{2,6},{8,0},{10,2},{16,8},{18,10},{24,16},{26,18},{28,24},{3... | collective-permute-start | bytes 1671176 | tf_op jit(solution)/shard_map/ppermute | solution.py:315
  129.1 20.0 %collective-permute-start.48 = (bf16[384,768]{1,0:T(8,128)(2,1)}, bf16[384,768]{1,0:T(8,128)(2,1)S(1)}, u32[]{:S(2)}, u32[]{:S(2)}) collective-permute-start(bf16[384,768]{1,0:T(8,128)(2,1)} %get-tuple-element.147), channel_id=1, source_target_pairs={{0,1},{1,0},{2,3},{3,2},{4,5},{5,4},{6,7},{7,6},{8,9},{9,8},{10,11... | collective-permute-start | bytes 1769480 | tf_op jit(solution)/shard_map/ppermute | solution.py:332
  133.8 13.9 %collective-permute-start.46 = (bf16[128,2176]{1,0:T(8,128)(2,1)S(1)}, bf16[128,2176]{1,0:T(8,128)(2,1)S(1)}, u32[]{:S(2)}, u32[]{:S(2)}) collective-permute-start(bf16[128,2176]{1,0:T(8,128)(2,1)S(1)} %add_convert_fusion.4), channel_id=1, source_target_pairs={{0,8},{2,10},{8,16},{10,18},{16,24},{18,26},{24,28},{26,30},{28,20... | collective-permute-start | bytes 1671176 | tf_op jit(solution)/shard_map/ppermute | solution.py:314
  135.6 13.6 %collective-permute-start.47 = (bf16[128,2176]{1,0:T(8,128)(2,1)S(1)}, bf16[128,2176]{1,0:T(8,128)(2,1)S(1)}, u32[]{:S(2)}, u32[]{:S(2)}) collective-permute-start(bf16[128,2176]{1,0:T(8,128)(2,1)S(1)} %add_convert_fusion.3), channel_id=1, source_target_pairs={{0,4},{2,6},{8,0},{10,2},{16,8},{18,10},{24,16},{26,18},{28,24},{3... | collective-permute-start | bytes 1671176 | tf_op jit(solution)/shard_map/ppermute | solution.py:315
  149.2 13.4 %collective-permute-start.51 = (bf16[384,768]{1,0:T(8,128)(2,1)S(1)}, bf16[384,768]{1,0:T(8,128)(2,1)S(1)}, u32[]{:S(2)}, u32[]{:S(2)}) collective-permute-start(bf16[384,768]{1,0:T(8,128)(2,1)S(1)} %copy-done.70), channel_id=1, source_target_pairs={{0,1},{1,0},{2,3},{3,2},{4,5},{5,4},{6,7},{7,6},{8,9},{9,8},{10,11... | collective-permute-start | bytes 1769480 | tf_op jit(solution)/shard_map/ppermute | solution.py:332
  (106 other events, 818.0 us)

commit v4 on v3

--- a/solution.py
+++ b/solution.py
@@ -160,10 +160,10 @@
     )(sources, *pieces, saved, gates, down_weight, gate_up_weight)
 
 
-def thirds(part):
-    units = part // 128
-    sizes = [128 * (units // 3 + (i < units % 3)) for i in range(3)]
-    return [size for size in sizes if size]
+def cut_rows(part):
+    quarter = max(128, part // 512 * 128)
+    sizes = [part - 2 * quarter, quarter, quarter]
+    return [size for size in sizes if size > 0]
 
 
 def first_rows(part):
@@ -196,6 +196,10 @@
             total[...] = product if at == 0 else total[...] + product
             continue
         start = 0
+        if len(outs) == 1:
+            product = dot(first[at:end], second[at:end], 0, 0)
+            outs[0][...] = (product if at == 0 else total[...] + product).astype(outs[0].dtype)
+            break
         for out in outs:
             rows = slice(start, start + out.shape[0])
             product = dot(first[at:end, rows], second[at:end], 0, 0)
@@ -217,13 +221,15 @@
     return pl.pallas_call(
         functools.partial(weight_kernel, len(wide), len(narrow), wide_first),
         in_specs=[pl.BlockSpec(memory_space=pltpu.SMEM)] + in_hbm(len(wide) + len(narrow)),
-        out_specs=in_hbm(len(sizes)),
-        out_shape=[pltpu.HBM((size, shape[1]), dtype) for size in sizes],
+        out_specs=in_hbm(len(sizes)) if cuts else in_vmem(1),
+        out_shape=[pltpu.HBM((size, shape[1]), dtype) for size in sizes]
+        if cuts
+        else [jax.ShapeDtypeStruct(shape, dtype)],
         scratch_shapes=[
             pltpu.VMEM((depth, part), wide[0].dtype),
             pltpu.VMEM((depth, thin), narrow[0].dtype),
             pltpu.VMEM(shape, jnp.float32),
-            pltpu.VMEM(shape, dtype),
+            pltpu.VMEM(shape if cuts else (8, 128), dtype),
             pltpu.SemaphoreType.DMA((len(wide) + len(narrow) + len(sizes),)),
         ],
         compiler_params=pltpu.CompilerParams(vmem_limit_bytes=2 * VMEM),
@@ -232,6 +238,37 @@
         ),
         name="weight_grad",
     )(share, *wide, *narrow)
+
+
+def add_kernel(at, total_ref, *refs):
+    parts, (out_ref, held, sems) = refs[:-3], refs[-3:]
+    rows = pl.ds(at, held.shape[0])
+    read = pltpu.make_async_copy(total_ref.at[rows], held, sems.at[0])
+    read.start()
+    read.wait()
+    for part in parts:
+        held[...] += part[...].astype(jnp.float32)
+    write = pltpu.make_async_copy(held, out_ref.at[rows], sems.at[1])
+    write.start()
+    write.wait()
+
+
+def add_rows(total, parts, at):
+    size = parts[0].shape[0]
+    return pl.pallas_call(
+        functools.partial(add_kernel, at),
+        in_specs=in_hbm(1) + in_vmem(len(parts)),
+        out_specs=pl.BlockSpec(memory_space=pltpu.HBM),
+        out_shape=pltpu.HBM(total.shape, total.dtype),
+        input_output_aliases={0: 0},
+        scratch_shapes=[
+            pltpu.VMEM((size, total.shape[1]), total.dtype),
+            pltpu.SemaphoreType.DMA((2,)),
+        ],
+        compiler_params=pltpu.CompilerParams(vmem_limit_bytes=VMEM),
+        cost_estimate=pl.CostEstimate(flops=size * total.shape[1], bytes_accessed=8 * size * total.shape[1], transcendentals=0),
+        name="add_rows",
+    )(total, *parts)
 
 
 class Ring:
@@ -337,9 +374,10 @@
     def add_to(self, total):
         while len(self.come) < len(self.parts):
             self.send()
-        for k in range(self.shares - 1):
-            arrived = jnp.concatenate([parts[k] for parts in self.come], axis=0)
-            total = total + arrived.astype(jnp.float32)
+        at = 0
+        for parts in self.come:
+            total = add_rows(total, parts, at)
+            at += parts[0].shape[0]
         return total
 
 
@@ -388,7 +426,7 @@
             shares,
             kind == 0,
             jnp.float32 if own else jnp.bfloat16,
-            None if own else (thirds if kind == 0 else first_rows),
+            None if own else (cut_rows if kind == 0 else first_rows),
         )
         return parts[0] if own else parts
 
@@ -462,11 +500,13 @@
     up_swap = None
     for step in range(2, far + 1):
         if step == 2:
-            by(home, inputs.heads, down_swap.come, down)
+            by(home, inputs.heads, down_swap.come)
+            home.heads, down = fence(home.heads, down)
         elif step == 3:
             by(home, up_swap.parts)
         elif step == 4:
-            by(home, up_swap.come[:1], up)
+            by(home, up_swap.come[:1])
+            home.heads, up = fence(home.heads, up)
         home.send()
         if step == 2:
             down_swap.send()

time: 175 us -> 174 us (level)
  Pallas kernels: 51.8 us -> 63 us
  waiting for transfers between devices: 52.3 us -> 45.9 us
  other arithmetic: 13.2 us -> 8.02 us
    pallas_call x0 -> x5, Pallas kernels: none -> 11.2 us  [add_rows(): pl.pallas_call(functools.partial(add_kernel, at), in_specs=in_hbm(1) + in...]
    ppermute x5, waiting for transfers between devices: 17.2 us -> 10.4 us  [send(): lax.ppermute(part, 'dp', [(i, (i + k) % self.shares) for i in range(self....]
    broadcast_in_dim x2 -> x0, other arithmetic: 5.7 us -> none  [on_device(): return (token_grads, gate_out, up[None], down[None])]
    unnamed x152 -> x136, local copies, waits for them, and re-layouts: 9.14 us -> 9.18 us
  transfers between devices with their start and end apart: 54 -> 54, of which waited for: 28 -> 26; matrix products, arithmetic and copies ran while one was open for 8% -> 5% of each run, Pallas kernels for 30% -> 35%
where the time goes in v4:
time: 174 us; the launch traced here: 173 us
  Pallas kernels  63 us (36%)
  waiting for transfers between devices  45.9 us (26%)
  starting transfers between devices  42.8 us (25%)
  local copies, waits for them, and re-layouts  11.7 us (7%)
  other arithmetic  8.02 us (5%)
    pallas_call x4, Pallas kernels, weight_grad(): pl.pallas_call(functools.partial(weight_kernel, len(wide), len(narrow), w...  27.3 us
    pallas_call x5, Pallas kernels, route_blocks(): pl.pallas_call(functools.partial(route_kernel, [len(block) for block in b...  24.5 us
    ppermute x11, waiting for transfers between devices, send(): rising = lax.ppermute(rising, 'expert', self.paths[0])  17.7 us
    ppermute x11, starting transfers between devices, send(): rising = lax.ppermute(rising, 'expert', self.paths[0])  12.6 us
    pallas_call x5, Pallas kernels, add_rows(): pl.pallas_call(functools.partial(add_kernel, at), in_specs=in_hbm(1) + in...  11.2 us
    ppermute x11, starting transfers between devices, send(): falling = lax.ppermute(falling, 'expert', self.paths[1])  11 us
    ppermute x5, waiting for transfers between devices, send(): lax.ppermute(part, 'dp', [(i, (i + k) % self.shares) for i in range(self....  10.4 us
    unnamed x136, local copies, waits for them, and re-layouts  9.18 us
  transfers between devices with their start and end apart: 54, of which 26 were waited for; matrix products, arithmetic and copies ran while one was open for 5% of the time, Pallas kernels for 35%

profile of v4, /device:TPU:0, one launch (start us, length us, event | category | flops | bytes accessed | tf_op | source)
XLA Modules:
  0.0 173.0 jit_solution(8557202949633481905)
XLA Ops:
  0.6 3.1 %collective-permute-start = (bf16[128,2048]{1,0:T(8,128)(2,1)}, bf16[128,2048]{1,0:T(8,128)(2,1)S(1)}, u32[]{:S(2)}, u32[]{:S(2)}) collective-permute-start(bf16[128,2048]{1,0:T(8,128)(2,1)} %refs_0_.7), channel_id=1, source_target_pairs={{0,8},{2,10},{8,16},{10,18},{16,24},{18,26},{24,28},{26,30},{28,20... | collective-permute-start | bytes 1572872 | tf_op jit(solution)/shard_map/ppermute | solution.py:294
  5.7 6.5 %all-to-all-start = ((bf16[16,1,128]{2,1,0:T(2,128)(2,1)}), bf16[16,1,128]{2,1,0:T(2,128)(2,1)S(1)}, u32[]{:S(2)}, u32[]{:S(2)}) async-start(bf16[16,1,128]{2,1,0:T(2,128)(2,1)} %copy.24), calls=%async_computation | async-start | bytes 16384 | tf_op jit(solution)/shard_map/all_to_all | solution.py:415
  12.2 7.1 %all-to-all-done = bf16[16,1,128]{2,1,0:T(2,128)(2,1)S(1)} async-done(((bf16[16,1,128]{2,1,0:T(2,128)(2,1)}), bf16[16,1,128]{2,1,0:T(2,128)(2,1)S(1)}, u32[]{:S(2)}, u32[]{:S(2)}) %all-to-all-start) | async-done | bytes 4128 | tf_op jit(solution)/shard_map/all_to_all | solution.py:415
  22.9 2.1 %copy-done = bf16[1,2048,768]{2,1,0:T(8,128)(2,1)S(1)} copy-done((bf16[1,2048,768]{2,1,0:T(8,128)(2,1)S(1)}, bf16[1,2048,768]{2,1,0:T(8,128)(2,1)}, u32[]{:S(2)}) %copy-start) | copy-done | bytes 3145752
  29.1 3.7 %route.5 = (bf16[256,768]{1,0:T(8,128)(2,1)}, bf16[256,384]{1,0:T(8,128)(2,1)}, bf16[128,2176]{1,0:T(8,128)(2,1)}, bf16[128,2176]{1,0:T(8,128)(2,1)}) custom-call(s32[3]{0:T(128)S(1)} %pad_add_fusion.sources, bf16[128,2048]{1,0:T(8,128)(2,1)S(1)} %copy-done.6, bf16[128,2048]{1,0:T(8,128)(2,1)S(1)} %collective-permute-done.4.refs_1_, ...), custom_call_target="tpu_custom_call" | custom-call | flops 1207959552 | bytes 16777216 | tf_op jit(solution)/shard_map/route/pallas_call | solution.py:148
  35.7 5.8 %route.6 = (bf16[512,768]{1,0:T(8,128)(2,1)}, bf16[512,384]{1,0:T(8,128)(2,1)}, bf16[128,2176]{1,0:T(8,128)(2,1)}, bf16[128,2176]{1,0:T(8,128)(2,1)}, bf16[128,2...) custom-call(s32[5]{0:T(128)S(1)} %pad_add_fusion.1.sources, bf16[128,2048]{1,0:T(8,128)(2,1)S(1)} %collective-permute-done.refs_0_.refs_2_, ...), custom_call_target="tpu_custom_call" | custom-call | flops 2415919104 | bytes 16777216 | tf_op jit(solution)/shard_map/route/pallas_call | solution.py:148
  41.5 5.3 %collective-permute-done.5.refs_2_.refs_10_ = bf16[128,2048]{1,0:T(8,128)(2,1)S(1)} collective-permute-done((bf16[128,2048]{1,0:T(8,128)(2,1)S(1)}, bf16[128,2048]{1,0:T(8,128)(2,1)S(1)}, u32[]{:S(2)}, u32[]{:S(2)}) %collective-permute-start.5) | collective-permute-done | bytes 524320 | tf_op jit(solution)/shard_map/ppermute | solution.py:294
  49.9 3.7 %route.7 = (bf16[256,768]{1,0:T(8,128)(2,1)}, bf16[256,384]{1,0:T(8,128)(2,1)}, bf16[128,2176]{1,0:T(8,128)(2,1)}, bf16[128,2176]{1,0:T(8,128)(2,1)}) custom-call(s32[3]{0:T(128)S(1)} %pad_add_fusion.2.sources, bf16[128,2048]{1,0:T(8,128)(2,1)S(1)} %collective-permute-done.2.refs_0_.refs_6_, bf16[128,2048]{1,0:T(8,128)(2,1)S(1)} %collective-permute-done.11.refs_1_.refs_7_, ...), custom_call_target="tpu_custom_call" | custom-call | flops 1207959552 | bytes 16777216 | tf_op jit(solution)/shard_map/route/pallas_call | solution.py:148
  57.0 7.8 %route.8 = (bf16[768,768]{1,0:T(8,128)(2,1)}, bf16[768,384]{1,0:T(8,128)(2,1)}, bf16[128,2176]{1,0:T(8,128)(2,1)}, bf16[128,2176]{1,0:T(8,128)(2,1)}, bf16[128,2...) custom-call(s32[7]{0:T(128)S(1)} %pad_add_fusion.3.sources, ...), custom_call_target="tpu_custom_call" | custom-call | flops 3623878656 | bytes 16777216 | tf_op jit(solution)/shard_map/route/pallas_call | solution.py:148
  64.8 3.1 %collective-permute-done.12.refs_2_ = bf16[128,2048]{1,0:T(8,128)(2,1)S(1)} collective-permute-done((bf16[128,2048]{1,0:T(8,128)(2,1)S(1)}, bf16[128,2048]{1,0:T(8,128)(2,1)S(1)}, u32[]{:S(2)}, u32[]{:S(2)}) %collective-permute-start.12) | collective-permute-done | bytes 524320 | tf_op jit(solution)/shard_map/ppermute | solution.py:294
  73.0 3.7 %route.9 = (bf16[256,768]{1,0:T(8,128)(2,1)}, bf16[256,384]{1,0:T(8,128)(2,1)}, bf16[128,2176]{1,0:T(8,128)(2,1)}, bf16[128,2176]{1,0:T(8,128)(2,1)}) custom-call(s32[3]{0:T(128)S(1)} %pad_add_fusion.4.sources, bf16[64,2048]{1,0:T(8,128)(2,1)S(1)} %collective-permute-done.9.refs_0_.refs_14_, bf16[64,2048]{1,0:T(8,128)(2,1)S(1)} %collective-permute-done.10.refs_1_.refs_15_, ...), custom_call_target="tpu_custom_call" | custom-call | flops 1207959552 | bytes 16777216 | tf_op jit(solution)/shard_map/route/pallas_call | solution.py:148
  76.7 4.4 %collective-permute-done.17.refs_6_ = bf16[128,2048]{1,0:T(8,128)(2,1)S(1)} collective-permute-done((bf16[128,2048]{1,0:T(8,128)(2,1)S(1)}, bf16[128,2048]{1,0:T(8,128)(2,1)S(1)}, u32[]{:S(2)}, u32[]{:S(2)}) %collective-permute-start.17) | collective-permute-done | bytes 524320 | tf_op jit(solution)/shard_map/ppermute | solution.py:294
  84.4 4.9 %weight_grad.4 = (bf16[32,1024]{1,0:T(8,128)(2,1)}, bf16[352,1024]{1,0:T(8,128)(2,1)}) custom-call(s32[1]{0:T(128)} %bitcast.10.share, bf16[128,2048]{1,0:T(8,128)(2,1)} %refs_0_.7, bf16[128,2048]{1,0:T(8,128)(2,1)} %copy-done.7, bf16[128,2048]{1,0:T(8,128)(2,1)} %copy-done.10, bf16[128,2048]{1,0:T(8,128)(2,1)} %copy-done.12, bf16[128,2048]{1,0:T(8,128)(2,1)} %copy-done.11, ...), custom_call_target="tpu_custom_call" | custom-call | flops 1610612736 | bytes 23068672 | tf_op jit(solution)/shard_map/weight_grad/pallas_call | solution.py:221
  91.4 2.5 %collective-permute-done.33.refs_0_ = bf16[32,1024]{1,0:T(8,128)(2,1)S(1)} collective-permute-done((bf16[32,1024]{1,0:T(8,128)(2,1)}, bf16[32,1024]{1,0:T(8,128)(2,1)S(1)}, u32[]{:S(2)}, u32[]{:S(2)}) %collective-permute-start.33) | collective-permute-done | bytes 65568 | tf_op jit(solution)/shard_map/ppermute | solution.py:369
  102.2 5.0 %weight_grad.5.total_ref = f32[384,1024]{1,0:T(8,128)} custom-call(s32[1]{0:T(128)} %bitcast.11.share, bf16[128,2048]{1,0:T(8,128)(2,1)} %refs_0_.7, bf16[128,2048]{1,0:T(8,128)(2,1)} %copy-done.7, bf16[128,2048]{1,0:T(8,128)(2,1)} %copy-done.10, bf16[128,2048]{1,0:T(8,128)(2,1)} %copy-done.12, bf16[128,2048]{1,0:T(8,128)(2,1)} %copy-done.11, ...), custom_call_target="tpu_custom_call" | custom-call | flops 1610612736 | bytes 23068672 | tf_op jit(solution)/shard_map/weight_grad/pallas_call | solution.py:221
  107.8 5.5 %collective-permute-done.34.refs_0_ = bf16[352,1024]{1,0:T(8,128)(2,1)S(1)} collective-permute-done((bf16[352,1024]{1,0:T(8,128)(2,1)}, bf16[352,1024]{1,0:T(8,128)(2,1)S(1)}, u32[]{:S(2)}, u32[]{:S(2)}) %collective-permute-start.34) | collective-permute-done | bytes 720928 | tf_op jit(solution)/shard_map/ppermute | solution.py:369
  121.0 8.2 %weight_grad.6 = (bf16[512,768]{1,0:T(8,128)(2,1)}, bf16[256,768]{1,0:T(8,128)(2,1)}, bf16[256,768]{1,0:T(8,128)(2,1)}) custom-call(s32[1]{0:T(128)} %bitcast.10.share, bf16[128,2048]{1,0:T(8,128)(2,1)} %refs_0_.9, bf16[128,2048]{1,0:T(8,128)(2,1)} %collective-permute-done.37.refs_1_, bf16[128,2048]{1,0:T(8,128)(2,1)} %copy-done.32, ...), custom_call_target="tpu_custom_call" | custom-call | flops 3221225472 | bytes 29360128 | tf_op jit(solution)/shard_map/weight_grad/pallas_call | solution.py:221
  134.0 1.8 %collective-permute-start.46 = (bf16[128,2176]{1,0:T(8,128)(2,1)S(1)}, bf16[128,2176]{1,0:T(8,128)(2,1)S(1)}, u32[]{:S(2)}, u32[]{:S(2)}) collective-permute-start(bf16[128,2176]{1,0:T(8,128)(2,1)S(1)} %add_convert_fusion.4), channel_id=1, source_target_pairs={{0,8},{2,10},{8,16},{10,18},{16,24},{18,26},{24,28},{26,30},{28,20... | collective-permute-start | bytes 1671176 | tf_op jit(solution)/shard_map/ppermute | solution.py:351
  136.1 9.1 %weight_grad.7.total_ref = f32[1024,768]{1,0:T(8,128)} custom-call(s32[1]{0:T(128)} %bitcast.11.share, bf16[128,2048]{1,0:T(8,128)(2,1)} %refs_0_.9, bf16[128,2048]{1,0:T(8,128)(2,1)} %collective-permute-done.37.refs_1_, bf16[128,2048]{1,0:T(8,128)(2,1)} %copy-done.32, bf16[128,2048]{1,0:T(8,128)(2,1)} %copy-done.38, bf16[128,2048]{1,0:T(8,128)(2,1)} %copy-done.34, ...), custom_call_target="tpu_custom_call" | custom-call | flops 3221225472 | bytes 29360128 | tf_op jit(solution)/shard_map/weight_grad/pallas_call | solution.py:221
  145.3 2.7 %collective-permute-done.46 = bf16[128,2176]{1,0:T(8,128)(2,1)S(1)} collective-permute-done((bf16[128,2176]{1,0:T(8,128)(2,1)S(1)}, bf16[128,2176]{1,0:T(8,128)(2,1)S(1)}, u32[]{:S(2)}, u32[]{:S(2)}) %collective-permute-start.46) | collective-permute-done | bytes 557088 | tf_op jit(solution)/shard_map/ppermute | solution.py:351
  156.2 2.6 %add_rows.9 = f32[384,1024]{1,0:T(8,128)} custom-call(f32[384,1024]{1,0:T(8,128)} %add_rows.8.total_ref, bf16[352,1024]{1,0:T(8,128)(2,1)S(1)} %collective-permute-done.34.refs_0_), custom_call_target="tpu_custom_call", output_to_operand_aliasing={{}: (0, {})} | custom-call | flops 360448 | bytes 2883584 | tf_op jit(solution)/shard_map/add_rows/pallas_call | solution.py:258
  158.9 2.8 %add_rows.5.total_ref = f32[1024,768]{1,0:T(8,128)} custom-call(f32[1024,768]{1,0:T(8,128)} %weight_grad.7.total_ref, bf16[512,768]{1,0:T(8,128)(2,1)S(1)} %collective-permute-done.48.refs_0_), custom_call_target="tpu_custom_call", output_to_operand_aliasing={{}: (0, {})} | custom-call | flops 393216 | bytes 3145728 | tf_op jit(solution)/shard_map/add_rows/pallas_call | solution.py:258
  163.9 2.1 %add_rows.6.total_ref = f32[1024,768]{1,0:T(8,128)} custom-call(f32[1024,768]{1,0:T(8,128)} %add_rows.5.total_ref, bf16[256,768]{1,0:T(8,128)(2,1)S(1)} %collective-permute-done.51.refs_0_), custom_call_target="tpu_custom_call", output_to_operand_aliasing={{}: (0, {})} | custom-call | flops 196608 | bytes 1572864 | tf_op jit(solution)/shard_map/add_rows/pallas_call | solution.py:258
  170.7 2.1 %add_rows.7 = f32[1024,768]{1,0:T(8,128)} custom-call(f32[1024,768]{1,0:T(8,128)} %add_rows.6.total_ref, bf16[256,768]{1,0:T(8,128)(2,1)S(1)} %collective-permute-done.52.refs_0_), custom_call_target="tpu_custom_call", output_to_operand_aliasing={{}: (0, {})} | custom-call | flops 196608 | bytes 1572864 | tf_op jit(solution)/shard_map/add_rows/pallas_call | solution.py:258
  (266 shorter events, 65.9 us)
Async XLA Ops:
  0.6 18.8 %collective-permute-start = (bf16[128,2048]{1,0:T(8,128)(2,1)}, bf16[128,2048]{1,0:T(8,128)(2,1)S(1)}, u32[]{:S(2)}, u32[]{:S(2)}) collective-permute-start(bf16[128,2048]{1,0:T(8,128)(2,1)} %refs_0_.7), channel_id=1, source_target_pairs={{0,8},{2,10},{8,16},{10,18},{16,24},{18,26},{24,28},{26,30},{28,20... | collective-permute-start | bytes 1572872 | tf_op jit(solution)/shard_map/ppermute | solution.py:294
  3.7 15.7 %collective-permute-start.1 = (bf16[128,2048]{1,0:T(8,128)(2,1)}, bf16[128,2048]{1,0:T(8,128)(2,1)S(1)}, u32[]{:S(2)}, u32[]{:S(2)}) collective-permute-start(bf16[128,2048]{1,0:T(8,128)(2,1)} %refs_0_.7), channel_id=1, source_target_pairs={{0,4},{2,6},{8,0},{10,2},{16,8},{18,10},{24,16},{26,18},{28,24},{3... | collective-permute-start | bytes 1572872 | tf_op jit(solution)/shard_map/ppermute | solution.py:295
  3.7 19.1 %collective-permute-start.4 = (bf16[128,2048]{1,0:T(8,128)(2,1)}, bf16[128,2048]{1,0:T(8,128)(2,1)S(1)}, u32[]{:S(2)}, u32[]{:S(2)}) collective-permute-start(bf16[128,2048]{1,0:T(8,128)(2,1)} %refs_0_.7), channel_id=1, source_target_pairs={{0,2},{2,0},{4,6},{6,4},{8,10},{10,8},{12,14},{14,12},{16,18},{18,... | collective-permute-start | bytes 1572872 | tf_op jit(solution)/shard_map/ppermute | solution.py:304
  5.7 13.6 %all-to-all-start = ((bf16[16,1,128]{2,1,0:T(2,128)(2,1)}), bf16[16,1,128]{2,1,0:T(2,128)(2,1)S(1)}, u32[]{:S(2)}, u32[]{:S(2)}) async-start(bf16[16,1,128]{2,1,0:T(2,128)(2,1)} %copy.24), calls=%async_computation | async-start | bytes 16384 | tf_op jit(solution)/shard_map/all_to_all | solution.py:415
  19.4 13.7 %collective-permute-start.2 = (bf16[128,2048]{1,0:T(8,128)(2,1)S(1)}, bf16[128,2048]{1,0:T(8,128)(2,1)S(1)}, u32[]{:S(2)}, u32[]{:S(2)}) collective-permute-start(bf16[128,2048]{1,0:T(8,128)(2,1)S(1)} %collective-permute-done.refs_0_.refs_2_), channel_id=1, source_target_pairs={{0,8},{2,10},{8,16},{10,18},{16,24},{18,26},{24,28},{26,30},{28,20... | collective-permute-start | bytes 1572872 | tf_op jit(solution)/shard_map/ppermute | solution.py:294
  20.1 13.4 %collective-permute-start.3 = (bf16[128,2048]{1,0:T(8,128)(2,1)S(1)}, bf16[128,2048]{1,0:T(8,128)(2,1)S(1)}, u32[]{:S(2)}, u32[]{:S(2)}) collective-permute-start(bf16[128,2048]{1,0:T(8,128)(2,1)S(1)} %collective-permute-done.1.refs_2_.refs_4_), channel_id=1, source_target_pairs={{0,4},{2,6},{8,0},{10,2},{16,8},{18,10},{24,16},{26,18},{28,24},{3... | collective-permute-start | bytes 1572872 | tf_op jit(solution)/shard_map/ppermute | solution.py:295
  22.3 13.4 %collective-permute-start.7 = (bf16[128,2048]{1,0:T(8,128)(2,1)S(1)}, bf16[128,2048]{1,0:T(8,128)(2,1)S(1)}, u32[]{:S(2)}, u32[]{:S(2)}) collective-permute-start(bf16[128,2048]{1,0:T(8,128)(2,1)S(1)} %collective-permute-done.refs_0_.refs_2_), channel_id=1, source_target_pairs={{0,2},{2,0},{4,6},{6,4},{8,10},{10,8},{12,14},{14,12},{16,18},{18,... | collective-permute-start | bytes 1572872 | tf_op jit(solution)/shard_map/ppermute | solution.py:304
  22.3 13.4 %collective-permute-start.8 = (bf16[128,2048]{1,0:T(8,128)(2,1)S(1)}, bf16[128,2048]{1,0:T(8,128)(2,1)S(1)}, u32[]{:S(2)}, u32[]{:S(2)}) collective-permute-start(bf16[128,2048]{1,0:T(8,128)(2,1)S(1)} %collective-permute-done.1.refs_2_.refs_4_), channel_id=1, source_target_pairs={{0,2},{2,0},{4,6},{6,4},{8,10},{10,8},{12,14},{14,12},{16,18},{18,... | collective-permute-start | bytes 1572872 | tf_op jit(solution)/shard_map/ppermute | solution.py:304
  33.5 13.3 %collective-permute-start.5 = (bf16[128,2048]{1,0:T(8,128)(2,1)S(1)}, bf16[128,2048]{1,0:T(8,128)(2,1)S(1)}, u32[]{:S(2)}, u32[]{:S(2)}) collective-permute-start(bf16[128,2048]{1,0:T(8,128)(2,1)S(1)} %collective-permute-done.2.refs_0_.refs_6_), channel_id=1, source_target_pairs={{0,8},{2,10},{8,16},{10,18},{16,24},{18,26},{24,28},{26,30},{28,20... | collective-permute-start | bytes 1572872 | tf_op jit(solution)/shard_map/ppermute | solution.py:294
  35.5 14.2 %collective-permute-start.11 = (bf16[128,2048]{1,0:T(8,128)(2,1)S(1)}, bf16[128,2048]{1,0:T(8,128)(2,1)S(1)}, u32[]{:S(2)}, u32[]{:S(2)}) collective-permute-start(bf16[128,2048]{1,0:T(8,128)(2,1)S(1)} %collective-permute-done.2.refs_0_.refs_6_), channel_id=1, source_target_pairs={{0,2},{2,0},{4,6},{6,4},{8,10},{10,8},{12,14},{14,12},{16,18},{18,... | collective-permute-start | bytes 1572872 | tf_op jit(solution)/shard_map/ppermute | solution.py:304
  54.8 13.2 %collective-permute-start.12 = (bf16[128,2048]{1,0:T(8,128)(2,1)S(1)}, bf16[128,2048]{1,0:T(8,128)(2,1)S(1)}, u32[]{:S(2)}, u32[]{:S(2)}) collective-permute-start(bf16[128,2048]{1,0:T(8,128)(2,1)S(1)} %copy-done.30), channel_id=1, source_target_pairs={{0,8},{2,10},{8,16},{10,18},{16,24},{18,26},{24,28},{26,30},{28,20... | collective-permute-start | bytes 1572872 | tf_op jit(solution)/shard_map/ppermute | solution.py:294
  71.5 17.9 %collective-permute-start.23 = (bf16[128,2176]{1,0:T(8,128)(2,1)}, bf16[128,2176]{1,0:T(8,128)(2,1)}, u32[]{:S(2)}, u32[]{:S(2)}) collective-permute-start(bf16[128,2176]{1,0:T(8,128)(2,1)} %get-tuple-element.115), channel_id=1, source_target_pairs={{0,2},{2,0},{4,6},{6,4},{8,10},{10,8},{12,14},{14,12},{16,18},{18,... | collective-permute-start | bytes 1671176 | tf_op jit(solution)/shard_map/ppermute | solution.py:407
  72.4 18.5 %collective-permute-start.24 = (bf16[128,2176]{1,0:T(8,128)(2,1)}, bf16[128,2176]{1,0:T(8,128)(2,1)}, u32[]{:S(2)}, u32[]{:S(2)}) collective-permute-start(bf16[128,2176]{1,0:T(8,128)(2,1)} %get-tuple-element.117), channel_id=1, source_target_pairs={{0,2},{2,0},{4,6},{6,4},{8,10},{10,8},{12,14},{14,12},{16,18},{18,... | collective-permute-start | bytes 1671176 | tf_op jit(solution)/shard_map/ppermute | solution.py:407
  72.8 18.1 %collective-permute-start.25 = (bf16[128,2176]{1,0:T(8,128)(2,1)}, bf16[128,2176]{1,0:T(8,128)(2,1)}, u32[]{:S(2)}, u32[]{:S(2)}) collective-permute-start(bf16[128,2176]{1,0:T(8,128)(2,1)} %get-tuple-element.119), channel_id=1, source_target_pairs={{0,2},{2,0},{4,6},{6,4},{8,10},{10,8},{12,14},{14,12},{16,18},{18,... | collective-permute-start | bytes 1671176 | tf_op jit(solution)/shard_map/ppermute | solution.py:407
  94.6 18.7 %collective-permute-start.34 = (bf16[352,1024]{1,0:T(8,128)(2,1)}, bf16[352,1024]{1,0:T(8,128)(2,1)S(1)}, u32[]{:S(2)}, u32[]{:S(2)}) collective-permute-start(bf16[352,1024]{1,0:T(8,128)(2,1)} %get-tuple-element.146), channel_id=1, source_target_pairs={{0,1},{1,0},{2,3},{3,2},{4,5},{5,4},{6,7},{7,6},{8,9},{9,8},{10,11... | collective-permute-start | bytes 2162696 | tf_op jit(solution)/shard_map/ppermute | solution.py:369
  99.3 14.5 %collective-permute-start.31 = (bf16[64,4224]{1,0:T(8,128)(2,1)}, bf16[64,4224]{1,0:T(8,128)(2,1)S(1)}, u32[]{:S(2)}, u32[]{:S(2)}) collective-permute-start(bf16[64,4224]{1,0:T(8,128)(2,1)} %pad_maximum_fusion), channel_id=1, source_target_pairs={{0,8},{2,10},{8,16},{10,18},{16,24},{18,26},{24,28},{26,30},{28,20... | collective-permute-start | bytes 1622024 | tf_op jit(solution)/shard_map/ppermute | solution.py:294
  100.8 14.2 %collective-permute-start.32 = (bf16[64,4224]{1,0:T(8,128)(2,1)}, bf16[64,4224]{1,0:T(8,128)(2,1)S(1)}, u32[]{:S(2)}, u32[]{:S(2)}) collective-permute-start(bf16[64,4224]{1,0:T(8,128)(2,1)} %pad_maximum_fusion.1), channel_id=1, source_target_pairs={{0,4},{2,6},{8,0},{10,2},{16,8},{18,10},{24,16},{26,18},{28,24},{3... | collective-permute-start | bytes 1622024 | tf_op jit(solution)/shard_map/ppermute | solution.py:295
  117.2 15.0 %collective-permute-start.35 = (bf16[128,2176]{1,0:T(8,128)(2,1)S(1)}, bf16[128,2176]{1,0:T(8,128)(2,1)S(1)}, u32[]{:S(2)}, u32[]{:S(2)}) collective-permute-start(bf16[128,2176]{1,0:T(8,128)(2,1)S(1)} %add_convert_fusion.6), channel_id=1, source_target_pairs={{0,8},{2,10},{8,16},{10,18},{16,24},{18,26},{24,28},{26,30},{28,20... | collective-permute-start | bytes 1671176 | tf_op jit(solution)/shard_map/ppermute | solution.py:351
  117.9 14.7 %collective-permute-start.36 = (bf16[128,2176]{1,0:T(8,128)(2,1)S(1)}, bf16[128,2176]{1,0:T(8,128)(2,1)S(1)}, u32[]{:S(2)}, u32[]{:S(2)}) collective-permute-start(bf16[128,2176]{1,0:T(8,128)(2,1)S(1)} %add_convert_fusion.5), channel_id=1, source_target_pairs={{0,4},{2,6},{8,0},{10,2},{16,8},{18,10},{24,16},{26,18},{28,24},{3... | collective-permute-start | bytes 1671176 | tf_op jit(solution)/shard_map/ppermute | solution.py:352
  129.3 20.2 %collective-permute-start.48 = (bf16[512,768]{1,0:T(8,128)(2,1)}, bf16[512,768]{1,0:T(8,128)(2,1)S(1)}, u32[]{:S(2)}, u32[]{:S(2)}) collective-permute-start(bf16[512,768]{1,0:T(8,128)(2,1)} %get-tuple-element.155), channel_id=1, source_target_pairs={{0,1},{1,0},{2,3},{3,2},{4,5},{5,4},{6,7},{7,6},{8,9},{9,8},{10,11... | collective-permute-start | bytes 2359304 | tf_op jit(solution)/shard_map/ppermute | solution.py:369
  134.0 13.9 %collective-permute-start.46 = (bf16[128,2176]{1,0:T(8,128)(2,1)S(1)}, bf16[128,2176]{1,0:T(8,128)(2,1)S(1)}, u32[]{:S(2)}, u32[]{:S(2)}) collective-permute-start(bf16[128,2176]{1,0:T(8,128)(2,1)S(1)} %add_convert_fusion.4), channel_id=1, source_target_pairs={{0,8},{2,10},{8,16},{10,18},{16,24},{18,26},{24,28},{26,30},{28,20... | collective-permute-start | bytes 1671176 | tf_op jit(solution)/shard_map/ppermute | solution.py:351
  135.8 13.6 %collective-permute-start.47 = (bf16[128,2176]{1,0:T(8,128)(2,1)S(1)}, bf16[128,2176]{1,0:T(8,128)(2,1)S(1)}, u32[]{:S(2)}, u32[]{:S(2)}) collective-permute-start(bf16[128,2176]{1,0:T(8,128)(2,1)S(1)} %add_convert_fusion.3), channel_id=1, source_target_pairs={{0,4},{2,6},{8,0},{10,2},{16,8},{18,10},{24,16},{26,18},{28,24},{3... | collective-permute-start | bytes 1671176 | tf_op jit(solution)/shard_map/ppermute | solution.py:352
  151.1 15.0 %collective-permute-start.50 = (bf16[128,2176]{1,0:T(8,128)(2,1)S(1)}, bf16[128,2176]{1,0:T(8,128)(2,1)S(1)}, u32[]{:S(2)}, u32[]{:S(2)}) collective-permute-start(bf16[128,2176]{1,0:T(8,128)(2,1)S(1)} %get-tuple-element.171), channel_id=1, source_target_pairs={{0,4},{2,6},{8,0},{10,2},{16,8},{18,10},{24,16},{26,18},{28,24},{3... | collective-permute-start | bytes 1671176 | tf_op jit(solution)/shard_map/ppermute | solution.py:352
  152.1 14.0 %collective-permute-start.49 = (bf16[128,2176]{1,0:T(8,128)(2,1)S(1)}, bf16[128,2176]{1,0:T(8,128)(2,1)S(1)}, u32[]{:S(2)}, u32[]{:S(2)}) collective-permute-start(bf16[128,2176]{1,0:T(8,128)(2,1)S(1)} %get-tuple-element.170), channel_id=1, source_target_pairs={{0,8},{2,10},{8,16},{10,18},{16,24},{18,26},{24,28},{26,30},{28,20... | collective-permute-start | bytes 1671176 | tf_op jit(solution)/shard_map/ppermute | solution.py:351
  (98 other events, 697.9 us)
